TPU v7x, 32 devices: a whole 2x2x4 slice. The times are simulated.
32 devices in a mesh: row: 4 (over y, core), pitch: 4 (over z), span: 2 (over x).
Axes of the slice: x: 2, y: 2, z: 4, core: 2. Of those that a mesh axis runs over, the one named last changes fastest.
Arguments:
- outlet: bfloat16 [4, 2, 5, 1024, 4096], P('row', None, None, 'span', 'pitch'), may hold values from -6 to 6
- remap_weight: bfloat16 [1024, 896], P('span'), may hold values from -0.4375 to 0.4375
- band_start: int32 [896], replicated, may hold values from 0 to 832, as said below
- blade_counts: int32 [2], replicated, may hold values from 12 to 60
- mode_orders: int32 [64, 2], replicated, may hold values from -4 to 4
Outputs:
- stator_inlet: bfloat16 [4, 2, 5, 896, 4096], P('row', None, None, 'span', 'pitch')
Inputs may be any that keep to these rules, and one draw needn't show every extreme that they name: Stator radial row m draws from rotor radial rows band_start[m] to band_start[m] + 191; band_start[m] lies within 6 rows of m * 832 / 895, band_start[0] = 0 and band_start[895] = 832.
All inputs are finite; a program needn't handle non-finite values.
Results may differ from a plain program's by a relative error of at most 0.0068.
Values may be sent and summed in bfloat16 or wider, within the bound.
No kernel may reach another device: no remote copies, remote signals or barrier semaphores. Data moves between devices by JAX's collectives and lax.ppermute only.
A program may use at most 64 MiB of HBM per device.

v0:
```python
import math

import jax
import jax.numpy as jnp
from jax import lax
from jax.sharding import PartitionSpec as P

BAND = 192


def passed_along(value, axis, steps):
    count = lax.axis_size(axis)
    pairs = [(source, (source + steps) % count) for source in range(count)]
    return lax.ppermute(value, axis, pairs)


def pitch_table(wavenumber, first_row, number, total_pitch):
    circumferential_coordinates = first_row + jnp.arange(number, dtype=jnp.int32)
    angular_offsets = jnp.mod(
        circumferential_coordinates[:, None] * wavenumber[None, :], total_pitch
    )
    angles = 2.0 * math.pi / total_pitch * angular_offsets.astype(jnp.float32)
    return jnp.stack([jnp.cos(angles), jnp.sin(angles)], axis=2).reshape(
        number, 2 * wavenumber.shape[0]
    )


def body(outlet, remap_weight, band_start, blade_counts, mode_orders):
    row_count = lax.axis_size("row")
    pitch_count = lax.axis_size("pitch")
    cascade_index_map = lax.axis_index("row")
    pitch_at = lax.axis_index("pitch")
    span_at = lax.axis_index("span")
    planes = outlet[0]
    drawn_cases, fields, rad_loc, pitch_location = planes.shape
    total_pitch = pitch_location * pitch_count
    harmonics = mode_orders.shape[0]
    columns = 2 * harmonics
    cols_loc = columns // pitch_count
    harm_loc = cols_loc // 2
    wavenumber = mode_orders[:, 0] * blade_counts[0] + mode_orders[:, 1] * blade_counts[1]
    analysis_scale = math.sqrt(2.0 / total_pitch)
    raw_local = pitch_table(wavenumber, pitch_at * pitch_location, pitch_location, total_pitch)
    local_table = (raw_local * analysis_scale).astype(jnp.bfloat16)
    flattened = planes.reshape(drawn_cases * fields * rad_loc, pitch_location)
    coefficients = lax.psum_scatter(
        lax.dot_general(
            local_table, flattened, (((0,), (1,)), ((), ())), preferred_element_type=jnp.float32
        ),
        "pitch",
        scatter_dimension=0,
        tiled=True,
    ).reshape(cols_loc, drawn_cases, fields, rad_loc)
    onsite_signal_trace = lax.dynamic_slice_in_dim(wavenumber, pitch_at * harm_loc, harm_loc)
    discrete_moments = cascade_index_map * drawn_cases + jnp.arange(drawn_cases, dtype=jnp.int32)
    vane_passing_interval = row_count * drawn_cases * blade_counts[0]
    angular_offsets = jnp.mod(
        onsite_signal_trace[:, None] * discrete_moments[None, :], vane_passing_interval
    )
    angles = (
        2.0
        * math.pi
        * angular_offsets.astype(jnp.float32)
        / vane_passing_interval.astype(jnp.float32)
    )
    cosine = jnp.cos(angles)[:, :, None, None]
    sine_part = jnp.sin(angles)[:, :, None, None]
    paired = coefficients.reshape(harm_loc, 2, drawn_cases, fields, rad_loc)
    cos_part = paired[:, 0]
    sin_part = paired[:, 1]
    rotated = jnp.stack(
        [cos_part * cosine - sin_part * sine_part, cos_part * sine_part + sin_part * cosine], axis=1
    )
    rotated = rotated.reshape(cols_loc, drawn_cases, fields, rad_loc).astype(jnp.bfloat16)
    radial_rows = span_at * rad_loc + jnp.arange(rad_loc, dtype=jnp.int32)
    in_band = (radial_rows[:, None] >= band_start[None, :]) & (
        radial_rows[:, None] < band_start[None, :] + BAND
    )
    banded = jnp.where(in_band, remap_weight, jnp.zeros_like(remap_weight))
    shift_by = row_count // 2
    partial_sums = lax.dot_general(
        rotated, banded, (((3,), (0,)), ((), ())), preferred_element_type=jnp.float32
    )
    remapped = passed_along(
        lax.psum_scatter(partial_sums, "span", scatter_dimension=3, tiled=True).astype(
            jnp.bfloat16
        ),
        "row",
        shift_by,
    )
    synth_table = (raw_local * (1.0 / math.sqrt(harmonics))).astype(jnp.bfloat16).T
    rs_loc = remapped.shape[3]
    shard_piece = lax.all_gather(remapped, "pitch", axis=0, tiled=True)
    number = shard_piece.shape[0]
    flattened_portion = shard_piece.reshape(number, drawn_cases * fields * rs_loc)
    summed = lax.dot_general(
        flattened_portion, synth_table, (((0,), (0,)), ((), ())), preferred_element_type=jnp.float32
    )
    return summed.reshape(1, drawn_cases, fields, rs_loc, pitch_location).astype(jnp.bfloat16)


def solution(mesh):
    placed = (P("row", None, None, "span", "pitch"), P("span", None), P(), P(), P())
    return jax.shard_map(
        body,
        mesh=mesh,
        in_specs=placed,
        out_specs=P("row", None, None, "span", "pitch"),
        check_vma=False,
    )
```

profile of v0, /device:TPU:0, one launch (start us, length us, event | category | flops | bytes accessed | tf_op | source)
XLA Modules:
  0.0 176.7 jit_solution(18159987637332007254)
XLA Ops:
  6.5 0.0 reduce-scatter.5.cloned.1.call-start
  6.5 1.3 fusion.25
  7.8 1.9 %fusion.29 = s32[64]{0:T(128)S(1)} fusion(s32[]{:T(128)} %bitcast.1, s32[64,2]{0,1:T(2,128)} %param.9, s32[]{:T(128)} %bitcast), kind=kLoop, calls=%fused_computation.47 | loop fusion | flops 192 | bytes 776 | tf_op jit(solution)/shard_map/add | solution.py:41
  9.8 1.1 fusion.14
  10.9 0.1 multiply_convert_fusion
  11.0 0.3 copy.17
  11.2 0.1 convert_element_type.66
  11.3 9.0 %fusion.26 = f32[128,5120]{1,0:T(8,128)} fusion(bf16[1024,128]{0,1:T(8,128)(2,1)S(1)} %convert_element_type.66, bf16[5120,1024]{1,0:T(8,128)(2,1)} %bitcast.35), kind=kOutput, calls=%fused_computation.46 | convolution fusion | flops 1342177280 | bytes 13369344 | tf_op jit(solution)/shard_map/dot_general | solution.py:47
  20.3 0.0 copy-start.1
  20.3 0.0 copy-start
  20.4 0.0 reduce-scatter.5.cloned.1.call-update
  20.4 0.0 reduce-scatter.7.cloned.1.call-start
  21.1 0.0 copy-done.1
  21.1 1.2 multiply_add_fusion
  22.3 0.1 dynamic-slice_bitcast_fusion
  22.3 0.0 copy-done
  22.4 0.2 fusion.23
  22.6 0.0 copy-start.2
  22.6 52.7 %reduce-scatter.5.cloned.1.call-done = f32[32,5120]{1,0:T(8,128)} async-done(((f32[128,5120]{1,0:T(8,128)}), f32[32,5120]{1,0:T(8,128)}) %reduce-scatter.5.cloned.1.call-update) | async-done | bytes 655376 | tf_op jit(solution)/shard_map/reduce_scatter | solution.py:46
  75.3 1.4 reshape_reshape.3
  76.8 0.2 subtract_convert_fusion
  77.0 0.1 pad_maximum_fusion.1
  77.1 0.0 copy-done.2
  77.1 0.8 fusion.2
  77.9 5.8 %copy.27 = f32[32,2,5,896]{0,2,1,3:T(8,128)} copy(f32[32,2,5,896]{3,0,2,1:T(8,128)S(1)} %fusion.2) | data formatting | bytes 2293760
  83.8 6.1 %reshape.252 = f32[896,320]{1,0:T(8,128)} reshape(f32[896,2,5,32]{3,2,1,0:T(8,128)} %bitcast.34) | data formatting | bytes 2293760
  89.8 0.0 reduce-scatter.7.cloned.1.call-update
  89.9 0.0 all-gather.2.cloned.1.call-start
  89.9 23.7 %reduce-scatter.7.cloned.1.call-done = f32[448,320]{1,0:T(8,128)} async-done(((f32[896,320]{1,0:T(8,128)}), f32[448,320]{1,0:T(8,128)}) %reduce-scatter.7.cloned.1.call-update) | async-done | bytes 573456
  113.6 2.3 %reshape.253 = bf16[448,2,5,32]{3,2,1,0:T(8,128)(2,1)S(1)} reshape(f32[448,320]{1,0:T(8,128)} %reduce-scatter.7.cloned.1.call-done) | data formatting | bytes 860160
  115.9 1.2 copy.28
  117.1 1.5 collective-permute-start
  118.6 8.0 %collective-permute-done = bf16[32,2,5,448]{3,0,2,1:T(8,128)(2,1)S(1)} collective-permute-done((bf16[32,2,5,448]{3,0,2,1:T(8,128)(2,1)S(1)}, bf16[32,2,5,448]{3,0,2,1:T(8,128)(2,1)S(1)}, u32[]{:S(2)}, u32[]{:S(2)}) %collective-permute-start) | collective-permute-done | bytes 286752 | tf_op jit(solution)/shard_map/ppermute | solution.py:14
  126.6 1.1 copy.19
  127.7 0.0 all-gather.2.cloned.1.call-update
  127.7 0.3 copy.21
  128.0 0.1 convert_element_type.72
  128.1 32.5 %all-gather.2.cloned.1.call-done = bf16[128,2,5,448]{3,1,2,0:T(2,128)(2,1)} async-done(((bf16[32,2,5,448]{3,1,2,0:T(2,128)(2,1)}), bf16[128,2,5,448]{3,1,2,0:T(2,128)(2,1)}) %all-gather.2.cloned.1.call-update) | async-done | bytes 1146896 | tf_op jit(solution)/shard_map/all_gather | solution.py:93
  160.6 3.5 %copy.20 = bf16[128,2,5,448]{0,3,2,1:T(8,128)(2,1)S(1)} copy(bf16[128,2,5,448]{3,1,2,0:T(2,128)(2,1)} %all-gather.2.cloned.1.call-done) | data formatting | bytes 2293760 | tf_op jit(solution)/shard_map/all_gather | solution.py:93
  164.0 6.2 %convert_bitcast_fusion = bf16[1,2,5,448,1024]{4,3,2,1,0:T(8,128)(2,1)} fusion(bf16[128,2,5,448]{0,3,2,1:T(8,128)(2,1)S(1)} %copy.20, bf16[1024,128]{0,1:T(8,128)(2,1)S(1)} %convert_element_type.72), kind=kOutput, calls=%fused_computation | convolution fusion | flops 1178992640 | bytes 10584064 | tf_op jit(solution)/shard_map/dot_general | solution.py:96
  (4 shorter events, 0.0 us)
Async XLA Ops:
  6.5 68.8 %reduce-scatter.5.cloned.1.call-start = ((), (), s32[]{:S(2)}) async-start(), calls=%async_computation.2 | async-start | bytes 3276800 | tf_op jit(solution)/shard_map/reduce_scatter | solution.py:46
  20.3 0.7 copy-start.1
  20.3 2.0 %copy-start = (s32[896]{0:T(1024)S(1)}, s32[896]{0:T(1024)}, u32[]{:S(2)}) copy-start(s32[896]{0:T(1024)} %param.7) | copy-start | bytes 10756
  20.4 93.2 %reduce-scatter.7.cloned.1.call-start = ((), (), s32[]{:S(2)}) async-start(), calls=%async_computation.4 | async-start | bytes 2064384
  22.6 54.5 %copy-start.2 = (bf16[512,896]{1,0:T(8,128)(2,1)S(1)}, bf16[512,896]{1,0:T(8,128)(2,1)}, u32[]{:S(2)}) copy-start(bf16[512,896]{1,0:T(8,128)(2,1)} %param.6) | copy-start | bytes 2752516
  89.9 70.7 %all-gather.2.cloned.1.call-start = ((), (), s32[]{:S(2)}) async-start(), calls=%async_computation.3 | async-start | bytes 1638400 | tf_op jit(solution)/shard_map/all_gather | solution.py:93
  117.1 9.5 %collective-permute-start = (bf16[32,2,5,448]{3,0,2,1:T(8,128)(2,1)S(1)}, bf16[32,2,5,448]{3,0,2,1:T(8,128)(2,1)S(1)}, u32[]{:S(2)}, u32[]{:S(2)}) collective-permute-start(bf16[32,2,5,448]{3,0,2,1:T(8,128)(2,1)S(1)} %copy.28), channel_id=1, source_target_pairs={{0,16},{8,24},{16,0},{24,8},{1,17},{9,25},{17,1},{25,9},{2,18},{10... | collective-permute-start | bytes 860168 | tf_op jit(solution)/shard_map/ppermute | solution.py:14
Sparse Core Ops, SparseCore 0:
  20.5 54.7 reduce-scatter.4
  90.0 23.5 reduce-scatter.6
  127.8 32.6 all-gather.1
where the time goes:
time: 177 us
  waiting for transfers between devices  117 us (66%)
  local copies, waits for them, and re-layouts  23.5 us (13%)
  matrix products  16 us (9%)
  between operations  13.9 us (8%)
  other arithmetic  4.83 us (3%)
    reduce_scatter x1, waiting for transfers between devices, body(): lax.psum_scatter(lax.dot_general(local_table, flattened, (((0,), (1,)), (...  52.7 us
    all_gather x1, waiting for transfers between devices, body(): shard_piece = lax.all_gather(remapped, 'pitch', axis=0, tiled=True)  32.5 us
    unnamed x4, waiting for transfers between devices  23.7 us
    unnamed x10, local copies, waits for them, and re-layouts  15.4 us
    dot_general x1, matrix products, body(): lax.dot_general(local_table, flattened, (((0,), (1,)), ((), ())), preferr...  9 us
    ppermute x1, waiting for transfers between devices, passed_along(): return lax.ppermute(value, axis, pairs)  7.99 us
    dot_general x1, matrix products, body(): lax.dot_general(flattened_portion, synth_table, (((0,), (0,)), ((), ())),...  6.19 us
  transfers between devices with their start and end apart: 4, of which 4 were waited for; matrix products, arithmetic and copies ran while one was open for 1% of the time, Pallas kernels for 0%

commit v1 on v0

v1 whole, which is shorter than its diff:
```python
import functools
import math

import jax
import jax.numpy as jnp
from jax import lax
from jax.experimental import pallas as pl
from jax.experimental.pallas import tpu as pltpu
from jax.sharding import PartitionSpec as P

BAND = 192
JITTER = 6
VMEM_BYTES = 48 * 1024 * 1024
PARTS = 2


def exchange(value, axis, distance):
    count = lax.axis_size(axis)
    return lax.ppermute(value, axis, [(i, i ^ distance) for i in range(count)])


def column_wavenumbers(counts_ref, orders_ref):
    harmonics = orders_ref.shape[1]
    columns = 2 * harmonics
    spread = (
        lax.broadcasted_iota(jnp.int32, (harmonics, columns), 1) // 2
        == lax.broadcasted_iota(jnp.int32, (harmonics, columns), 0)
    )
    orders = jnp.dot(
        orders_ref[...].astype(jnp.float32),
        spread.astype(jnp.float32),
        preferred_element_type=jnp.float32,
    ).astype(jnp.int32)
    return orders[0:1] * counts_ref[0] + orders[1:2] * counts_ref[1]


def table_factors(wave, first_row, rows, total_pitch, turn):
    fine = 32
    coarse = rows // fine
    columns = wave.shape[1]
    step = 2.0 * math.pi / total_pitch
    at_coarse = first_row + fine * lax.broadcasted_iota(jnp.int32, (coarse, columns), 0)
    at_fine = lax.broadcasted_iota(jnp.int32, (fine, columns), 0)
    odd = lax.broadcasted_iota(jnp.int32, (fine, columns), 1) % 2
    q_coarse = lax.rem(at_coarse * wave, total_pitch)
    q_fine = lax.rem(at_fine * wave - odd * (total_pitch // 4), total_pitch)
    a = step * q_coarse.astype(jnp.float32)
    b = step * q_fine.astype(jnp.float32) + turn
    return jnp.cos(a), jnp.sin(a), jnp.cos(b), jnp.sin(b)


def fill_table(ref, at, factors, scale):
    cos_a, sin_a, cos_b, sin_b = factors
    fine = cos_b.shape[0]
    cos_b = cos_b * scale
    sin_b = sin_b * scale
    for i in range(cos_a.shape[0]):
        value = cos_a[i : i + 1] * cos_b - sin_a[i : i + 1] * sin_b
        ref[at + (pl.ds(i * fine, fine), slice(None))] = value.astype(ref.dtype)


def masked_weights(weight, band_start, first_row):
    rows = first_row + lax.broadcasted_iota(jnp.int32, weight.shape, 0)
    inside = (rows >= band_start) & (rows < band_start + BAND)
    return jnp.where(inside, weight.astype(jnp.float32), 0.0)


def edge_kernel(
    sizes,
    counts_ref,
    orders_ref,
    starts_ref,
    weight_ref,
    planes_ref,
    *rest,
):
    parts, instances, fields, edge, halo, pitch_count, row_count, total_pitch = sizes
    halo_refs = rest[:parts]
    table_ref, edge_ref, edge_weight, flipped, planes_sem, weight_sem = rest[parts:]
    count, rows, pitch = planes_ref.shape
    span_at = lax.axis_index("span")
    rs_loc = weight_ref.shape[1] // 2
    first = pl.multiple_of((1 - span_at) * (rows - edge), 16)
    fetch = [
        pltpu.make_async_copy(
            planes_ref.at[pl.ds(j * fields, fields), pl.ds(first, edge), :],
            edge_ref.at[pl.ds(j * fields, fields)],
            planes_sem.at[j],
        )
        for j in range(instances)
    ]
    fetch_weight = pltpu.make_async_copy(
        weight_ref.at[pl.ds(first, edge), :], edge_weight, weight_sem
    )
    fetch_weight.start()
    for copy in fetch:
        copy.start()
    wave = column_wavenumbers(counts_ref, orders_ref)
    first_instance = lax.axis_index("row") * instances
    period = row_count * instances * counts_ref[0]
    scale = math.sqrt(2.0 / total_pitch)
    for j in range(instances):
        turned = (wave * (first_instance + j)).astype(jnp.float32)
        whole = period.astype(jnp.float32)
        turn = (2.0 * math.pi) * (turned - whole * jnp.floor(turned / whole)) / whole
        factors = table_factors(wave, lax.axis_index("pitch") * pitch, pitch, total_pitch, turn)
        fill_table(table_ref, (j,), factors, scale)
    fetch_weight.wait()
    masked = masked_weights(edge_weight[...], starts_ref[...], span_at * rows + first)
    flipped[...] = masked.T.astype(flipped.dtype)
    halo_first = pl.multiple_of(jnp.where(span_at == 0, rs_loc, rs_loc - halo), 16)
    weights = flipped[pl.ds(halo_first, halo), :]
    per = count // parts
    for j in range(instances):
        fetch[j].wait()
        spectra = jnp.dot(
            edge_ref[pl.ds(j * fields, fields)].reshape(fields * edge, pitch),
            table_ref[j],
            preferred_element_type=jnp.float32,
        ).astype(jnp.bfloat16)
        for f in range(fields):
            at = j * fields + f
            halo_refs[at // per][at % per] = jnp.dot(
                weights,
                spectra[f * edge : (f + 1) * edge],
                preferred_element_type=jnp.float32,
            ).astype(jnp.bfloat16)


def edge_call(sizes, counts, orders, starts, weight, planes):
    parts, instances, fields, edge, halo = sizes[:5]
    count, rows, pitch = planes.shape
    columns = 2 * orders.shape[1]
    vmem = pl.BlockSpec(memory_space=pltpu.VMEM)
    anywhere = pl.BlockSpec(memory_space=pl.ANY)
    return pl.pallas_call(
        functools.partial(edge_kernel, sizes),
        out_shape=[jax.ShapeDtypeStruct((count // parts, halo, columns), jnp.bfloat16)] * parts
        + [jax.ShapeDtypeStruct((instances, pitch, columns), jnp.bfloat16)],
        in_specs=[pl.BlockSpec(memory_space=pltpu.SMEM), vmem, vmem, anywhere, anywhere],
        out_specs=[vmem] * (parts + 1),
        scratch_shapes=[
            pltpu.VMEM((count, edge, pitch), jnp.bfloat16),
            pltpu.VMEM((edge, weight.shape[1]), jnp.bfloat16),
            pltpu.VMEM((weight.shape[1], edge), jnp.bfloat16),
            pltpu.SemaphoreType.DMA((instances,)),
            pltpu.SemaphoreType.DMA,
        ],
        compiler_params=pltpu.CompilerParams(vmem_limit_bytes=VMEM_BYTES),
        cost_estimate=pl.CostEstimate(
            flops=2 * count * edge * columns * (pitch + halo),
            bytes_accessed=2 * count * edge * pitch,
            transcendentals=0,
        ),
        name="edge",
    )(counts, orders, starts, weight, planes)


def band_kernel(starts_ref, weight_ref, band_ref, flipped):
    rows = weight_ref.shape[0]
    shards, per, _ = band_ref.shape
    span_at = lax.axis_index("span")
    pitch_at = lax.axis_index("pitch")
    masked = masked_weights(weight_ref[...], starts_ref[...], span_at * rows)
    flipped[...] = masked.T.astype(flipped.dtype)
    for k in range(shards):
        at = jnp.bitwise_xor(pitch_at, k) if shards > 1 else 0
        first = pl.multiple_of(span_at * (shards * per) + at * per, 16)
        band_ref[k] = flipped[pl.ds(first, per), :]


def band_call(shards, starts, weight):
    rows, stator_rows = weight.shape
    per = stator_rows // 2 // shards
    vmem = pl.BlockSpec(memory_space=pltpu.VMEM)
    return pl.pallas_call(
        band_kernel,
        out_shape=jax.ShapeDtypeStruct((shards, per, rows), jnp.bfloat16),
        in_specs=[vmem, vmem],
        out_specs=vmem,
        scratch_shapes=[pltpu.VMEM((stator_rows, rows), jnp.bfloat16)],
        compiler_params=pltpu.CompilerParams(vmem_limit_bytes=VMEM_BYTES),
        name="band",
    )(starts, weight)


def analyse_kernel(shards, planes_ref, table_ref, band_ref, *out_refs):
    spectra = jnp.dot(
        planes_ref[0], table_ref[0], preferred_element_type=jnp.float32
    ).astype(jnp.bfloat16)
    rows = band_ref.shape[0] // shards
    result = jnp.dot(band_ref[...], spectra, preferred_element_type=jnp.float32)
    for k in range(shards):
        out_refs[k][0] = result[k * rows : (k + 1) * rows].astype(out_refs[k].dtype)


def analyse_call(shards, first, number, fields, planes, table, band):
    count, rows, pitch = planes.shape
    columns = table.shape[2]
    stator = band.shape[0]
    per = stator // shards
    kinds = [jnp.bfloat16 if k % 2 else jnp.float32 for k in range(shards)]
    return pl.pallas_call(
        functools.partial(analyse_kernel, shards),
        grid=(number,),
        out_shape=[jax.ShapeDtypeStruct((number, per, columns), kind) for kind in kinds],
        in_specs=[
            pl.BlockSpec((1, rows, pitch), lambda i: (first + i, 0, 0)),
            pl.BlockSpec((1, pitch, columns), lambda i: ((first + i) // fields, 0, 0)),
            pl.BlockSpec((stator, rows), lambda i: (0, 0)),
        ],
        out_specs=[pl.BlockSpec((1, per, columns), lambda i: (i, 0, 0))] * shards,
        compiler_params=pltpu.CompilerParams(vmem_limit_bytes=VMEM_BYTES),
        cost_estimate=pl.CostEstimate(
            flops=2 * number * rows * columns * (pitch + stator),
            bytes_accessed=2 * number * rows * pitch,
            transcendentals=0,
        ),
        name="analyse",
    )(planes, table, band)


def synthesis_table_kernel(total_pitch, harmonics, counts_ref, orders_ref, table_ref):
    wave = column_wavenumbers(counts_ref, orders_ref)
    rows = table_ref.shape[0]
    factors = table_factors(wave, lax.axis_index("pitch") * rows, rows, total_pitch, 0.0)
    fill_table(table_ref, (), factors, 1.0 / math.sqrt(harmonics))


def synthesis_table(pitch, total_pitch, counts, orders):
    columns = 2 * orders.shape[1]
    vmem = pl.BlockSpec(memory_space=pltpu.VMEM)
    return pl.pallas_call(
        functools.partial(synthesis_table_kernel, total_pitch, orders.shape[1]),
        out_shape=jax.ShapeDtypeStruct((pitch, columns), jnp.bfloat16),
        in_specs=[pl.BlockSpec(memory_space=pltpu.SMEM), vmem],
        out_specs=vmem,
        name="synthesis_table",
    )(counts, orders)


def synthesise_kernel(shards, table_ref, *rest):
    shard_refs = rest[:shards]
    out_ref, gathered = rest[-2:]
    per = shard_refs[0].shape[1]
    pitch_at = lax.axis_index("pitch")
    for k in range(shards):
        at = jnp.bitwise_xor(pitch_at, k) if shards > 1 else 0
        gathered[pl.ds(pl.multiple_of(at * per, 16), per), :] = shard_refs[k][0]
    out_ref[0] = lax.dot_general(
        gathered[...], table_ref[...], (((1,), (1,)), ((), ())), preferred_element_type=jnp.float32
    ).astype(out_ref.dtype)


def synthesise_call(first, count, table, shards, base):
    pitch, columns = table.shape
    number, per, _ = shards[0].shape
    stator = per * len(shards)
    block = pl.BlockSpec((1, per, columns), lambda i: (i, 0, 0))
    operands = [table, *shards]
    in_specs = [pl.BlockSpec((pitch, columns), lambda i: (0, 0))] + [block] * len(shards)
    aliases = {}
    if base is not None:
        aliases = {len(operands): 0}
        operands.append(base)
        in_specs.append(pl.BlockSpec(memory_space=pl.ANY))
    return pl.pallas_call(
        functools.partial(synthesise_kernel, len(shards)),
        grid=(number,),
        out_shape=jax.ShapeDtypeStruct((count, stator, pitch), jnp.bfloat16),
        in_specs=in_specs,
        out_specs=pl.BlockSpec((1, stator, pitch), lambda i: (first + i, 0, 0)),
        scratch_shapes=[pltpu.VMEM((stator, columns), jnp.bfloat16)],
        input_output_aliases=aliases,
        compiler_params=pltpu.CompilerParams(vmem_limit_bytes=VMEM_BYTES),
        cost_estimate=pl.CostEstimate(
            flops=2 * number * stator * columns * pitch,
            bytes_accessed=2 * number * stator * pitch,
            transcendentals=0,
        ),
        name="synthesise",
    )(*operands)


def body(outlet, remap_weight, band_start, blade_counts, mode_orders):
    row_count = lax.axis_size("row")
    pitch_count = lax.axis_size("pitch")
    pitch_at = lax.axis_index("pitch")
    span_at = lax.axis_index("span")
    instances, fields, rows, pitch = outlet.shape[1:]
    stator_rows = remap_weight.shape[1]
    total_rows = rows * 2
    total_pitch = pitch * pitch_count
    rs_loc = stator_rows // 2
    count = instances * fields
    slope = (stator_rows - 1) / (total_rows - BAND)
    above = math.floor((rows - 1 + JITTER) * slope) + 1 - rs_loc
    below = rs_loc - math.ceil((rows - BAND + 1 - JITTER) * slope)
    halo = -(-max(above, below) // 16) * 16
    reach = max(
        rows - math.floor(rs_loc / slope - JITTER),
        math.floor((rs_loc - 1) / slope + JITTER) + BAND - rows,
    )
    edge = -(-reach // 128) * 128
    by_shards = (
        pitch_count & (pitch_count - 1) == 0
        and pitch_count > 1
        and rs_loc % (16 * pitch_count) == 0
        and halo == rs_loc // pitch_count
    )
    shards = pitch_count if by_shards else 1
    parts = PARTS if count % PARTS == 0 else 1
    per_part = count // parts

    planes = outlet.reshape(count, rows, pitch)
    orders = mode_orders.T
    starts = band_start.reshape(1, stator_rows)
    sizes = (parts, instances, fields, edge, halo, pitch_count, row_count, total_pitch)
    *halos, table = edge_call(sizes, blade_counts, orders, starts, remap_weight, planes)
    halos = [exchange(value, "span", 1) for value in halos]
    band = band_call(shards, starts, remap_weight).reshape(rs_loc, rows)
    synthesis = synthesis_table(pitch, total_pitch, blade_counts, orders)
    shift = row_count // 2
    joined = None
    for part in range(parts):
        first = part * per_part
        own = analyse_call(shards, first, per_part, fields, planes, table, band)
        from_span = halos[part].astype(jnp.float32)
        if by_shards:
            halo_at = jnp.where(span_at == 0, pitch_count - 1, 0)

            def with_halo(k, *terms):
                total = jnp.where(jnp.bitwise_xor(pitch_at, k) == halo_at, from_span, 0.0)
                for term in terms:
                    total = total + term.astype(jnp.float32)
                return total.astype(jnp.bfloat16)

            met = {}
            for k in range(2, pitch_count, 2):
                met[k] = exchange(with_halo(k + 1, own[k + 1]), "pitch", 1)
            beside = exchange(with_halo(1, own[1]), "pitch", 1)
            across = [
                exchange(with_halo(k, own[k], met[k]), "pitch", k)
                for k in range(2, pitch_count, 2)
            ]
            total = with_halo(0, own[0], beside, *across)
            held = {}
            for k in range(0, pitch_count, 2):
                pairs = [
                    (g * pitch_count + z, ((g + shift) % row_count) * pitch_count + (z ^ k))
                    for g in range(row_count)
                    for z in range(pitch_count)
                ]
                held[k] = lax.ppermute(total, ("row", "pitch"), pairs)
            for k in range(0, pitch_count, 2):
                held[k + 1] = exchange(held[k], "pitch", 1)
            pieces = [held[k] for k in range(pitch_count)]
        else:
            low = jnp.pad(from_span, ((0, 0), (rs_loc - halo, 0), (0, 0)))
            high = jnp.pad(from_span, ((0, 0), (0, rs_loc - halo), (0, 0)))
            mine = own[0] + jnp.where(span_at == 0, low, high)
            total = lax.psum(mine, "pitch").astype(jnp.bfloat16)
            pairs = [(g, (g + shift) % row_count) for g in range(row_count)]
            pieces = [lax.ppermute(total, "row", pairs)]
        joined = synthesise_call(first, count, synthesis, pieces, joined)
    return joined.reshape(1, instances, fields, rs_loc, pitch)


def solution(mesh):
    placed = (P("row", None, None, "span", "pitch"), P("span", None), P(), P(), P())
    return jax.shard_map(
        body,
        mesh=mesh,
        in_specs=placed,
        out_specs=P("row", None, None, "span", "pitch"),
        check_vma=False,
    )
```

time: 177 us -> 75.6 us (0.43)
  waiting for transfers between devices: 117 us -> 18.6 us
  Pallas kernels: 0 us -> 26.9 us
  starting transfers between devices: 1.6 us -> 25 us
  local copies, waits for them, and re-layouts: 23.5 us -> 4.15 us
  matrix products: 16 us -> 0 us
  between operations: 13.9 us -> 0.1 us
  other arithmetic: 4.83 us -> 0.48 us
    reduce_scatter x1 -> x0, waiting for transfers between devices: 52.7 us -> none  [body(): lax.psum_scatter(lax.dot_general(local_table, flattened, (((0,), (1,)), (...]
    all_gather x1 -> x0, waiting for transfers between devices: 32.5 us -> none  [body(): shard_piece = lax.all_gather(remapped, 'pitch', axis=0, tiled=True)]
    pallas_call x0 -> x7, Pallas kernels: none -> 26.9 us  [the longest x2 12.5 us: analyse_call(): pl.pallas_call(functools.partial(analyse_kernel, shards), grid=(number,),...]
    unnamed x4 -> x0, waiting for transfers between devices: 23.7 us -> none
    ppermute x1 -> x16, starting transfers between devices: 1.52 us -> 25 us  [the longest x12 21.3 us: exchange(): return lax.ppermute(value, axis, [(i, i ^ distance) for i in range(count)])]
    dot_general x3 -> x0, matrix products: 16 us -> none  [the longest x1 9 us: body(): lax.dot_general(local_table, flattened, (((0,), (1,)), ((), ())), preferr...]
    unnamed x10, local copies, waits for them, and re-layouts: 15.4 us -> 3.47 us
    ppermute x1 -> x16, waiting for transfers between devices: 7.99 us -> 18.6 us  [the longest x12 13.8 us: exchange(): return lax.ppermute(value, axis, [(i, i ^ distance) for i in range(count)])]
  transfers between devices with their start and end apart: 4 -> 16, of which waited for: 4 -> 6; matrix products, arithmetic and copies ran while one was open for 1% -> 1% of each run, Pallas kernels for 0% -> 25%
where the time goes in v1:
time: 75.6 us; the launch traced here: 75.1 us
  Pallas kernels  26.9 us (36%)
  starting transfers between devices  25 us (33%)
  waiting for transfers between devices  18.6 us (25%)
  local copies, waits for them, and re-layouts  4.15 us (5%)
    ppermute x12, starting transfers between devices, exchange(): return lax.ppermute(value, axis, [(i, i ^ distance) for i in range(count)])  21.3 us
    ppermute x12, waiting for transfers between devices, exchange(): return lax.ppermute(value, axis, [(i, i ^ distance) for i in range(count)])  13.8 us
    pallas_call x2, Pallas kernels, analyse_call(): pl.pallas_call(functools.partial(analyse_kernel, shards), grid=(number,),...  12.5 us
    pallas_call x2, Pallas kernels, synthesise_call(): pl.pallas_call(functools.partial(synthesise_kernel, len(shards)), grid=(n...  7.96 us
    ppermute x4, waiting for transfers between devices, body(): held[k] = lax.ppermute(total, ('row', 'pitch'), pairs)  4.72 us
    pallas_call x1, Pallas kernels, edge_call(): pl.pallas_call(functools.partial(edge_kernel, sizes), out_shape=[jax.Shap...  4.13 us
    ppermute x4, starting transfers between devices, body(): held[k] = lax.ppermute(total, ('row', 'pitch'), pairs)  3.61 us
    unnamed x10, local copies, waits for them, and re-layouts  3.47 us
  transfers between devices with their start and end apart: 16, of which 6 were waited for; matrix products, arithmetic and copies ran while one was open for 1% of the time, Pallas kernels for 25%

profile of v1, /device:TPU:0, one launch (start us, length us, event | category | flops | bytes accessed | tf_op | source)
XLA Modules:
  0.0 75.1 jit_solution(10404320313386855383)
XLA Ops:
  0.0 0.7 reshape.12.starts_ref
  0.7 1.2 %copy-done = bf16[512,896]{1,0:T(8,128)(2,1)S(1)} copy-done((bf16[512,896]{1,0:T(8,128)(2,1)S(1)}, bf16[512,896]{1,0:T(8,128)(2,1)}, u32[]{:S(2)}) %copy-start) | copy-done | bytes 917528
  1.9 0.7 copy-done.3
  2.6 0.7 copy-done.4
  3.2 4.1 %edge.1 = (bf16[5,112,128]{2,1,0:T(8,128)(2,1)S(1)}, bf16[5,112,128]{2,1,0:T(8,128)(2,1)S(1)}, bf16[2,1024,128]{2,1,0:T(8,128)(2,1)S(1)}) custom-call(s32[2]{0:T(128)S(1)} %copy-done.4, s32[2,64]{1,0:T(2,128)S(1)} %bitcast.7, s32[1,896]{1,0:T(1,128)S(1)} %reshape.12.starts_ref, bf16[512,896]{1,0:T(8,128)(2,1)S(1)} %copy-done, bf16[10,512,1024]{2,1,0:T(8,128)(2,1)} %bitcast.8), custom_call_target="tpu_custom_call" | custom-call | flops 372244480 | bytes 2621440 | tf_op jit(solution)/shard_map/edge/pallas_call | solution.py:136
  7.3 3.0 %collective-permute-start = (bf16[5,112,128]{2,1,0:T(8,128)(2,1)S(1)}, bf16[5,112,128]{2,1,0:T(8,128)(2,1)S(1)}, u32[]{:S(2)}, u32[]{:S(2)}) collective-permute-start(bf16[5,112,128]{2,1,0:T(8,128)(2,1)S(1)} %get-tuple-element.16), channel_id=1, source_target_pairs={{0,1},{1,0},{2,3},{3,2},{4,5},{5,4},{6,7},{7,6},{8,9},{9,8},{10,11... | collective-permute-start | bytes 430088 | tf_op jit(solution)/shard_map/ppermute | solution.py:19
  10.3 0.1 collective-permute-start.8
  10.4 0.5 band.1
  10.9 6.3 %analyse.3 = (f32[5,112,128]{2,1,0:T(8,128)S(1)}, bf16[5,112,128]{2,1,0:T(8,128)(2,1)S(1)}, f32[5,112,128]{2,1,0:T(8,128)S(1)}, bf16[5,112,128]{2,1,0:T(8,128)(2,1)S(1)}) custom-call(bf16[10,512,1024]{2,1,0:T(8,128)(2,1)} %bitcast.9, bf16[2,1024,128]{2,1,0:T(8,128)(2,1)S(1)} %get-tuple-element.17.table_ref, bf16[448,512]{1,0:T(8,128)(2,1)S(1)} %bitcast.4), custom_call_target="tpu_custom_call" | custom-call | flops 964689920 | bytes 5242880 | tf_op jit(solution)/shard_map/analyse/pallas_call | solution.py:203
  17.2 6.3 %analyse.2 = (f32[5,112,128]{2,1,0:T(8,128)S(1)}, bf16[5,112,128]{2,1,0:T(8,128)(2,1)S(1)}, f32[5,112,128]{2,1,0:T(8,128)S(1)}, bf16[5,112,128]{2,1,0:T(8,128)(2,1)S(1)}) custom-call(bf16[10,512,1024]{2,1,0:T(8,128)(2,1)} %bitcast.10, bf16[2,1024,128]{2,1,0:T(8,128)(2,1)S(1)} %get-tuple-element.17.table_ref, bf16[448,512]{1,0:T(8,128)(2,1)S(1)} %bitcast.5), custom_call_target="tpu_custom_call" | custom-call | flops 964689920 | bytes 5242880 | tf_op jit(solution)/shard_map/analyse/pallas_call | solution.py:203
  23.5 0.0 collective-permute-done.8
  23.5 0.1 fusion.21
  23.6 2.1 %collective-permute-start.10 = (bf16[5,112,128]{2,1,0:T(8,128)(2,1)S(1)}, bf16[5,112,128]{2,1,0:T(8,128)(2,1)S(1)}, u32[]{:S(2)}, u32[]{:S(2)}) collective-permute-start(bf16[5,112,128]{2,1,0:T(8,128)(2,1)S(1)} %fusion.21), channel_id=1, source_target_pairs={{0,2},{2,0},{4,6},{6,4},{1,3},{3,1},{5,7},{7,5},{8,10},{10,8},{12,... | collective-permute-start | bytes 430088 | tf_op jit(solution)/shard_map/ppermute | solution.py:19
  25.7 0.0 collective-permute-done
  25.7 0.1 fusion.10
  25.7 0.1 collective-permute-start.2
  25.8 4.5 %collective-permute-done.10 = bf16[5,112,128]{2,1,0:T(8,128)(2,1)S(1)} collective-permute-done((bf16[5,112,128]{2,1,0:T(8,128)(2,1)S(1)}, bf16[5,112,128]{2,1,0:T(8,128)(2,1)S(1)}, u32[]{:S(2)}, u32[]{:S(2)}) %collective-permute-start.10) | collective-permute-done | bytes 143392 | tf_op jit(solution)/shard_map/ppermute | solution.py:19
  30.3 0.1 fusion.16
  30.4 2.1 %collective-permute-start.9 = (bf16[5,112,128]{2,1,0:T(8,128)(2,1)S(1)}, bf16[5,112,128]{2,1,0:T(8,128)(2,1)S(1)}, u32[]{:S(2)}, u32[]{:S(2)}) collective-permute-start(bf16[5,112,128]{2,1,0:T(8,128)(2,1)S(1)} %get-tuple-element.27), channel_id=1, source_target_pairs={{0,2},{2,0},{4,6},{6,4},{1,3},{3,1},{5,7},{7,5},{8,10},{10,8},{12,... | collective-permute-start | bytes 430088 | tf_op jit(solution)/shard_map/ppermute | solution.py:19
  32.5 2.6 %collective-permute-start.11 = (bf16[5,112,128]{2,1,0:T(8,128)(2,1)S(1)}, bf16[5,112,128]{2,1,0:T(8,128)(2,1)S(1)}, u32[]{:S(2)}, u32[]{:S(2)}) collective-permute-start(bf16[5,112,128]{2,1,0:T(8,128)(2,1)S(1)} %get-tuple-element.28), channel_id=1, source_target_pairs={{0,4},{2,6},{4,0},{6,2},{1,5},{3,7},{5,1},{7,3},{8,12},{10,14},{12... | collective-permute-start | bytes 430088 | tf_op jit(solution)/shard_map/ppermute | solution.py:19
  35.1 0.0 collective-permute-done.2
  35.1 0.1 fusion.5
  35.2 0.5 collective-permute-start.1
  35.8 6.8 %collective-permute-start.3 = (bf16[5,112,128]{2,1,0:T(8,128)(2,1)S(1)}, bf16[5,112,128]{2,1,0:T(8,128)(2,1)S(1)}, u32[]{:S(2)}, u32[]{:S(2)}) collective-permute-start(bf16[5,112,128]{2,1,0:T(8,128)(2,1)S(1)} %get-tuple-element.30), channel_id=1, source_target_pairs={{0,4},{2,6},{4,0},{6,2},{1,5},{3,7},{5,1},{7,3},{8,12},{10,14},{12... | collective-permute-start | bytes 430088 | tf_op jit(solution)/shard_map/ppermute | solution.py:19
  42.6 0.0 collective-permute-done.9
  42.6 1.2 %collective-permute-done.11 = bf16[5,112,128]{2,1,0:T(8,128)(2,1)S(1)} collective-permute-done((bf16[5,112,128]{2,1,0:T(8,128)(2,1)S(1)}, bf16[5,112,128]{2,1,0:T(8,128)(2,1)S(1)}, u32[]{:S(2)}, u32[]{:S(2)}) %collective-permute-start.11) | collective-permute-done | bytes 143392 | tf_op jit(solution)/shard_map/ppermute | solution.py:19
  43.8 0.1 fusion.14
  43.9 0.8 %collective-permute-start.14 = (bf16[5,112,128]{2,1,0:T(8,128)(2,1)S(1)}, bf16[5,112,128]{2,1,0:T(8,128)(2,1)S(1)}, u32[]{:S(2)}, u32[]{:S(2)}) collective-permute-start(bf16[5,112,128]{2,1,0:T(8,128)(2,1)S(1)} %fusion.14), channel_id=1, source_target_pairs={{0,20},{2,22},{4,16},{6,18},{8,28},{10,30},{12,24},{14,26},{16,4},... | collective-permute-start | bytes 430088 | tf_op jit(solution)/shard_map/ppermute | solution.py:354
  44.7 1.2 %collective-permute-start.12 = (bf16[5,112,128]{2,1,0:T(8,128)(2,1)S(1)}, bf16[5,112,128]{2,1,0:T(8,128)(2,1)S(1)}, u32[]{:S(2)}, u32[]{:S(2)}) collective-permute-start(bf16[5,112,128]{2,1,0:T(8,128)(2,1)S(1)} %fusion.14), channel_id=1, source_target_pairs={{0,16},{2,18},{4,20},{6,22},{8,24},{10,26},{12,28},{14,30},{16,0},... | collective-permute-start | bytes 430088 | tf_op jit(solution)/shard_map/ppermute | solution.py:354
  45.9 0.0 collective-permute-done.1
  45.9 7.0 %collective-permute-done.3 = bf16[5,112,128]{2,1,0:T(8,128)(2,1)S(1)} collective-permute-done((bf16[5,112,128]{2,1,0:T(8,128)(2,1)S(1)}, bf16[5,112,128]{2,1,0:T(8,128)(2,1)S(1)}, u32[]{:S(2)}, u32[]{:S(2)}) %collective-permute-start.3) | collective-permute-done | bytes 143392 | tf_op jit(solution)/shard_map/ppermute | solution.py:19
  52.9 0.1 fusion.3
  53.0 0.5 collective-permute-start.6
  53.5 1.1 %collective-permute-start.4 = (bf16[5,112,128]{2,1,0:T(8,128)(2,1)S(1)}, bf16[5,112,128]{2,1,0:T(8,128)(2,1)S(1)}, u32[]{:S(2)}, u32[]{:S(2)}) collective-permute-start(bf16[5,112,128]{2,1,0:T(8,128)(2,1)S(1)} %fusion.3), channel_id=1, source_target_pairs={{0,16},{2,18},{4,20},{6,22},{8,24},{10,26},{12,28},{14,30},{16,0},... | collective-permute-start | bytes 430088 | tf_op jit(solution)/shard_map/ppermute | solution.py:354
  54.6 1.9 %collective-permute-done.14.rest_2_ = bf16[5,112,128]{2,1,0:T(8,128)(2,1)S(1)} collective-permute-done((bf16[5,112,128]{2,1,0:T(8,128)(2,1)S(1)}, bf16[5,112,128]{2,1,0:T(8,128)(2,1)S(1)}, u32[]{:S(2)}, u32[]{:S(2)}) %collective-permute-start.14) | collective-permute-done | bytes 143392 | tf_op jit(solution)/shard_map/ppermute | solution.py:354
  56.5 0.7 collective-permute-start.15
  57.2 0.0 collective-permute-done.12.rest_0_
  57.2 1.3 %collective-permute-start.13 = (bf16[5,112,128]{2,1,0:T(8,128)(2,1)S(1)}, bf16[5,112,128]{2,1,0:T(8,128)(2,1)S(1)}, u32[]{:S(2)}, u32[]{:S(2)}) collective-permute-start(bf16[5,112,128]{2,1,0:T(8,128)(2,1)S(1)} %collective-permute-done.12.rest_0_), channel_id=1, source_target_pairs={{0,2},{2,0},{4,6},{6,4},{1,3},{3,1},{5,7},{7,5},{8,10},{10,8},{12,... | collective-permute-start | bytes 430088 | tf_op jit(solution)/shard_map/ppermute | solution.py:19
  58.5 2.8 %collective-permute-done.6.rest_2_ = bf16[5,112,128]{2,1,0:T(8,128)(2,1)S(1)} collective-permute-done((bf16[5,112,128]{2,1,0:T(8,128)(2,1)S(1)}, bf16[5,112,128]{2,1,0:T(8,128)(2,1)S(1)}, u32[]{:S(2)}, u32[]{:S(2)}) %collective-permute-start.6) | collective-permute-done | bytes 143392 | tf_op jit(solution)/shard_map/ppermute | solution.py:354
  61.4 0.2 collective-permute-start.7
  61.6 0.0 collective-permute-done.4.rest_0_
  61.6 1.8 %collective-permute-start.5 = (bf16[5,112,128]{2,1,0:T(8,128)(2,1)S(1)}, bf16[5,112,128]{2,1,0:T(8,128)(2,1)S(1)}, u32[]{:S(2)}, u32[]{:S(2)}) collective-permute-start(bf16[5,112,128]{2,1,0:T(8,128)(2,1)S(1)} %collective-permute-done.4.rest_0_), channel_id=1, source_target_pairs={{0,2},{2,0},{4,6},{6,4},{1,3},{3,1},{5,7},{7,5},{8,10},{10,8},{12,... | collective-permute-start | bytes 430088 | tf_op jit(solution)/shard_map/ppermute | solution.py:19
  63.4 1.7 %synthesis_table.1.table_ref = bf16[1024,128]{1,0:T(8,128)(2,1)} custom-call(s32[2]{0:T(128)} %counts_ref.3, s32[2,64]{1,0:T(2,128)} %bitcast.6), custom_call_target="tpu_custom_call" | custom-call | tf_op jit(solution)/shard_map/synthesis_table/pallas_call | solution.py:233
  65.1 0.0 collective-permute-done.15.rest_3_
  65.1 1.0 %collective-permute-done.13.rest_1_ = bf16[5,112,128]{2,1,0:T(8,128)(2,1)S(1)} collective-permute-done((bf16[5,112,128]{2,1,0:T(8,128)(2,1)S(1)}, bf16[5,112,128]{2,1,0:T(8,128)(2,1)S(1)}, u32[]{:S(2)}, u32[]{:S(2)}) %collective-permute-start.13) | collective-permute-done | bytes 143392 | tf_op jit(solution)/shard_map/ppermute | solution.py:19
  66.2 0.9 %copy-done.2 = bf16[1024,128]{1,0:T(8,128)(2,1)S(1)} copy-done((bf16[1024,128]{1,0:T(8,128)(2,1)S(1)}, bf16[1024,128]{1,0:T(8,128)(2,1)}, u32[]{:S(2)}) %copy-start.2) | copy-done | bytes 262168
  67.1 4.0 %synthesise.2.rest_4_ = bf16[10,448,1024]{2,1,0:T(8,128)(2,1)} custom-call(bf16[1024,128]{1,0:T(8,128)(2,1)S(1)} %copy-done.2, bf16[5,112,128]{2,1,0:T(8,128)(2,1)S(1)} %collective-permute-done.12.rest_0_, bf16[5,112,128]{2,1,0:T(8,128)(2,1)S(1)} %collective-permute-done.13.rest_1_, bf16[5,112,128]{2,1,0:T(8,128)(2,1)S(1)} %collective-permute-done.14.rest_2_, ...), custom_call_target="tpu_custom_call" | custom-call | flops 587202560 | bytes 4587520 | tf_op jit(solution)/shard_map/synthesise/pallas_call | solution.py:267
  71.1 4.0 %synthesise.3 = bf16[10,448,1024]{2,1,0:T(8,128)(2,1)} custom-call(bf16[1024,128]{1,0:T(8,128)(2,1)S(1)} %copy-done.2, bf16[5,112,128]{2,1,0:T(8,128)(2,1)S(1)} %collective-permute-done.4.rest_0_, bf16[5,112,128]{2,1,0:T(8,128)(2,1)S(1)} %collective-permute-done.5.rest_1_, ...), custom_call_target="tpu_custom_call", output_to_operand_aliasing={{}: (5, {})} | custom-call | flops 587202560 | bytes 4587520 | tf_op jit(solution)/shard_map/synthesise/pallas_call | solution.py:267
  (8 shorter events, 0.0 us)
Async XLA Ops:
  0.7 1.2 %copy-start = (bf16[512,896]{1,0:T(8,128)(2,1)S(1)}, bf16[512,896]{1,0:T(8,128)(2,1)}, u32[]{:S(2)}) copy-start(bf16[512,896]{1,0:T(8,128)(2,1)} %weight_ref.3) | copy-start | bytes 2752516
  1.9 0.7 copy-start.3
  2.5 0.7 copy-start.4
  3.2 7.2 %copy-start.1 = (bf16[512,896]{1,0:T(8,128)(2,1)S(1)}, bf16[512,896]{1,0:T(8,128)(2,1)}, u32[]{:S(2)}) copy-start(bf16[512,896]{1,0:T(8,128)(2,1)} %weight_ref.3) | copy-start | bytes 2752516
  7.3 18.3 %collective-permute-start = (bf16[5,112,128]{2,1,0:T(8,128)(2,1)S(1)}, bf16[5,112,128]{2,1,0:T(8,128)(2,1)S(1)}, u32[]{:S(2)}, u32[]{:S(2)}) collective-permute-start(bf16[5,112,128]{2,1,0:T(8,128)(2,1)S(1)} %get-tuple-element.16), channel_id=1, source_target_pairs={{0,1},{1,0},{2,3},{3,2},{4,5},{5,4},{6,7},{7,6},{8,9},{9,8},{10,11... | collective-permute-start | bytes 430088 | tf_op jit(solution)/shard_map/ppermute | solution.py:19
  10.3 13.2 %collective-permute-start.8 = (bf16[5,112,128]{2,1,0:T(8,128)(2,1)S(1)}, bf16[5,112,128]{2,1,0:T(8,128)(2,1)S(1)}, u32[]{:S(2)}, u32[]{:S(2)}) collective-permute-start(bf16[5,112,128]{2,1,0:T(8,128)(2,1)S(1)} %get-tuple-element.22), channel_id=1, source_target_pairs={{0,1},{1,0},{2,3},{3,2},{4,5},{5,4},{6,7},{7,6},{8,9},{9,8},{10,11... | collective-permute-start | bytes 430088 | tf_op jit(solution)/shard_map/ppermute | solution.py:19
  23.6 6.8 %collective-permute-start.10 = (bf16[5,112,128]{2,1,0:T(8,128)(2,1)S(1)}, bf16[5,112,128]{2,1,0:T(8,128)(2,1)S(1)}, u32[]{:S(2)}, u32[]{:S(2)}) collective-permute-start(bf16[5,112,128]{2,1,0:T(8,128)(2,1)S(1)} %fusion.21), channel_id=1, source_target_pairs={{0,2},{2,0},{4,6},{6,4},{1,3},{3,1},{5,7},{7,5},{8,10},{10,8},{12,... | collective-permute-start | bytes 430088 | tf_op jit(solution)/shard_map/ppermute | solution.py:19
  25.7 9.4 %collective-permute-start.2 = (bf16[5,112,128]{2,1,0:T(8,128)(2,1)S(1)}, bf16[5,112,128]{2,1,0:T(8,128)(2,1)S(1)}, u32[]{:S(2)}, u32[]{:S(2)}) collective-permute-start(bf16[5,112,128]{2,1,0:T(8,128)(2,1)S(1)} %fusion.10), channel_id=1, source_target_pairs={{0,2},{2,0},{4,6},{6,4},{1,3},{3,1},{5,7},{7,5},{8,10},{10,8},{12,... | collective-permute-start | bytes 430088 | tf_op jit(solution)/shard_map/ppermute | solution.py:19
  30.4 12.1 %collective-permute-start.9 = (bf16[5,112,128]{2,1,0:T(8,128)(2,1)S(1)}, bf16[5,112,128]{2,1,0:T(8,128)(2,1)S(1)}, u32[]{:S(2)}, u32[]{:S(2)}) collective-permute-start(bf16[5,112,128]{2,1,0:T(8,128)(2,1)S(1)} %get-tuple-element.27), channel_id=1, source_target_pairs={{0,2},{2,0},{4,6},{6,4},{1,3},{3,1},{5,7},{7,5},{8,10},{10,8},{12,... | collective-permute-start | bytes 430088 | tf_op jit(solution)/shard_map/ppermute | solution.py:19
  32.5 11.3 %collective-permute-start.11 = (bf16[5,112,128]{2,1,0:T(8,128)(2,1)S(1)}, bf16[5,112,128]{2,1,0:T(8,128)(2,1)S(1)}, u32[]{:S(2)}, u32[]{:S(2)}) collective-permute-start(bf16[5,112,128]{2,1,0:T(8,128)(2,1)S(1)} %get-tuple-element.28), channel_id=1, source_target_pairs={{0,4},{2,6},{4,0},{6,2},{1,5},{3,7},{5,1},{7,3},{8,12},{10,14},{12... | collective-permute-start | bytes 430088 | tf_op jit(solution)/shard_map/ppermute | solution.py:19
  35.2 10.7 %collective-permute-start.1 = (bf16[5,112,128]{2,1,0:T(8,128)(2,1)S(1)}, bf16[5,112,128]{2,1,0:T(8,128)(2,1)S(1)}, u32[]{:S(2)}, u32[]{:S(2)}) collective-permute-start(bf16[5,112,128]{2,1,0:T(8,128)(2,1)S(1)} %get-tuple-element.29), channel_id=1, source_target_pairs={{0,2},{2,0},{4,6},{6,4},{1,3},{3,1},{5,7},{7,5},{8,10},{10,8},{12,... | collective-permute-start | bytes 430088 | tf_op jit(solution)/shard_map/ppermute | solution.py:19
  35.8 17.2 %collective-permute-start.3 = (bf16[5,112,128]{2,1,0:T(8,128)(2,1)S(1)}, bf16[5,112,128]{2,1,0:T(8,128)(2,1)S(1)}, u32[]{:S(2)}, u32[]{:S(2)}) collective-permute-start(bf16[5,112,128]{2,1,0:T(8,128)(2,1)S(1)} %get-tuple-element.30), channel_id=1, source_target_pairs={{0,4},{2,6},{4,0},{6,2},{1,5},{3,7},{5,1},{7,3},{8,12},{10,14},{12... | collective-permute-start | bytes 430088 | tf_op jit(solution)/shard_map/ppermute | solution.py:19
  43.9 12.6 %collective-permute-start.14 = (bf16[5,112,128]{2,1,0:T(8,128)(2,1)S(1)}, bf16[5,112,128]{2,1,0:T(8,128)(2,1)S(1)}, u32[]{:S(2)}, u32[]{:S(2)}) collective-permute-start(bf16[5,112,128]{2,1,0:T(8,128)(2,1)S(1)} %fusion.14), channel_id=1, source_target_pairs={{0,20},{2,22},{4,16},{6,18},{8,28},{10,30},{12,24},{14,26},{16,4},... | collective-permute-start | bytes 430088 | tf_op jit(solution)/shard_map/ppermute | solution.py:354
  44.7 12.5 %collective-permute-start.12 = (bf16[5,112,128]{2,1,0:T(8,128)(2,1)S(1)}, bf16[5,112,128]{2,1,0:T(8,128)(2,1)S(1)}, u32[]{:S(2)}, u32[]{:S(2)}) collective-permute-start(bf16[5,112,128]{2,1,0:T(8,128)(2,1)S(1)} %fusion.14), channel_id=1, source_target_pairs={{0,16},{2,18},{4,20},{6,22},{8,24},{10,26},{12,28},{14,30},{16,0},... | collective-permute-start | bytes 430088 | tf_op jit(solution)/shard_map/ppermute | solution.py:354
  53.0 8.4 %collective-permute-start.6 = (bf16[5,112,128]{2,1,0:T(8,128)(2,1)S(1)}, bf16[5,112,128]{2,1,0:T(8,128)(2,1)S(1)}, u32[]{:S(2)}, u32[]{:S(2)}) collective-permute-start(bf16[5,112,128]{2,1,0:T(8,128)(2,1)S(1)} %fusion.3), channel_id=1, source_target_pairs={{0,20},{2,22},{4,16},{6,18},{8,28},{10,30},{12,24},{14,26},{16,4},... | collective-permute-start | bytes 430088 | tf_op jit(solution)/shard_map/ppermute | solution.py:354
  53.5 8.1 %collective-permute-start.4 = (bf16[5,112,128]{2,1,0:T(8,128)(2,1)S(1)}, bf16[5,112,128]{2,1,0:T(8,128)(2,1)S(1)}, u32[]{:S(2)}, u32[]{:S(2)}) collective-permute-start(bf16[5,112,128]{2,1,0:T(8,128)(2,1)S(1)} %fusion.3), channel_id=1, source_target_pairs={{0,16},{2,18},{4,20},{6,22},{8,24},{10,26},{12,28},{14,30},{16,0},... | collective-permute-start | bytes 430088 | tf_op jit(solution)/shard_map/ppermute | solution.py:354
  56.5 8.6 %collective-permute-start.15 = (bf16[5,112,128]{2,1,0:T(8,128)(2,1)S(1)}, bf16[5,112,128]{2,1,0:T(8,128)(2,1)S(1)}, u32[]{:S(2)}, u32[]{:S(2)}) collective-permute-start(bf16[5,112,128]{2,1,0:T(8,128)(2,1)S(1)} %collective-permute-done.14.rest_2_), channel_id=1, source_target_pairs={{0,2},{2,0},{4,6},{6,4},{1,3},{3,1},{5,7},{7,5},{8,10},{10,8},{12,... | collective-permute-start | bytes 430088 | tf_op jit(solution)/shard_map/ppermute | solution.py:19
  57.2 9.0 %collective-permute-start.13 = (bf16[5,112,128]{2,1,0:T(8,128)(2,1)S(1)}, bf16[5,112,128]{2,1,0:T(8,128)(2,1)S(1)}, u32[]{:S(2)}, u32[]{:S(2)}) collective-permute-start(bf16[5,112,128]{2,1,0:T(8,128)(2,1)S(1)} %collective-permute-done.12.rest_0_), channel_id=1, source_target_pairs={{0,2},{2,0},{4,6},{6,4},{1,3},{3,1},{5,7},{7,5},{8,10},{10,8},{12,... | collective-permute-start | bytes 430088 | tf_op jit(solution)/shard_map/ppermute | solution.py:19
  61.4 9.7 %collective-permute-start.7 = (bf16[5,112,128]{2,1,0:T(8,128)(2,1)S(1)}, bf16[5,112,128]{2,1,0:T(8,128)(2,1)S(1)}, u32[]{:S(2)}, u32[]{:S(2)}) collective-permute-start(bf16[5,112,128]{2,1,0:T(8,128)(2,1)S(1)} %collective-permute-done.6.rest_2_), channel_id=1, source_target_pairs={{0,2},{2,0},{4,6},{6,4},{1,3},{3,1},{5,7},{7,5},{8,10},{10,8},{12,... | collective-permute-start | bytes 430088 | tf_op jit(solution)/shard_map/ppermute | solution.py:19
  61.6 9.5 %collective-permute-start.5 = (bf16[5,112,128]{2,1,0:T(8,128)(2,1)S(1)}, bf16[5,112,128]{2,1,0:T(8,128)(2,1)S(1)}, u32[]{:S(2)}, u32[]{:S(2)}) collective-permute-start(bf16[5,112,128]{2,1,0:T(8,128)(2,1)S(1)} %collective-permute-done.4.rest_0_), channel_id=1, source_target_pairs={{0,2},{2,0},{4,6},{6,4},{1,3},{3,1},{5,7},{7,5},{8,10},{10,8},{12,... | collective-permute-start | bytes 430088 | tf_op jit(solution)/shard_map/ppermute | solution.py:19
  66.2 1.0 %copy-start.2 = (bf16[1024,128]{1,0:T(8,128)(2,1)S(1)}, bf16[1024,128]{1,0:T(8,128)(2,1)}, u32[]{:S(2)}) copy-start(bf16[1024,128]{1,0:T(8,128)(2,1)} %synthesis_table.1.table_ref) | copy-start | bytes 786436

commit v2 on v0

v2 whole, which is shorter than its diff:
```python
import functools
import math

import jax
import jax.numpy as jnp
from jax import lax
from jax.experimental import pallas as pl
from jax.experimental.pallas import tpu as pltpu
from jax.sharding import PartitionSpec as P

BAND = 192
JITTER = 6
LANES = 128
ORDER = {}
GROUPS = (
    ((0, 0), (0, 1), (0, 2), (0, 3), (1, 0), (1, 2)),
    ((1, 1), (1, 3)),
)
VMEM_BYTES = 32 * 1024 * 1024


def exchange(value, axis, distance):
    count = lax.axis_size(axis)
    return lax.ppermute(value, axis, [(i, i ^ distance) for i in range(count)])


def after(value, *others):
    return lax.optimization_barrier((value, *others))[0] if others else value


def column_wavenumbers(counts_ref, orders_ref):
    harmonics = orders_ref.shape[1]
    columns = 2 * harmonics
    spread = (
        lax.broadcasted_iota(jnp.int32, (harmonics, columns), 1) // 2
        == lax.broadcasted_iota(jnp.int32, (harmonics, columns), 0)
    )
    orders = jnp.dot(
        orders_ref[...].astype(jnp.float32),
        spread.astype(jnp.float32),
        preferred_element_type=jnp.float32,
    ).astype(jnp.int32)
    return orders[0:1] * counts_ref[0] + orders[1:2] * counts_ref[1]


def table_factors(wave, first_row, rows, total_pitch, turn):
    fine = 32
    coarse = rows // fine
    columns = wave.shape[1]
    step = 2.0 * math.pi / total_pitch
    at_coarse = first_row + fine * lax.broadcasted_iota(jnp.int32, (coarse, columns), 0)
    at_fine = lax.broadcasted_iota(jnp.int32, (fine, columns), 0)
    odd = lax.broadcasted_iota(jnp.int32, (fine, columns), 1) % 2
    q_coarse = lax.rem(at_coarse * wave, total_pitch)
    q_fine = lax.rem(at_fine * wave - odd * (total_pitch // 4), total_pitch)
    a = step * q_coarse.astype(jnp.float32)
    b = step * q_fine.astype(jnp.float32) + turn
    return jnp.cos(a), jnp.sin(a), jnp.cos(b), jnp.sin(b)


def fill_table(ref, at, factors, scale):
    cos_a, sin_a, cos_b, sin_b = factors
    fine = cos_b.shape[0]
    cos_b = cos_b * scale
    sin_b = sin_b * scale
    for i in range(cos_a.shape[0]):
        value = cos_a[i : i + 1] * cos_b - sin_a[i : i + 1] * sin_b
        ref[at + (pl.ds(i * fine, fine), slice(None))] = value.astype(ref.dtype)


def geometry(outlet_shape, stator_rows):
    rows = outlet_shape[-2]
    total_rows = 2 * rows
    rs_loc = stator_rows // 2
    slope = (stator_rows - 1) / (total_rows - BAND)
    above = math.floor((rows - 1 + JITTER) * slope) + 1 - rs_loc
    below = rs_loc - math.ceil((rows - BAND + 1 - JITTER) * slope)
    halo = -(-max(above, below) // 16) * 16
    reach = max(
        rows - math.floor(rs_loc / slope - JITTER),
        math.floor((rs_loc - 1) / slope + JITTER) + BAND - rows,
    )
    edge = -(-reach // LANES) * LANES
    return rs_loc, halo, edge


def window(first, number):
    starts = [at // LANES * LANES for at in first]
    width = max(-(-(at + number) // LANES) * LANES - start for at, start in zip(first, starts))
    return starts, width


def by_span(span_at, values, multiple):
    return pl.multiple_of(jnp.where(span_at == 0, values[0], values[1]), multiple)


def flip_weights(weight_ref, starts_ref, first_row, first_column, flipped):
    rows, width = weight_ref.shape
    row = first_row + lax.broadcasted_iota(jnp.int32, (rows, LANES), 0)
    for block in range(width // LANES):
        start = starts_ref[pl.ds(first_column // LANES + block, 1), :]
        inside = (row >= start) & (row < start + BAND)
        at = slice(block * LANES, (block + 1) * LANES)
        value = jnp.where(inside, weight_ref[:, at].astype(jnp.float32), 0.0)
        flipped[at, :] = value.T.astype(flipped.dtype)


def instance_turn(wave, instance, period):
    whole = period.astype(jnp.float32)
    steps = (wave * instance).astype(jnp.float32)
    return (2.0 * math.pi) * (steps - whole * jnp.floor(steps / whole)) / whole


def fill_analysis(wave, counts_ref, part, instances, total_pitch, table_ref):
    pitch = table_ref.shape[0]
    instance = lax.axis_index("row") * instances + part
    period = lax.axis_size("row") * instances * counts_ref[0]
    turn = instance_turn(wave, instance, period)
    factors = table_factors(wave, lax.axis_index("pitch") * pitch, pitch, total_pitch, turn)
    fill_table(table_ref, (), factors, math.sqrt(2.0 / total_pitch))


def started(*copies):
    for copy in copies:
        copy.start()
    return copies


def edge_kernel(
    sizes, counts_hbm, orders_hbm, starts_hbm, weight_hbm, planes_hbm, *rest,
):
    instances, fields, rs_loc, halo, edge, total_pitch = sizes
    halo_refs, (table_ref, planes_ref, mask_ref) = rest[:instances], rest[instances : instances + 3]
    counts, orders, starts, weight, edges, flipped, spectra, sems, plane_sems = rest[
        instances + 3 :
    ]
    rows, pitch = planes_hbm.shape[1:]
    others = rows - edge
    span_at = lax.axis_index("span")
    first_halo = (rs_loc, rs_loc - halo)
    columns, width = window(first_halo, halo)
    first_row = pl.multiple_of((1 - span_at) * (rows - edge), 16)
    first_column = by_span(span_at, columns, LANES)
    small = started(
        pltpu.make_async_copy(counts_hbm, counts, sems.at[0]),
        pltpu.make_async_copy(orders_hbm, orders, sems.at[1]),
        pltpu.make_async_copy(starts_hbm, starts, sems.at[2]),
        pltpu.make_async_copy(
            weight_hbm.at[pl.ds(first_row, edge), pl.ds(first_column, width)], weight, sems.at[3]
        ),
    )
    edge_rows = pl.ds(first_row, edge)
    other_rows = pl.ds(pl.multiple_of(span_at * edge, 16), others)
    fetched = started(
        pltpu.make_async_copy(
            planes_hbm.at[pl.ds(0, fields), edge_rows, :],
            planes_ref.at[:, edge_rows, :],
            plane_sems.at[0],
        ),
        *(
            pltpu.make_async_copy(
                planes_hbm.at[pl.ds(j * fields, fields), edge_rows, :],
                edges.at[j - 1],
                plane_sems.at[j],
            )
            for j in range(1, instances)
        ),
    )
    (rest_fetched,) = started(
        pltpu.make_async_copy(
            planes_hbm.at[pl.ds(0, fields), other_rows, :],
            planes_ref.at[:, other_rows, :],
            plane_sems.at[instances],
        )
    )
    pitch_at = lax.axis_index("pitch")
    for k in range(mask_ref.shape[0]):
        halo_at = jnp.where(span_at == 0, mask_ref.shape[0] - 1, 0)
        at_halo = jnp.bitwise_xor(pitch_at, k) == halo_at
        mask_ref[k] = jnp.full(mask_ref.shape[1:], at_halo.astype(jnp.float32))
    for copy in small[:2]:
        copy.wait()
    wave = column_wavenumbers(counts, orders)
    for j in range(instances):
        fill_analysis(wave, counts, j, instances, total_pitch, table_ref.at[j])
    for copy in small[2:]:
        copy.wait()
    flip_weights(weight, starts, span_at * rows + first_row, first_column, flipped)
    inner = [first - start for first, start in zip(first_halo, columns)]
    weights = flipped[pl.ds(by_span(span_at, inner, 16), halo), :]
    number = table_ref.shape[2]
    for j in range(instances):
        fetched[j].wait()
        taken = planes_ref[:, edge_rows, :] if j == 0 else edges[j - 1]
        result = jnp.dot(
            taken.reshape(fields * edge, pitch),
            table_ref[j],
            preferred_element_type=jnp.float32,
        ).astype(jnp.bfloat16)
        for f in range(fields):
            at = (j * fields + f) * number
            spectra[:, at : at + number] = result[f * edge : (f + 1) * edge]
    result = jnp.dot(weights, spectra[...], preferred_element_type=jnp.float32)
    for j in range(instances):
        for f in range(fields):
            at = (j * fields + f) * number
            halo_refs[j][f] = result[:, at : at + number].astype(jnp.bfloat16)
    rest_fetched.wait()


def edge_call(sizes, shards, counts, orders, starts, weight, planes):
    instances, fields, rs_loc, halo, edge, total_pitch = sizes
    pitch = planes.shape[2]
    columns = 2 * orders.shape[1]
    width = window((rs_loc, rs_loc - halo), halo)[1]
    count = instances * fields
    vmem = pl.BlockSpec(memory_space=pltpu.VMEM)
    hbm = pl.BlockSpec(memory_space=pltpu.HBM)
    return pl.pallas_call(
        functools.partial(edge_kernel, sizes),
        out_shape=[jax.ShapeDtypeStruct((fields, halo, columns), jnp.bfloat16)] * instances
        + [
            jax.ShapeDtypeStruct((instances, pitch, columns), jnp.bfloat16),
            pltpu.VMEM((fields, *planes.shape[1:]), jnp.bfloat16),
            jax.ShapeDtypeStruct((shards, 8, columns), jnp.float32),
        ],
        in_specs=[hbm] * 5,
        out_specs=[vmem] * (instances + 3),
        scratch_shapes=[
            pltpu.SMEM(counts.shape, jnp.int32),
            pltpu.VMEM(orders.shape, jnp.int32),
            pltpu.VMEM(starts.shape, jnp.int32),
            pltpu.VMEM((edge, width), jnp.bfloat16),
            pltpu.VMEM((max(instances - 1, 1), fields, edge, pitch), jnp.bfloat16),
            pltpu.VMEM((width, edge), jnp.bfloat16),
            pltpu.VMEM((edge, count * columns), jnp.bfloat16),
            pltpu.SemaphoreType.DMA((4,)),
            pltpu.SemaphoreType.DMA((instances + 1,)),
        ],
        compiler_params=pltpu.CompilerParams(vmem_limit_bytes=VMEM_BYTES),
        cost_estimate=pl.CostEstimate(
            flops=2 * count * edge * columns * (pitch + halo),
            bytes_accessed=2 * count * edge * pitch,
            transcendentals=0,
        ),
        name="edge",
    )(counts, orders, starts, weight, planes)


def analyse_planes(planes_ref, table_ref, band_ref, spectra, out_refs):
    fields, rows, pitch = planes_ref.shape
    columns = table_ref.shape[1]
    per = band_ref.shape[0] // len(out_refs)
    result = jnp.dot(
        planes_ref[...].reshape(fields * rows, pitch),
        table_ref[...],
        preferred_element_type=jnp.float32,
    ).astype(jnp.bfloat16)
    for f in range(fields):
        spectra[:, f * columns : (f + 1) * columns] = result[f * rows : (f + 1) * rows]
    result = jnp.dot(band_ref[...], spectra[...], preferred_element_type=jnp.float32)
    for k, out_ref in enumerate(out_refs):
        for f in range(fields):
            out_ref[f] = result[
                k * per : (k + 1) * per, f * columns : (f + 1) * columns
            ].astype(out_ref.dtype)


def next_planes(planes_hbm, part, next_ref, sem):
    return pltpu.make_async_copy(
        planes_hbm.at[pl.ds((part + 1) * next_ref.shape[0], next_ref.shape[0])], next_ref, sem
    )


def first_kernel(
    sizes, shards, starts_hbm, weight_hbm, planes_hbm, planes_ref, table_ref, *rest,
):
    instances, fields, rs_loc, halo, edge, total_pitch = sizes
    out_refs, band_ref, next_refs = rest[:shards], rest[shards], rest[shards + 1 : -5]
    starts, weight, flipped, spectra, sems = rest[-5:]
    rows = weight_hbm.shape[0]
    per = rs_loc // shards
    span_at = lax.axis_index("span")
    pitch_at = lax.axis_index("pitch")
    columns, width = window((0, rs_loc), rs_loc)
    first_column = by_span(span_at, columns, LANES)
    small = started(
        pltpu.make_async_copy(starts_hbm, starts, sems.at[0]),
        pltpu.make_async_copy(weight_hbm.at[:, pl.ds(first_column, width)], weight, sems.at[1]),
    )
    following = started(*(next_planes(planes_hbm, 0, ref, sems.at[2]) for ref in next_refs))
    for copy in small:
        copy.wait()
    flip_weights(weight, starts, span_at * rows, first_column, flipped)
    own = by_span(span_at, (0, rs_loc - columns[1]), 16)
    for k in range(shards):
        at = jnp.bitwise_xor(pitch_at, k) if shards > 1 else 0
        source = pl.multiple_of(own + at * per, 16)
        band_ref[k * per : (k + 1) * per] = flipped[pl.ds(source, per), :]
    analyse_planes(planes_ref, table_ref.at[0], band_ref, spectra, out_refs)
    for copy in following:
        copy.wait()


def own_shapes(shards, fields, per, columns):
    kinds = [jnp.bfloat16 if k % 2 else jnp.float32 for k in range(shards)]
    return [jax.ShapeDtypeStruct((fields, per, columns), kind) for kind in kinds]


def first_call(sizes, shards, starts, weight, planes, held, table):
    instances, fields, rs_loc, halo, edge, total_pitch = sizes
    rows, pitch = planes.shape[1:]
    columns = table.shape[2]
    width = window((0, rs_loc), rs_loc)[1]
    vmem = pl.BlockSpec(memory_space=pltpu.VMEM)
    hbm = pl.BlockSpec(memory_space=pltpu.HBM)
    following = [pltpu.VMEM((fields, rows, pitch), jnp.bfloat16)] * (instances > 1)
    return pl.pallas_call(
        functools.partial(first_kernel, sizes, shards),
        out_shape=own_shapes(shards, fields, rs_loc // shards, columns)
        + [jax.ShapeDtypeStruct((rs_loc, rows), jnp.bfloat16)]
        + following,
        in_specs=[hbm, hbm, hbm, vmem, vmem],
        out_specs=[vmem] * (shards + 1 + len(following)),
        scratch_shapes=[
            pltpu.VMEM(starts.shape, jnp.int32),
            pltpu.VMEM((rows, width), jnp.bfloat16),
            pltpu.VMEM((width, rows), jnp.bfloat16),
            pltpu.VMEM((rows, fields * columns), jnp.bfloat16),
            pltpu.SemaphoreType.DMA((3,)),
        ],
        compiler_params=pltpu.CompilerParams(vmem_limit_bytes=VMEM_BYTES),
        cost_estimate=pl.CostEstimate(
            flops=2 * fields * rows * columns * (pitch + rs_loc),
            bytes_accessed=2 * fields * rows * pitch,
            transcendentals=0,
        ),
        name="first_part",
    )(starts, weight, planes, held, table)


def later_kernel(
    sizes, shards, part,
    counts_hbm, orders_hbm, planes_hbm, planes_ref, table_ref, band_ref, after_ref, *rest,
):
    out_refs, synthesis_ref, next_refs = rest[:shards], rest[shards], rest[shards + 1 : -4]
    counts, orders, spectra, sems = rest[-4:]
    small = started(
        pltpu.make_async_copy(counts_hbm, counts, sems.at[0]),
        pltpu.make_async_copy(orders_hbm, orders, sems.at[1]),
    )
    following = started(*(next_planes(planes_hbm, part, ref, sems.at[2]) for ref in next_refs))
    analyse_planes(planes_ref, table_ref.at[part], band_ref, spectra, out_refs)
    for copy in small:
        copy.wait()
    wave = column_wavenumbers(counts, orders)
    pitch = synthesis_ref.shape[0]
    factors = table_factors(wave, lax.axis_index("pitch") * pitch, pitch, sizes[-1], 0.0)
    fill_table(synthesis_ref, (), factors, 1.0 / math.sqrt(wave.shape[1] // 2))
    for copy in following:
        copy.wait()


def later_call(sizes, shards, part, counts, orders, planes, held, table, band, after):
    instances, fields, rs_loc, halo, edge, total_pitch = sizes
    rows, pitch = planes.shape[1:]
    columns = table.shape[2]
    vmem = pl.BlockSpec(memory_space=pltpu.VMEM)
    hbm = pl.BlockSpec(memory_space=pltpu.HBM)
    following = [pltpu.VMEM((fields, rows, pitch), jnp.bfloat16)] * (part + 1 < instances)
    return pl.pallas_call(
        functools.partial(later_kernel, sizes, shards, part),
        out_shape=own_shapes(shards, fields, rs_loc // shards, columns)
        + [jax.ShapeDtypeStruct((pitch, columns), jnp.bfloat16)]
        + following,
        in_specs=[hbm, hbm, hbm, vmem, vmem, vmem, pl.BlockSpec(memory_space=pl.ANY)],
        out_specs=[vmem] * (shards + 1 + len(following)),
        scratch_shapes=[
            pltpu.SMEM(counts.shape, jnp.int32),
            pltpu.VMEM(orders.shape, jnp.int32),
            pltpu.VMEM((rows, fields * columns), jnp.bfloat16),
            pltpu.SemaphoreType.DMA((3,)),
        ],
        compiler_params=pltpu.CompilerParams(vmem_limit_bytes=VMEM_BYTES),
        cost_estimate=pl.CostEstimate(
            flops=2 * fields * rows * columns * (pitch + rs_loc),
            bytes_accessed=2 * fields * rows * pitch,
            transcendentals=0,
        ),
        name="later_part",
    )(counts, orders, planes, held, table, band, after)


def synthesise_kernel(fields, ranks, shards, per, table_ref, *rest):
    piece_refs = rest[: len(ranks)]
    out_hbm, rows_ref, sems = rest[-3:]
    pitch_at = lax.axis_index("pitch")
    copies = []
    for i, (part, k) in enumerate(ranks):
        piece = piece_refs[i][...]
        value = lax.dot_general(
            piece.reshape(fields * per, piece.shape[2]),
            table_ref[...],
            (((1,), (1,)), ((), ())),
            preferred_element_type=jnp.float32,
        )
        rows_ref[i] = value.astype(rows_ref.dtype).reshape(fields, per, value.shape[1])
        at = jnp.bitwise_xor(pitch_at, k) if shards > 1 else 0
        copies += started(
            pltpu.make_async_copy(
                rows_ref.at[i],
                out_hbm.at[
                    pl.ds(part * fields, fields), pl.ds(pl.multiple_of(at * per, 16), per), :
                ],
                sems.at[i],
            )
        )
    for copy in copies:
        copy.wait()


def synthesise_call(count, shards, table, pieces, base):
    ranks = list(pieces)
    fields, per, columns = pieces[ranks[0]].shape
    pitch = table.shape[0]
    vmem = pl.BlockSpec(memory_space=pltpu.VMEM)
    hbm = pl.BlockSpec(memory_space=pltpu.HBM)
    operands = [table, *pieces.values()]
    in_specs = [vmem] * len(operands)
    aliases = {}
    if base is not None:
        aliases = {len(operands): 0}
        operands.append(base)
        in_specs.append(hbm)
    return pl.pallas_call(
        functools.partial(synthesise_kernel, fields, ranks, shards, per),
        out_shape=jax.ShapeDtypeStruct((count, per * shards, pitch), jnp.bfloat16),
        in_specs=in_specs,
        out_specs=hbm,
        scratch_shapes=[
            pltpu.VMEM((len(ranks), fields, per, pitch), jnp.bfloat16),
            pltpu.SemaphoreType.DMA((len(ranks),)),
        ],
        input_output_aliases=aliases,
        compiler_params=pltpu.CompilerParams(vmem_limit_bytes=VMEM_BYTES),
        cost_estimate=pl.CostEstimate(
            flops=2 * len(ranks) * fields * per * columns * pitch,
            bytes_accessed=2 * len(ranks) * fields * per * pitch,
            transcendentals=0,
        ),
        name="synthesise",
    )(*operands)


def body(outlet, remap_weight, band_start, blade_counts, mode_orders):
    row_count = lax.axis_size("row")
    pitch_count = lax.axis_size("pitch")
    instances, fields, rows, pitch = outlet.shape[1:]
    stator_rows = remap_weight.shape[1]
    total_pitch = pitch * pitch_count
    rs_loc, halo_rows, edge = geometry(outlet.shape, stator_rows)
    count = instances * fields
    by_shards = (
        pitch_count == 4
        and rs_loc % (16 * pitch_count) == 0
        and halo_rows == rs_loc // pitch_count
    )
    shards = pitch_count if by_shards else 1
    shift = row_count // 2

    def stay(value):
        return pltpu.with_memory_space_constraint(value, pltpu.HBM)

    planes = stay(outlet.reshape(count, rows, pitch))
    orders = stay(mode_orders.T)
    starts = stay(band_start.reshape(stator_rows // LANES, LANES))
    blade_counts = stay(blade_counts)
    remap_weight = stay(remap_weight)
    sizes = (instances, fields, rs_loc, halo_rows, edge, total_pitch)
    *halos, table, held, masks = edge_call(
        sizes, shards, blade_counts, orders, starts, remap_weight, planes
    )
    made = first_call(sizes, shards, starts, remap_weight, planes, held, table)
    owns, band, held = [made[:shards]], made[shards], made[-1]
    known = {}

    def get(kind, part):
        if (kind, part) not in known:
            known[kind, part] = steps[kind](part)
        return known[kind, part]

    def ready(kind, part, value):
        return after(value, *(get(*step) for step in ORDER.get((kind, part), ())))

    def later(part):
        if part == 0:
            return owns[0][-1]
        first_sent = halos[0] if shards == 1 else get("meet", 0)[1]
        made = later_call(
            sizes, shards, part, blade_counts, orders, planes,
            known.get(("held", part), held), table, band, ready("later", part, first_sent),
        )
        owns.append(made[:shards])
        known["synthesis", 0] = made[shards]
        known["held", part + 1] = made[-1]
        return made[0]

    def halo(part):
        return exchange(ready("halo", part, halos[part]), "span", 1)

    def with_halo(part, k, *terms):
        get("later", part)
        total = jnp.where(masks[k, :1] > 0.0, get("halo", part).astype(jnp.float32), 0.0)
        for term in (owns[part][k], *terms):
            total = total + term.astype(jnp.float32)
        return total.astype(jnp.bfloat16)

    def meet(part):
        return None, with_halo(part, 3)

    def pair(part):
        return exchange(ready("pair", part, get("meet", part)[1]), "pitch", 1)

    def beside(part):
        return exchange(ready("beside", part, with_halo(part, 1)), "pitch", 1)

    def across(part):
        return exchange(
            ready("across", part, with_halo(part, 2, get("pair", part))), "pitch", 2
        )

    def total(part):
        return with_halo(part, 0, get("beside", part), get("across", part))

    def spread(value, k):
        pairs = [
            (g * pitch_count + z, ((g + shift) % row_count) * pitch_count + (z ^ k))
            for g in range(row_count)
            for z in range(pitch_count)
        ]
        return lax.ppermute(value, ("row", "pitch"), pairs)

    def swap(part):
        return spread(ready("swap", part, get("total", part)), 0)

    def swap_across(part):
        return spread(ready("swap_across", part, get("total", part)), 2)

    def swap_on(part):
        return exchange(ready("swap_on", part, get("swap", part)), "pitch", 1)

    def across_on(part):
        return exchange(ready("across_on", part, get("swap_across", part)), "pitch", 1)

    steps = dict(
        later=later, halo=halo, meet=meet, pair=pair, beside=beside, across=across, total=total,
        swap=swap, swap_across=swap_across, swap_on=swap_on, across_on=across_on,
    )
    names = ("swap", "swap_on", "swap_across", "across_on")

    def whole_sum(part):
        get("later", part)
        wide = get("halo", part).astype(jnp.float32)
        low = jnp.pad(wide, ((0, 0), (rs_loc - halo_rows, 0), (0, 0)))
        high = jnp.pad(wide, ((0, 0), (0, rs_loc - halo_rows), (0, 0)))
        mine = owns[part][0] + jnp.where(lax.axis_index("span") == 0, low, high)
        return lax.psum(mine, "pitch").astype(jnp.bfloat16)

    joined = None
    if by_shards:
        for group in GROUPS:
            group = {(part, k): get(names[k], part) for part, k in group}
            joined = synthesise_call(count, shards, known["synthesis", 0], group, joined)
    else:
        pairs = [(g, (g + shift) % row_count) for g in range(row_count)]
        pieces = {
            (part, 0): lax.ppermute(whole_sum(part), "row", pairs) for part in range(instances)
        }
        joined = synthesise_call(count, shards, known["synthesis", 0], pieces, joined)
    return joined.reshape(1, instances, fields, rs_loc, pitch)


def solution(mesh):
    placed = (P("row", None, None, "span", "pitch"), P("span", None), P(), P(), P())
    return jax.shard_map(
        body,
        mesh=mesh,
        in_specs=placed,
        out_specs=P("row", None, None, "span", "pitch"),
        check_vma=False,
    )
```

time: 177 us -> 61.9 us (0.35)
  waiting for transfers between devices: 117 us -> 23.7 us
  local copies, waits for them, and re-layouts: 23.5 us -> 0 us
  starting transfers between devices: 1.6 us -> 22.2 us
  matrix products: 16 us -> 0 us
  Pallas kernels: 0 us -> 15.2 us
  between operations: 13.9 us -> 0.09 us
  other arithmetic: 4.83 us -> 0.48 us
    reduce_scatter x1 -> x0, waiting for transfers between devices: 52.7 us -> none  [body(): lax.psum_scatter(lax.dot_general(local_table, flattened, (((0,), (1,)), (...]
    all_gather x1 -> x0, waiting for transfers between devices: 32.5 us -> none  [body(): shard_piece = lax.all_gather(remapped, 'pitch', axis=0, tiled=True)]
    unnamed x4 -> x0, waiting for transfers between devices: 23.7 us -> none
    ppermute x1 -> x16, starting transfers between devices: 1.52 us -> 22.2 us  [the longest x12 16.3 us: exchange(): return lax.ppermute(value, axis, [(i, i ^ distance) for i in range(count)])]
    dot_general x3 -> x0, matrix products: 16 us -> none  [the longest x1 9 us: body(): lax.dot_general(local_table, flattened, (((0,), (1,)), ((), ())), preferr...]
    ppermute x1 -> x16, waiting for transfers between devices: 7.99 us -> 23.7 us  [the longest x12 19.4 us: exchange(): return lax.ppermute(value, axis, [(i, i ^ distance) for i in range(count)])]
    unnamed x10 -> x0, local copies, waits for them, and re-layouts: 15.4 us -> none
    pallas_call x0 -> x5, Pallas kernels: none -> 15.2 us  [the longest x2 5.24 us: synthesise_call(): pl.pallas_call(functools.partial(synthesise_kernel, fields, ranks, shards...]
  transfers between devices with their start and end apart: 4 -> 16, of which waited for: 4 -> 9; matrix products, arithmetic and copies ran while one was open for 1% -> 0% of each run, Pallas kernels for 0% -> 16%
where the time goes in v2:
time: 61.9 us; the launch traced here: 61.7 us
  waiting for transfers between devices  23.7 us (38%)
  starting transfers between devices  22.2 us (36%)
  Pallas kernels  15.2 us (25%)
    ppermute x12, waiting for transfers between devices, exchange(): return lax.ppermute(value, axis, [(i, i ^ distance) for i in range(count)])  19.4 us
    ppermute x12, starting transfers between devices, exchange(): return lax.ppermute(value, axis, [(i, i ^ distance) for i in range(count)])  16.3 us
    ppermute x4, starting transfers between devices, spread(): return lax.ppermute(value, ('row', 'pitch'), pairs)  5.92 us
    pallas_call x2, Pallas kernels, synthesise_call(): pl.pallas_call(functools.partial(synthesise_kernel, fields, ranks, shards...  5.24 us
    ppermute x4, waiting for transfers between devices, spread(): return lax.ppermute(value, ('row', 'pitch'), pairs)  4.28 us
    pallas_call x1, Pallas kernels, edge_call(): pl.pallas_call(functools.partial(edge_kernel, sizes), out_shape=[jax.Shap...  3.68 us
    pallas_call x1, Pallas kernels, first_call(): pl.pallas_call(functools.partial(first_kernel, sizes, shards), out_shape=...  3.5 us
    pallas_call x1, Pallas kernels, later_call(): pl.pallas_call(functools.partial(later_kernel, sizes, shards, part), out_...  2.8 us
  transfers between devices with their start and end apart: 16, of which 9 were waited for; matrix products, arithmetic and copies ran while one was open for 0% of the time, Pallas kernels for 16%

profile of v2, /device:TPU:0, one launch (start us, length us, event | category | flops | bytes accessed | tf_op | source)
XLA Modules:
  0.0 61.7 jit_solution(16175384543726196636)
XLA Ops:
  0.0 3.7 %edge.1 = (bf16[5,112,128]{2,1,0:T(8,128)(2,1)S(1)}, bf16[5,112,128]{2,1,0:T(8,128)(2,1)S(1)}, bf16[2,1024,128]{2,1,0:T(8,128)(2,1)S(1)}, bf16[5,512,1024]{2,1,0:T(8,128)(2,1)S(1)}, f32[4,8,128]{2,1,0:T(8,128)S(1)}) custom-call(s32[2]{0:T(128)} %counts_hbm.3, s32[2,64]{1,0:T(2,128)} %bitcast.17, s32[7,128]{1,0:T(8,128)} %bitcast.15, ...), custom_call_target="tpu_custom_call" | custom-call | flops 372244480 | bytes 2621440 | tf_op jit(solution)/shard_map/edge/pallas_call | solution.py:219
  3.7 3.0 %collective-permute-start = (bf16[5,112,128]{2,1,0:T(8,128)(2,1)S(1)}, bf16[5,112,128]{2,1,0:T(8,128)(2,1)S(1)}, u32[]{:S(2)}, u32[]{:S(2)}) collective-permute-start(bf16[5,112,128]{2,1,0:T(8,128)(2,1)S(1)} %get-tuple-element.26), channel_id=1, source_target_pairs={{0,1},{1,0},{2,3},{3,2},{4,5},{5,4},{6,7},{7,6},{8,9},{9,8},{10,11... | collective-permute-start | bytes 430088 | tf_op jit(solution)/shard_map/ppermute | solution.py:24
  6.7 0.1 collective-permute-start.1
  6.8 3.5 %first_part.1 = (f32[5,112,128]{2,1,0:T(8,128)S(1)}, bf16[5,112,128]{2,1,0:T(8,128)(2,1)S(1)}, f32[5,112,128]{2,1,0:T(8,128)S(1)}, bf16[5,112,128]{2,1,0:T(8,128...) custom-call(s32[7,128]{1,0:T(8,128)} %bitcast.16, bf16[512,896]{1,0:T(8,128)(2,1)} %weight_hbm.3, ...), custom_call_target="tpu_custom_call" | custom-call | flops 964689920 | bytes 5242880 | tf_op jit(solution)/shard_map/first_part/pallas_call | solution.py:318
  10.3 1.0 %collective-permute-done = bf16[5,112,128]{2,1,0:T(8,128)(2,1)S(1)} collective-permute-done((bf16[5,112,128]{2,1,0:T(8,128)(2,1)S(1)}, bf16[5,112,128]{2,1,0:T(8,128)(2,1)S(1)}, u32[]{:S(2)}, u32[]{:S(2)}) %collective-permute-start) | collective-permute-done | bytes 143392 | tf_op jit(solution)/shard_map/ppermute | solution.py:24
  11.3 0.1 fusion.1.after_ref
  11.3 2.8 %later_part.1 = (f32[5,112,128]{2,1,0:T(8,128)S(1)}, bf16[5,112,128]{2,1,0:T(8,128)(2,1)S(1)}, f32[5,112,128]{2,1,0:T(8,128)S(1)}, bf16[5,112,128]{2,1,0:T(8,128)(2,1)S(1)}, bf16[1024,128]{1,0:T(8,128)(2,1)S(1)}) custom-call(s32[2]{0:T(128)} %counts_hbm.3, s32[2,64]{1,0:T(2,128)} %bitcast.18, bf16[10,512,1024]{2,1,0:T(8,128)(2,1)} %bitcast.14, ...), custom_call_target="tpu_custom_call" | custom-call | flops 964689920 | bytes 5242880 | tf_op jit(solution)/shard_map/later_part/pallas_call | solution.py:371
  14.2 0.0 collective-permute-done.1
  14.2 0.1 fusion.21
  14.2 2.2 %collective-permute-start.3 = (bf16[5,112,128]{2,1,0:T(8,128)(2,1)S(1)}, bf16[5,112,128]{2,1,0:T(8,128)(2,1)S(1)}, u32[]{:S(2)}, u32[]{:S(2)}) collective-permute-start(bf16[5,112,128]{2,1,0:T(8,128)(2,1)S(1)} %fusion.21), channel_id=1, source_target_pairs={{0,2},{2,0},{4,6},{6,4},{1,3},{3,1},{5,7},{7,5},{8,10},{10,8},{12,... | collective-permute-start | bytes 430088 | tf_op jit(solution)/shard_map/ppermute | solution.py:24
  16.4 0.1 collective-permute-start.10
  16.5 3.6 %collective-permute-done.3 = bf16[5,112,128]{2,1,0:T(8,128)(2,1)S(1)} collective-permute-done((bf16[5,112,128]{2,1,0:T(8,128)(2,1)S(1)}, bf16[5,112,128]{2,1,0:T(8,128)(2,1)S(1)}, u32[]{:S(2)}, u32[]{:S(2)}) %collective-permute-start.3) | collective-permute-done | bytes 143392 | tf_op jit(solution)/shard_map/ppermute | solution.py:24
  20.1 1.5 %collective-permute-done.10 = bf16[5,112,128]{2,1,0:T(8,128)(2,1)S(1)} collective-permute-done((bf16[5,112,128]{2,1,0:T(8,128)(2,1)S(1)}, bf16[5,112,128]{2,1,0:T(8,128)(2,1)S(1)}, u32[]{:S(2)}, u32[]{:S(2)}) %collective-permute-start.10) | collective-permute-done | bytes 143392 | tf_op jit(solution)/shard_map/ppermute | solution.py:24
  21.7 0.2 fusion.16
  21.9 1.7 %collective-permute-start.2 = (bf16[5,112,128]{2,1,0:T(8,128)(2,1)S(1)}, bf16[5,112,128]{2,1,0:T(8,128)(2,1)S(1)}, u32[]{:S(2)}, u32[]{:S(2)}) collective-permute-start(bf16[5,112,128]{2,1,0:T(8,128)(2,1)S(1)} %get-tuple-element.39), channel_id=1, source_target_pairs={{0,2},{2,0},{4,6},{6,4},{1,3},{3,1},{5,7},{7,5},{8,10},{10,8},{12,... | collective-permute-start | bytes 430088 | tf_op jit(solution)/shard_map/ppermute | solution.py:24
  23.6 2.6 %collective-permute-start.4 = (bf16[5,112,128]{2,1,0:T(8,128)(2,1)S(1)}, bf16[5,112,128]{2,1,0:T(8,128)(2,1)S(1)}, u32[]{:S(2)}, u32[]{:S(2)}) collective-permute-start(bf16[5,112,128]{2,1,0:T(8,128)(2,1)S(1)} %get-tuple-element.40), channel_id=1, source_target_pairs={{0,4},{2,6},{4,0},{6,2},{1,5},{3,7},{5,1},{7,3},{8,12},{10,14},{12... | collective-permute-start | bytes 430088 | tf_op jit(solution)/shard_map/ppermute | solution.py:24
  26.2 0.3 collective-permute-start.11
  26.5 0.4 collective-permute-start.9
  26.9 2.6 %collective-permute-done.2 = bf16[5,112,128]{2,1,0:T(8,128)(2,1)S(1)} collective-permute-done((bf16[5,112,128]{2,1,0:T(8,128)(2,1)S(1)}, bf16[5,112,128]{2,1,0:T(8,128)(2,1)S(1)}, u32[]{:S(2)}, u32[]{:S(2)}) %collective-permute-start.2) | collective-permute-done | bytes 143392 | tf_op jit(solution)/shard_map/ppermute | solution.py:24
  29.5 5.4 %collective-permute-done.4 = bf16[5,112,128]{2,1,0:T(8,128)(2,1)S(1)} collective-permute-done((bf16[5,112,128]{2,1,0:T(8,128)(2,1)S(1)}, bf16[5,112,128]{2,1,0:T(8,128)(2,1)S(1)}, u32[]{:S(2)}, u32[]{:S(2)}) %collective-permute-start.4) | collective-permute-done | bytes 143392 | tf_op jit(solution)/shard_map/ppermute | solution.py:24
  34.8 1.5 %collective-permute-done.11 = bf16[5,112,128]{2,1,0:T(8,128)(2,1)S(1)} collective-permute-done((bf16[5,112,128]{2,1,0:T(8,128)(2,1)S(1)}, bf16[5,112,128]{2,1,0:T(8,128)(2,1)S(1)}, u32[]{:S(2)}, u32[]{:S(2)}) %collective-permute-start.11) | collective-permute-done | bytes 143392 | tf_op jit(solution)/shard_map/ppermute | solution.py:24
  36.4 0.0 collective-permute-done.9
  36.4 0.2 fusion.5
  36.6 1.5 %collective-permute-start.14 = (bf16[5,112,128]{2,1,0:T(8,128)(2,1)S(1)}, bf16[5,112,128]{2,1,0:T(8,128)(2,1)S(1)}, u32[]{:S(2)}, u32[]{:S(2)}) collective-permute-start(bf16[5,112,128]{2,1,0:T(8,128)(2,1)S(1)} %get-tuple-element.47), channel_id=1, source_target_pairs={{0,20},{2,22},{4,16},{6,18},{8,28},{10,30},{12,24},{14,26},{16,4},... | collective-permute-start | bytes 430088 | tf_op jit(solution)/shard_map/ppermute | solution.py:541
  38.1 0.5 collective-permute-start.12
  38.6 3.4 %collective-permute-start.7 = (bf16[5,112,128]{2,1,0:T(8,128)(2,1)S(1)}, bf16[5,112,128]{2,1,0:T(8,128)(2,1)S(1)}, u32[]{:S(2)}, u32[]{:S(2)}) collective-permute-start(bf16[5,112,128]{2,1,0:T(8,128)(2,1)S(1)} %get-tuple-element.48), channel_id=1, source_target_pairs={{0,20},{2,22},{4,16},{6,18},{8,28},{10,30},{12,24},{14,26},{16,4},... | collective-permute-start | bytes 430088 | tf_op jit(solution)/shard_map/ppermute | solution.py:541
  42.0 0.5 collective-permute-start.5
  42.5 4.3 %collective-permute-done.14.rest_2_ = bf16[5,112,128]{2,1,0:T(8,128)(2,1)S(1)} collective-permute-done((bf16[5,112,128]{2,1,0:T(8,128)(2,1)S(1)}, bf16[5,112,128]{2,1,0:T(8,128)(2,1)S(1)}, u32[]{:S(2)}, u32[]{:S(2)}) %collective-permute-start.14) | collective-permute-done | bytes 143392 | tf_op jit(solution)/shard_map/ppermute | solution.py:541
  46.7 1.2 %collective-permute-start.15 = (bf16[5,112,128]{2,1,0:T(8,128)(2,1)S(1)}, bf16[5,112,128]{2,1,0:T(8,128)(2,1)S(1)}, u32[]{:S(2)}, u32[]{:S(2)}) collective-permute-start(bf16[5,112,128]{2,1,0:T(8,128)(2,1)S(1)} %collective-permute-done.14.rest_2_), channel_id=1, source_target_pairs={{0,2},{2,0},{4,6},{6,4},{1,3},{3,1},{5,7},{7,5},{8,10},{10,8},{12,... | collective-permute-start | bytes 430088 | tf_op jit(solution)/shard_map/ppermute | solution.py:24
  48.0 0.0 collective-permute-done.12.rest_0_
  48.0 2.7 %collective-permute-start.13 = (bf16[5,112,128]{2,1,0:T(8,128)(2,1)S(1)}, bf16[5,112,128]{2,1,0:T(8,128)(2,1)S(1)}, u32[]{:S(2)}, u32[]{:S(2)}) collective-permute-start(bf16[5,112,128]{2,1,0:T(8,128)(2,1)S(1)} %collective-permute-done.12.rest_0_), channel_id=1, source_target_pairs={{0,2},{2,0},{4,6},{6,4},{1,3},{3,1},{5,7},{7,5},{8,10},{10,8},{12,... | collective-permute-start | bytes 430088 | tf_op jit(solution)/shard_map/ppermute | solution.py:24
  50.6 0.0 collective-permute-done.7.rest_5_
  50.6 0.0 collective-permute-start.8
  50.7 0.0 collective-permute-done.5.rest_4_
  50.7 2.0 %collective-permute-start.6 = (bf16[5,112,128]{2,1,0:T(8,128)(2,1)S(1)}, bf16[5,112,128]{2,1,0:T(8,128)(2,1)S(1)}, u32[]{:S(2)}, u32[]{:S(2)}) collective-permute-start(bf16[5,112,128]{2,1,0:T(8,128)(2,1)S(1)} %collective-permute-done.5.rest_4_), channel_id=1, source_target_pairs={{0,2},{2,0},{4,6},{6,4},{1,3},{3,1},{5,7},{7,5},{8,10},{10,8},{12,... | collective-permute-start | bytes 430088 | tf_op jit(solution)/shard_map/ppermute | solution.py:24
  52.7 0.8 %collective-permute-done.15.rest_3_ = bf16[5,112,128]{2,1,0:T(8,128)(2,1)S(1)} collective-permute-done((bf16[5,112,128]{2,1,0:T(8,128)(2,1)S(1)}, bf16[5,112,128]{2,1,0:T(8,128)(2,1)S(1)}, u32[]{:S(2)}, u32[]{:S(2)}) %collective-permute-start.15) | collective-permute-done | bytes 143392 | tf_op jit(solution)/shard_map/ppermute | solution.py:24
  53.4 3.0 %collective-permute-done.13.rest_1_ = bf16[5,112,128]{2,1,0:T(8,128)(2,1)S(1)} collective-permute-done((bf16[5,112,128]{2,1,0:T(8,128)(2,1)S(1)}, bf16[5,112,128]{2,1,0:T(8,128)(2,1)S(1)}, u32[]{:S(2)}, u32[]{:S(2)}) %collective-permute-start.13) | collective-permute-done | bytes 143392 | tf_op jit(solution)/shard_map/ppermute | solution.py:24
  56.4 3.4 %synthesise.2.rest_2_ = bf16[10,448,1024]{2,1,0:T(8,128)(2,1)} custom-call(bf16[1024,128]{1,0:T(8,128)(2,1)S(1)} %get-tuple-element.28.table_ref, bf16[5,112,128]{2,1,0:T(8,128)(2,1)S(1)} %collective-permute-done.12.rest_0_, bf16[5,112,128]{2,1,0:T(8,128)(2,1)S(1)} %collective-permute-done.13.rest_1_, ...), custom_call_target="tpu_custom_call" | custom-call | flops 880803840 | bytes 6881280 | tf_op jit(solution)/shard_map/synthesise/pallas_call | solution.py:435
  59.8 0.0 collective-permute-done.8.rest_1_
  59.8 0.0 collective-permute-done.6.rest_0_
  59.8 1.9 %synthesise.3 = bf16[10,448,1024]{2,1,0:T(8,128)(2,1)} custom-call(bf16[1024,128]{1,0:T(8,128)(2,1)S(1)} %get-tuple-element.28.table_ref, bf16[5,112,128]{2,1,0:T(8,128)(2,1)S(1)} %collective-permute-done.6.rest_0_, bf16[5,112,128]{2,1,0:T(8,128)(2,1)S(1)} %collective-permute-done.8.rest_1_, ...), custom_call_target="tpu_custom_call", output_to_operand_aliasing={{}: (3, {})} | custom-call | flops 293601280 | bytes 2293760 | tf_op jit(solution)/shard_map/synthesise/pallas_call | solution.py:435
  (1 shorter events, 0.0 us)
Async XLA Ops:
  3.7 7.6 %collective-permute-start = (bf16[5,112,128]{2,1,0:T(8,128)(2,1)S(1)}, bf16[5,112,128]{2,1,0:T(8,128)(2,1)S(1)}, u32[]{:S(2)}, u32[]{:S(2)}) collective-permute-start(bf16[5,112,128]{2,1,0:T(8,128)(2,1)S(1)} %get-tuple-element.26), channel_id=1, source_target_pairs={{0,1},{1,0},{2,3},{3,2},{4,5},{5,4},{6,7},{7,6},{8,9},{9,8},{10,11... | collective-permute-start | bytes 430088 | tf_op jit(solution)/shard_map/ppermute | solution.py:24
  6.7 7.5 %collective-permute-start.1 = (bf16[5,112,128]{2,1,0:T(8,128)(2,1)S(1)}, bf16[5,112,128]{2,1,0:T(8,128)(2,1)S(1)}, u32[]{:S(2)}, u32[]{:S(2)}) collective-permute-start(bf16[5,112,128]{2,1,0:T(8,128)(2,1)S(1)} %get-tuple-element.29), channel_id=1, source_target_pairs={{0,1},{1,0},{2,3},{3,2},{4,5},{5,4},{6,7},{7,6},{8,9},{9,8},{10,11... | collective-permute-start | bytes 430088 | tf_op jit(solution)/shard_map/ppermute | solution.py:24
  14.2 5.9 %collective-permute-start.3 = (bf16[5,112,128]{2,1,0:T(8,128)(2,1)S(1)}, bf16[5,112,128]{2,1,0:T(8,128)(2,1)S(1)}, u32[]{:S(2)}, u32[]{:S(2)}) collective-permute-start(bf16[5,112,128]{2,1,0:T(8,128)(2,1)S(1)} %fusion.21), channel_id=1, source_target_pairs={{0,2},{2,0},{4,6},{6,4},{1,3},{3,1},{5,7},{7,5},{8,10},{10,8},{12,... | collective-permute-start | bytes 430088 | tf_op jit(solution)/shard_map/ppermute | solution.py:24
  16.4 5.2 %collective-permute-start.10 = (bf16[5,112,128]{2,1,0:T(8,128)(2,1)S(1)}, bf16[5,112,128]{2,1,0:T(8,128)(2,1)S(1)}, u32[]{:S(2)}, u32[]{:S(2)}) collective-permute-start(bf16[5,112,128]{2,1,0:T(8,128)(2,1)S(1)} %fusion.1.after_ref), channel_id=1, source_target_pairs={{0,2},{2,0},{4,6},{6,4},{1,3},{3,1},{5,7},{7,5},{8,10},{10,8},{12,... | collective-permute-start | bytes 430088 | tf_op jit(solution)/shard_map/ppermute | solution.py:24
  21.9 7.6 %collective-permute-start.2 = (bf16[5,112,128]{2,1,0:T(8,128)(2,1)S(1)}, bf16[5,112,128]{2,1,0:T(8,128)(2,1)S(1)}, u32[]{:S(2)}, u32[]{:S(2)}) collective-permute-start(bf16[5,112,128]{2,1,0:T(8,128)(2,1)S(1)} %get-tuple-element.39), channel_id=1, source_target_pairs={{0,2},{2,0},{4,6},{6,4},{1,3},{3,1},{5,7},{7,5},{8,10},{10,8},{12,... | collective-permute-start | bytes 430088 | tf_op jit(solution)/shard_map/ppermute | solution.py:24
  23.6 11.2 %collective-permute-start.4 = (bf16[5,112,128]{2,1,0:T(8,128)(2,1)S(1)}, bf16[5,112,128]{2,1,0:T(8,128)(2,1)S(1)}, u32[]{:S(2)}, u32[]{:S(2)}) collective-permute-start(bf16[5,112,128]{2,1,0:T(8,128)(2,1)S(1)} %get-tuple-element.40), channel_id=1, source_target_pairs={{0,4},{2,6},{4,0},{6,2},{1,5},{3,7},{5,1},{7,3},{8,12},{10,14},{12... | collective-permute-start | bytes 430088 | tf_op jit(solution)/shard_map/ppermute | solution.py:24
  26.2 10.2 %collective-permute-start.11 = (bf16[5,112,128]{2,1,0:T(8,128)(2,1)S(1)}, bf16[5,112,128]{2,1,0:T(8,128)(2,1)S(1)}, u32[]{:S(2)}, u32[]{:S(2)}) collective-permute-start(bf16[5,112,128]{2,1,0:T(8,128)(2,1)S(1)} %get-tuple-element.45), channel_id=1, source_target_pairs={{0,4},{2,6},{4,0},{6,2},{1,5},{3,7},{5,1},{7,3},{8,12},{10,14},{12... | collective-permute-start | bytes 430088 | tf_op jit(solution)/shard_map/ppermute | solution.py:24
  26.5 9.8 %collective-permute-start.9 = (bf16[5,112,128]{2,1,0:T(8,128)(2,1)S(1)}, bf16[5,112,128]{2,1,0:T(8,128)(2,1)S(1)}, u32[]{:S(2)}, u32[]{:S(2)}) collective-permute-start(bf16[5,112,128]{2,1,0:T(8,128)(2,1)S(1)} %get-tuple-element.46), channel_id=1, source_target_pairs={{0,2},{2,0},{4,6},{6,4},{1,3},{3,1},{5,7},{7,5},{8,10},{10,8},{12,... | collective-permute-start | bytes 430088 | tf_op jit(solution)/shard_map/ppermute | solution.py:24
  36.6 10.2 %collective-permute-start.14 = (bf16[5,112,128]{2,1,0:T(8,128)(2,1)S(1)}, bf16[5,112,128]{2,1,0:T(8,128)(2,1)S(1)}, u32[]{:S(2)}, u32[]{:S(2)}) collective-permute-start(bf16[5,112,128]{2,1,0:T(8,128)(2,1)S(1)} %get-tuple-element.47), channel_id=1, source_target_pairs={{0,20},{2,22},{4,16},{6,18},{8,28},{10,30},{12,24},{14,26},{16,4},... | collective-permute-start | bytes 430088 | tf_op jit(solution)/shard_map/ppermute | solution.py:541
  38.1 9.9 %collective-permute-start.12 = (bf16[5,112,128]{2,1,0:T(8,128)(2,1)S(1)}, bf16[5,112,128]{2,1,0:T(8,128)(2,1)S(1)}, u32[]{:S(2)}, u32[]{:S(2)}) collective-permute-start(bf16[5,112,128]{2,1,0:T(8,128)(2,1)S(1)} %get-tuple-element.47), channel_id=1, source_target_pairs={{0,16},{2,18},{4,20},{6,22},{8,24},{10,26},{12,28},{14,30},{16,0},... | collective-permute-start | bytes 430088 | tf_op jit(solution)/shard_map/ppermute | solution.py:541
  38.6 12.1 %collective-permute-start.7 = (bf16[5,112,128]{2,1,0:T(8,128)(2,1)S(1)}, bf16[5,112,128]{2,1,0:T(8,128)(2,1)S(1)}, u32[]{:S(2)}, u32[]{:S(2)}) collective-permute-start(bf16[5,112,128]{2,1,0:T(8,128)(2,1)S(1)} %get-tuple-element.48), channel_id=1, source_target_pairs={{0,20},{2,22},{4,16},{6,18},{8,28},{10,30},{12,24},{14,26},{16,4},... | collective-permute-start | bytes 430088 | tf_op jit(solution)/shard_map/ppermute | solution.py:541
  42.0 8.7 %collective-permute-start.5 = (bf16[5,112,128]{2,1,0:T(8,128)(2,1)S(1)}, bf16[5,112,128]{2,1,0:T(8,128)(2,1)S(1)}, u32[]{:S(2)}, u32[]{:S(2)}) collective-permute-start(bf16[5,112,128]{2,1,0:T(8,128)(2,1)S(1)} %get-tuple-element.48), channel_id=1, source_target_pairs={{0,16},{2,18},{4,20},{6,22},{8,24},{10,26},{12,28},{14,30},{16,0},... | collective-permute-start | bytes 430088 | tf_op jit(solution)/shard_map/ppermute | solution.py:541
  46.7 6.7 %collective-permute-start.15 = (bf16[5,112,128]{2,1,0:T(8,128)(2,1)S(1)}, bf16[5,112,128]{2,1,0:T(8,128)(2,1)S(1)}, u32[]{:S(2)}, u32[]{:S(2)}) collective-permute-start(bf16[5,112,128]{2,1,0:T(8,128)(2,1)S(1)} %collective-permute-done.14.rest_2_), channel_id=1, source_target_pairs={{0,2},{2,0},{4,6},{6,4},{1,3},{3,1},{5,7},{7,5},{8,10},{10,8},{12,... | collective-permute-start | bytes 430088 | tf_op jit(solution)/shard_map/ppermute | solution.py:24
  48.0 8.5 %collective-permute-start.13 = (bf16[5,112,128]{2,1,0:T(8,128)(2,1)S(1)}, bf16[5,112,128]{2,1,0:T(8,128)(2,1)S(1)}, u32[]{:S(2)}, u32[]{:S(2)}) collective-permute-start(bf16[5,112,128]{2,1,0:T(8,128)(2,1)S(1)} %collective-permute-done.12.rest_0_), channel_id=1, source_target_pairs={{0,2},{2,0},{4,6},{6,4},{1,3},{3,1},{5,7},{7,5},{8,10},{10,8},{12,... | collective-permute-start | bytes 430088 | tf_op jit(solution)/shard_map/ppermute | solution.py:24
  50.6 9.2 %collective-permute-start.8 = (bf16[5,112,128]{2,1,0:T(8,128)(2,1)S(1)}, bf16[5,112,128]{2,1,0:T(8,128)(2,1)S(1)}, u32[]{:S(2)}, u32[]{:S(2)}) collective-permute-start(bf16[5,112,128]{2,1,0:T(8,128)(2,1)S(1)} %collective-permute-done.7.rest_5_), channel_id=1, source_target_pairs={{0,2},{2,0},{4,6},{6,4},{1,3},{3,1},{5,7},{7,5},{8,10},{10,8},{12,... | collective-permute-start | bytes 430088 | tf_op jit(solution)/shard_map/ppermute | solution.py:24
  50.7 9.1 %collective-permute-start.6 = (bf16[5,112,128]{2,1,0:T(8,128)(2,1)S(1)}, bf16[5,112,128]{2,1,0:T(8,128)(2,1)S(1)}, u32[]{:S(2)}, u32[]{:S(2)}) collective-permute-start(bf16[5,112,128]{2,1,0:T(8,128)(2,1)S(1)} %collective-permute-done.5.rest_4_), channel_id=1, source_target_pairs={{0,2},{2,0},{4,6},{6,4},{1,3},{3,1},{5,7},{7,5},{8,10},{10,8},{12,... | collective-permute-start | bytes 430088 | tf_op jit(solution)/shard_map/ppermute | solution.py:24

commit v3 on v2

--- a/solution.py
+++ b/solution.py
@@ -12,10 +12,9 @@
 JITTER = 6
 LANES = 128
 ORDER = {}
-GROUPS = (
-    ((0, 0), (0, 1), (0, 2), (0, 3), (1, 0), (1, 2)),
-    ((1, 1), (1, 3)),
-)
+JOIN = True
+DIRECT = True
+GROUPS = (((0, 0), (0, 1), (0, 2), (0, 3), (1, 0), (1, 2)), ((1, 1), (1, 3)))
 VMEM_BYTES = 32 * 1024 * 1024
 
 
@@ -130,9 +129,9 @@
     sizes, counts_hbm, orders_hbm, starts_hbm, weight_hbm, planes_hbm, *rest,
 ):
     instances, fields, rs_loc, halo, edge, total_pitch = sizes
-    halo_refs, (table_ref, planes_ref, mask_ref) = rest[:instances], rest[instances : instances + 3]
+    halo_refs, (table_ref, planes_ref) = rest[:instances], rest[instances : instances + 2]
     counts, orders, starts, weight, edges, flipped, spectra, sems, plane_sems = rest[
-        instances + 3 :
+        instances + 2 :
     ]
     rows, pitch = planes_hbm.shape[1:]
     others = rows - edge
@@ -173,11 +172,6 @@
             plane_sems.at[instances],
         )
     )
-    pitch_at = lax.axis_index("pitch")
-    for k in range(mask_ref.shape[0]):
-        halo_at = jnp.where(span_at == 0, mask_ref.shape[0] - 1, 0)
-        at_halo = jnp.bitwise_xor(pitch_at, k) == halo_at
-        mask_ref[k] = jnp.full(mask_ref.shape[1:], at_halo.astype(jnp.float32))
     for copy in small[:2]:
         copy.wait()
     wave = column_wavenumbers(counts, orders)
@@ -208,7 +202,7 @@
     rest_fetched.wait()
 
 
-def edge_call(sizes, shards, counts, orders, starts, weight, planes):
+def edge_call(sizes, counts, orders, starts, weight, planes):
     instances, fields, rs_loc, halo, edge, total_pitch = sizes
     pitch = planes.shape[2]
     columns = 2 * orders.shape[1]
@@ -222,10 +216,9 @@
         + [
             jax.ShapeDtypeStruct((instances, pitch, columns), jnp.bfloat16),
             pltpu.VMEM((fields, *planes.shape[1:]), jnp.bfloat16),
-            jax.ShapeDtypeStruct((shards, 8, columns), jnp.float32),
         ],
         in_specs=[hbm] * 5,
-        out_specs=[vmem] * (instances + 3),
+        out_specs=[vmem] * (instances + 2),
         scratch_shapes=[
             pltpu.SMEM(counts.shape, jnp.int32),
             pltpu.VMEM(orders.shape, jnp.int32),
@@ -477,8 +470,10 @@
     blade_counts = stay(blade_counts)
     remap_weight = stay(remap_weight)
     sizes = (instances, fields, rs_loc, halo_rows, edge, total_pitch)
-    *halos, table, held, masks = edge_call(
-        sizes, shards, blade_counts, orders, starts, remap_weight, planes
+    halo_at = jnp.where(lax.axis_index("span") == 0, shards - 1, 0)
+    holds = [jnp.bitwise_xor(lax.axis_index("pitch"), k) == halo_at for k in range(shards)]
+    *halos, table, held = edge_call(
+        sizes, after(blade_counts, *holds), orders, starts, remap_weight, planes
     )
     made = first_call(sizes, shards, starts, remap_weight, planes, held, table)
     owns, band, held = [made[:shards]], made[shards], made[-1]
@@ -510,7 +505,7 @@
 
     def with_halo(part, k, *terms):
         get("later", part)
-        total = jnp.where(masks[k, :1] > 0.0, get("halo", part).astype(jnp.float32), 0.0)
+        total = jnp.where(holds[k], get("halo", part).astype(jnp.float32), 0.0)
         for term in (owns[part][k], *terms):
             total = total + term.astype(jnp.float32)
         return total.astype(jnp.bfloat16)
@@ -518,10 +513,18 @@
     def meet(part):
         return None, with_halo(part, 3)
 
+    def pair_sent(part):
+        sent = [get("meet", part)[1]]
+        if part > 0 and JOIN:
+            sent.append(with_halo(part - 1, 1))
+        return exchange(ready("pair", part, jnp.stack(sent)), "pitch", 1)
+
     def pair(part):
-        return exchange(ready("pair", part, get("meet", part)[1]), "pitch", 1)
+        return get("pair_sent", part)[0]
 
     def beside(part):
+        if part + 1 < instances and JOIN:
+            return get("pair_sent", part + 1)[1]
         return exchange(ready("beside", part, with_halo(part, 1)), "pitch", 1)
 
     def across(part):
@@ -546,17 +549,25 @@
     def swap_across(part):
         return spread(ready("swap_across", part, get("total", part)), 2)
 
-    def swap_on(part):
-        return exchange(ready("swap_on", part, get("swap", part)), "pitch", 1)
+    def swap_beside(part):
+        if DIRECT:
+            return spread(ready("swap_beside", part, get("total", part)), 1)
+        return exchange(ready("swap_beside", part, get("swap", part)), "pitch", 1)
 
     def across_on(part):
         return exchange(ready("across_on", part, get("swap_across", part)), "pitch", 1)
 
+    def synth(at):
+        base = get("synth", at - 1) if at else None
+        group = {(part, k): get(names[k], part) for part, k in GROUPS[at]}
+        return synthesise_call(count, shards, known["synthesis", 0], group, base)
+
     steps = dict(
-        later=later, halo=halo, meet=meet, pair=pair, beside=beside, across=across, total=total,
-        swap=swap, swap_across=swap_across, swap_on=swap_on, across_on=across_on,
-    )
-    names = ("swap", "swap_on", "swap_across", "across_on")
+        synth=synth,
+        later=later, halo=halo, meet=meet, pair_sent=pair_sent, pair=pair, beside=beside, across=across, total=total,
+        swap=swap, swap_across=swap_across, swap_beside=swap_beside, across_on=across_on,
+    )
+    names = ("swap", "swap_beside", "swap_across", "across_on")
 
     def whole_sum(part):
         get("later", part)
@@ -567,10 +578,9 @@
         return lax.psum(mine, "pitch").astype(jnp.bfloat16)
 
     joined = None
+    get("later", instances - 1)
     if by_shards:
-        for group in GROUPS:
-            group = {(part, k): get(names[k], part) for part, k in group}
-            joined = synthesise_call(count, shards, known["synthesis", 0], group, joined)
+        joined = get("synth", len(GROUPS) - 1)
     else:
         pairs = [(g, (g + shift) % row_count) for g in range(row_count)]
         pieces = {

time: 61.9 us -> 57.2 us (0.924)
  waiting for transfers between devices: 23.7 us -> 13 us
  starting transfers between devices: 22.2 us -> 28.2 us
    ppermute x12 -> x9, waiting for transfers between devices: 19.4 us -> 10.3 us  [exchange(): return lax.ppermute(value, axis, [(i, i ^ distance) for i in range(count)])]
    ppermute x12 -> x9, starting transfers between devices: 16.3 us -> 19.5 us  [exchange(): return lax.ppermute(value, axis, [(i, i ^ distance) for i in range(count)])]
    ppermute x4 -> x6, starting transfers between devices: 5.92 us -> 8.68 us  [spread(): return lax.ppermute(value, ('row', 'pitch'), pairs)]
    ppermute x4 -> x6, waiting for transfers between devices: 4.28 us -> 2.75 us  [spread(): return lax.ppermute(value, ('row', 'pitch'), pairs)]
  transfers between devices with their start and end apart: 16 -> 15, of which waited for: 9 -> 9; matrix products, arithmetic and copies ran while one was open for 0% -> 0% of each run, Pallas kernels for 16% -> 17%
where the time goes in v3:
time: 57.2 us; the launch traced here: 57 us
  starting transfers between devices  28.2 us (49%)
  Pallas kernels  15.2 us (27%)
  waiting for transfers between devices  13 us (23%)
    ppermute x9, starting transfers between devices, exchange(): return lax.ppermute(value, axis, [(i, i ^ distance) for i in range(count)])  19.5 us
    ppermute x9, waiting for transfers between devices, exchange(): return lax.ppermute(value, axis, [(i, i ^ distance) for i in range(count)])  10.3 us
    ppermute x6, starting transfers between devices, spread(): return lax.ppermute(value, ('row', 'pitch'), pairs)  8.68 us
    pallas_call x2, Pallas kernels, synthesise_call(): pl.pallas_call(functools.partial(synthesise_kernel, fields, ranks, shards...  5.24 us
    pallas_call x1, Pallas kernels, edge_call(): pl.pallas_call(functools.partial(edge_kernel, sizes), out_shape=[jax.Shap...  3.68 us
    pallas_call x1, Pallas kernels, first_call(): pl.pallas_call(functools.partial(first_kernel, sizes, shards), out_shape=...  3.5 us
    pallas_call x1, Pallas kernels, later_call(): pl.pallas_call(functools.partial(later_kernel, sizes, shards, part), out_...  2.8 us
    ppermute x6, waiting for transfers between devices, spread(): return lax.ppermute(value, ('row', 'pitch'), pairs)  2.75 us
  transfers between devices with their start and end apart: 15, of which 9 were waited for; matrix products, arithmetic and copies ran while one was open for 0% of the time, Pallas kernels for 17%

profile of v3, /device:TPU:0, one launch (start us, length us, event | category | flops | bytes accessed | tf_op | source)
XLA Modules:
  0.0 57.0 jit_solution(3086897456621450871)
XLA Ops:
  0.0 3.7 %edge.1 = (bf16[5,112,128]{2,1,0:T(8,128)(2,1)S(1)}, bf16[5,112,128]{2,1,0:T(8,128)(2,1)S(1)}, bf16[2,1024,128]{2,1,0:T(8,128)(2,1)S(1)}, bf16[5,512,1024]{2,1,0:T(8,128)(2,1)S(1)}) custom-call(s32[2]{0:T(128)} %counts_hbm.2, s32[2,64]{1,0:T(2,128)} %bitcast.28, s32[7,128]{1,0:T(8,128)} %bitcast.26, bf16[512,896]{1,0:T(8,128)(2,1)} %weight_hbm.3, ...), custom_call_target="tpu_custom_call" | custom-call | flops 372244480 | bytes 2621440 | tf_op jit(solution)/shard_map/edge/pallas_call | solution.py:213
  3.7 3.0 %collective-permute-start = (bf16[5,112,128]{2,1,0:T(8,128)(2,1)S(1)}, bf16[5,112,128]{2,1,0:T(8,128)(2,1)S(1)}, u32[]{:S(2)}, u32[]{:S(2)}) collective-permute-start(bf16[5,112,128]{2,1,0:T(8,128)(2,1)S(1)} %get-tuple-element.26), channel_id=1, source_target_pairs={{0,1},{1,0},{2,3},{3,2},{4,5},{5,4},{6,7},{7,6},{8,9},{9,8},{10,11... | collective-permute-start | bytes 430088 | tf_op jit(solution)/shard_map/ppermute | solution.py:23
  6.7 0.1 collective-permute-start.1
  6.8 3.5 %first_part.1 = (f32[5,112,128]{2,1,0:T(8,128)S(1)}, bf16[5,112,128]{2,1,0:T(8,128)(2,1)S(1)}, f32[5,112,128]{2,1,0:T(8,128)S(1)}, bf16[5,112,128]{2,1,0:T(8,128...) custom-call(s32[7,128]{1,0:T(8,128)} %bitcast.27, bf16[512,896]{1,0:T(8,128)(2,1)} %weight_hbm.3, ...), custom_call_target="tpu_custom_call" | custom-call | flops 964689920 | bytes 5242880 | tf_op jit(solution)/shard_map/first_part/pallas_call | solution.py:311
  10.3 1.0 %collective-permute-done = bf16[5,112,128]{2,1,0:T(8,128)(2,1)S(1)} collective-permute-done((bf16[5,112,128]{2,1,0:T(8,128)(2,1)S(1)}, bf16[5,112,128]{2,1,0:T(8,128)(2,1)S(1)}, u32[]{:S(2)}, u32[]{:S(2)}) %collective-permute-start) | collective-permute-done | bytes 143392 | tf_op jit(solution)/shard_map/ppermute | solution.py:23
  11.3 0.1 fusion.1.after_ref
  11.3 2.2 %collective-permute-start.8 = (bf16[1,5,112,128]{3,2,1,0:T(8,128)(2,1)S(1)}, bf16[1,5,112,128]{3,2,1,0:T(8,128)(2,1)S(1)}, u32[]{:S(2)}, u32[]{:S(2)}) collective-permute-start(bf16[1,5,112,128]{3,2,1,0:T(8,128)(2,1)S(1)} %bitcast.22), channel_id=1, source_target_pairs={{0,2},{2,0},{4,6},{6,4},{1,3},{3,1},{5,7},{7,5},{8,10},{10,8},{12,... | collective-permute-start | bytes 430088 | tf_op jit(solution)/shard_map/ppermute | solution.py:23
  13.5 2.8 %later_part.1 = (f32[5,112,128]{2,1,0:T(8,128)S(1)}, bf16[5,112,128]{2,1,0:T(8,128)(2,1)S(1)}, f32[5,112,128]{2,1,0:T(8,128)S(1)}, bf16[5,112,128]{2,1,0:T(8,128)(2,1)S(1)}, bf16[1024,128]{1,0:T(8,128)(2,1)S(1)}) custom-call(s32[2]{0:T(128)} %counts_hbm.2, s32[2,64]{1,0:T(2,128)} %bitcast.29, bf16[10,512,1024]{2,1,0:T(8,128)(2,1)} %bitcast.25, ...), custom_call_target="tpu_custom_call" | custom-call | flops 964689920 | bytes 5242880 | tf_op jit(solution)/shard_map/later_part/pallas_call | solution.py:364
  16.4 0.0 collective-permute-done.1
  16.4 0.1 fusion.22
  16.4 0.2 collective-permute-done.8
  16.6 0.1 fusion.10
  16.8 2.2 %collective-permute-start.3 = (bf16[2,5,112,128]{3,2,1,0:T(8,128)(2,1)S(1)}, bf16[2,5,112,128]{3,2,1,0:T(8,128)(2,1)S(1)}, u32[]{:S(2)}, u32[]{:S(2)}) collective-permute-start(bf16[2,5,112,128]{3,2,1,0:T(8,128)(2,1)S(1)} %pad_maximum_fusion), channel_id=1, source_target_pairs={{0,2},{2,0},{4,6},{6,4},{1,3},{3,1},{5,7},{7,5},{8,10},{10,8},{12,... | collective-permute-start | bytes 860168 | tf_op jit(solution)/shard_map/ppermute | solution.py:23
  19.0 2.6 %collective-permute-start.9 = (bf16[5,112,128]{2,1,0:T(8,128)(2,1)S(1)}, bf16[5,112,128]{2,1,0:T(8,128)(2,1)S(1)}, u32[]{:S(2)}, u32[]{:S(2)}) collective-permute-start(bf16[5,112,128]{2,1,0:T(8,128)(2,1)S(1)} %get-tuple-element.40), channel_id=1, source_target_pairs={{0,4},{2,6},{4,0},{6,2},{1,5},{3,7},{5,1},{7,3},{8,12},{10,14},{12... | collective-permute-start | bytes 430088 | tf_op jit(solution)/shard_map/ppermute | solution.py:23
  21.6 4.1 %collective-permute-done.9 = bf16[5,112,128]{2,1,0:T(8,128)(2,1)S(1)} collective-permute-done((bf16[5,112,128]{2,1,0:T(8,128)(2,1)S(1)}, bf16[5,112,128]{2,1,0:T(8,128)(2,1)S(1)}, u32[]{:S(2)}, u32[]{:S(2)}) %collective-permute-start.9) | collective-permute-done | bytes 143392 | tf_op jit(solution)/shard_map/ppermute | solution.py:23
  25.7 0.7 %collective-permute-done.3 = bf16[2,5,112,128]{3,2,1,0:T(8,128)(2,1)S(1)} collective-permute-done((bf16[2,5,112,128]{3,2,1,0:T(8,128)(2,1)S(1)}, bf16[2,5,112,128]{3,2,1,0:T(8,128)(2,1)S(1)}, u32[]{:S(2)}, u32[]{:S(2)}) %collective-permute-start.3) | collective-permute-done | bytes 286752 | tf_op jit(solution)/shard_map/ppermute | solution.py:23
  26.4 0.2 fusion.7
  26.5 2.8 %collective-permute-start.4 = (bf16[5,112,128]{2,1,0:T(8,128)(2,1)S(1)}, bf16[5,112,128]{2,1,0:T(8,128)(2,1)S(1)}, u32[]{:S(2)}, u32[]{:S(2)}) collective-permute-start(bf16[5,112,128]{2,1,0:T(8,128)(2,1)S(1)} %get-tuple-element.38), channel_id=1, source_target_pairs={{0,4},{2,6},{4,0},{6,2},{1,5},{3,7},{5,1},{7,3},{8,12},{10,14},{12... | collective-permute-start | bytes 430088 | tf_op jit(solution)/shard_map/ppermute | solution.py:23
  29.3 1.4 %collective-permute-start.2 = (bf16[5,112,128]{2,1,0:T(8,128)(2,1)S(1)}, bf16[5,112,128]{2,1,0:T(8,128)(2,1)S(1)}, u32[]{:S(2)}, u32[]{:S(2)}) collective-permute-start(bf16[5,112,128]{2,1,0:T(8,128)(2,1)S(1)} %get-tuple-element.39), channel_id=1, source_target_pairs={{0,2},{2,0},{4,6},{6,4},{1,3},{3,1},{5,7},{7,5},{8,10},{10,8},{12,... | collective-permute-start | bytes 430088 | tf_op jit(solution)/shard_map/ppermute | solution.py:23
  30.7 2.5 %collective-permute-start.12 = (bf16[5,112,128]{2,1,0:T(8,128)(2,1)S(1)}, bf16[5,112,128]{2,1,0:T(8,128)(2,1)S(1)}, u32[]{:S(2)}, u32[]{:S(2)}) collective-permute-start(bf16[5,112,128]{2,1,0:T(8,128)(2,1)S(1)} %get-tuple-element.37), channel_id=1, source_target_pairs={{0,20},{2,22},{4,16},{6,18},{8,28},{10,30},{12,24},{14,26},{16,4},... | collective-permute-start | bytes 430088 | tf_op jit(solution)/shard_map/ppermute | solution.py:544
  33.2 0.0 collective-permute-start.11
  33.2 3.3 %collective-permute-done.4 = bf16[5,112,128]{2,1,0:T(8,128)(2,1)S(1)} collective-permute-done((bf16[5,112,128]{2,1,0:T(8,128)(2,1)S(1)}, bf16[5,112,128]{2,1,0:T(8,128)(2,1)S(1)}, u32[]{:S(2)}, u32[]{:S(2)}) %collective-permute-start.4) | collective-permute-done | bytes 143392 | tf_op jit(solution)/shard_map/ppermute | solution.py:23
  36.5 0.9 %collective-permute-done.2 = bf16[5,112,128]{2,1,0:T(8,128)(2,1)S(1)} collective-permute-done((bf16[5,112,128]{2,1,0:T(8,128)(2,1)S(1)}, bf16[5,112,128]{2,1,0:T(8,128)(2,1)S(1)}, u32[]{:S(2)}, u32[]{:S(2)}) %collective-permute-start.2) | collective-permute-done | bytes 143392 | tf_op jit(solution)/shard_map/ppermute | solution.py:23
  37.5 0.1 fusion.14
  37.5 3.5 %collective-permute-start.6 = (bf16[5,112,128]{2,1,0:T(8,128)(2,1)S(1)}, bf16[5,112,128]{2,1,0:T(8,128)(2,1)S(1)}, u32[]{:S(2)}, u32[]{:S(2)}) collective-permute-start(bf16[5,112,128]{2,1,0:T(8,128)(2,1)S(1)} %fusion.14), channel_id=1, source_target_pairs={{0,20},{2,22},{4,16},{6,18},{8,28},{10,30},{12,24},{14,26},{16,4},... | collective-permute-start | bytes 430088 | tf_op jit(solution)/shard_map/ppermute | solution.py:544
  41.1 0.5 collective-permute-start.10
  41.6 1.5 %collective-permute-start.14 = (bf16[5,112,128]{2,1,0:T(8,128)(2,1)S(1)}, bf16[5,112,128]{2,1,0:T(8,128)(2,1)S(1)}, u32[]{:S(2)}, u32[]{:S(2)}) collective-permute-start(bf16[5,112,128]{2,1,0:T(8,128)(2,1)S(1)} %fusion.14), channel_id=1, source_target_pairs={{0,16},{2,18},{4,20},{6,22},{8,24},{10,26},{12,28},{14,30},{16,0},... | collective-permute-start | bytes 430088 | tf_op jit(solution)/shard_map/ppermute | solution.py:544
  43.1 1.1 %collective-permute-done.12.rest_2_ = bf16[5,112,128]{2,1,0:T(8,128)(2,1)S(1)} collective-permute-done((bf16[5,112,128]{2,1,0:T(8,128)(2,1)S(1)}, bf16[5,112,128]{2,1,0:T(8,128)(2,1)S(1)}, u32[]{:S(2)}, u32[]{:S(2)}) %collective-permute-start.12) | collective-permute-done | bytes 143392 | tf_op jit(solution)/shard_map/ppermute | solution.py:544
  44.2 0.7 %collective-permute-start.13 = (bf16[5,112,128]{2,1,0:T(8,128)(2,1)S(1)}, bf16[5,112,128]{2,1,0:T(8,128)(2,1)S(1)}, u32[]{:S(2)}, u32[]{:S(2)}) collective-permute-start(bf16[5,112,128]{2,1,0:T(8,128)(2,1)S(1)} %collective-permute-done.12.rest_2_), channel_id=1, source_target_pairs={{0,2},{2,0},{4,6},{6,4},{1,3},{3,1},{5,7},{7,5},{8,10},{10,8},{12,... | collective-permute-start | bytes 430088 | tf_op jit(solution)/shard_map/ppermute | solution.py:23
  45.0 0.0 collective-permute-done.11.rest_1_
  45.0 0.7 %collective-permute-start.5 = (bf16[5,112,128]{2,1,0:T(8,128)(2,1)S(1)}, bf16[5,112,128]{2,1,0:T(8,128)(2,1)S(1)}, u32[]{:S(2)}, u32[]{:S(2)}) collective-permute-start(bf16[5,112,128]{2,1,0:T(8,128)(2,1)S(1)} %fusion.14), channel_id=1, source_target_pairs={{0,18},{2,16},{4,22},{6,20},{8,26},{10,24},{12,30},{14,28},{16,2},... | collective-permute-start | bytes 430088 | tf_op jit(solution)/shard_map/ppermute | solution.py:544
  45.6 0.4 collective-permute-done.6.rest_5_
  46.0 4.5 %collective-permute-start.7 = (bf16[5,112,128]{2,1,0:T(8,128)(2,1)S(1)}, bf16[5,112,128]{2,1,0:T(8,128)(2,1)S(1)}, u32[]{:S(2)}, u32[]{:S(2)}) collective-permute-start(bf16[5,112,128]{2,1,0:T(8,128)(2,1)S(1)} %collective-permute-done.6.rest_5_), channel_id=1, source_target_pairs={{0,2},{2,0},{4,6},{6,4},{1,3},{3,1},{5,7},{7,5},{8,10},{10,8},{12,... | collective-permute-start | bytes 430088 | tf_op jit(solution)/shard_map/ppermute | solution.py:23
  50.5 0.0 collective-permute-done.10.rest_0_
  50.5 1.2 %collective-permute-done.14.rest_4_ = bf16[5,112,128]{2,1,0:T(8,128)(2,1)S(1)} collective-permute-done((bf16[5,112,128]{2,1,0:T(8,128)(2,1)S(1)}, bf16[5,112,128]{2,1,0:T(8,128)(2,1)S(1)}, u32[]{:S(2)}, u32[]{:S(2)}) %collective-permute-start.14) | collective-permute-done | bytes 143392 | tf_op jit(solution)/shard_map/ppermute | solution.py:544
  51.7 0.0 collective-permute-done.13.rest_3_
  51.7 3.4 %synthesise.2.rest_2_ = bf16[10,448,1024]{2,1,0:T(8,128)(2,1)} custom-call(bf16[1024,128]{1,0:T(8,128)(2,1)S(1)} %get-tuple-element.28.table_ref, bf16[5,112,128]{2,1,0:T(8,128)(2,1)S(1)} %collective-permute-done.10.rest_0_, bf16[5,112,128]{2,1,0:T(8,128)(2,1)S(1)} %collective-permute-done.11.rest_1_, ...), custom_call_target="tpu_custom_call" | custom-call | flops 880803840 | bytes 6881280 | tf_op jit(solution)/shard_map/synthesise/pallas_call | solution.py:428
  55.1 0.0 collective-permute-done.5.rest_0_
  55.1 0.0 collective-permute-done.7.rest_1_
  55.1 1.9 %synthesise.3 = bf16[10,448,1024]{2,1,0:T(8,128)(2,1)} custom-call(bf16[1024,128]{1,0:T(8,128)(2,1)S(1)} %get-tuple-element.28.table_ref, bf16[5,112,128]{2,1,0:T(8,128)(2,1)S(1)} %collective-permute-done.5.rest_0_, bf16[5,112,128]{2,1,0:T(8,128)(2,1)S(1)} %collective-permute-done.7.rest_1_, ...), custom_call_target="tpu_custom_call", output_to_operand_aliasing={{}: (3, {})} | custom-call | flops 293601280 | bytes 2293760 | tf_op jit(solution)/shard_map/synthesise/pallas_call | solution.py:428
  (1 shorter events, 0.0 us)
Async XLA Ops:
  3.7 7.6 %collective-permute-start = (bf16[5,112,128]{2,1,0:T(8,128)(2,1)S(1)}, bf16[5,112,128]{2,1,0:T(8,128)(2,1)S(1)}, u32[]{:S(2)}, u32[]{:S(2)}) collective-permute-start(bf16[5,112,128]{2,1,0:T(8,128)(2,1)S(1)} %get-tuple-element.26), channel_id=1, source_target_pairs={{0,1},{1,0},{2,3},{3,2},{4,5},{5,4},{6,7},{7,6},{8,9},{9,8},{10,11... | collective-permute-start | bytes 430088 | tf_op jit(solution)/shard_map/ppermute | solution.py:23
  6.7 9.7 %collective-permute-start.1 = (bf16[5,112,128]{2,1,0:T(8,128)(2,1)S(1)}, bf16[5,112,128]{2,1,0:T(8,128)(2,1)S(1)}, u32[]{:S(2)}, u32[]{:S(2)}) collective-permute-start(bf16[5,112,128]{2,1,0:T(8,128)(2,1)S(1)} %get-tuple-element.29), channel_id=1, source_target_pairs={{0,1},{1,0},{2,3},{3,2},{4,5},{5,4},{6,7},{7,6},{8,9},{9,8},{10,11... | collective-permute-start | bytes 430088 | tf_op jit(solution)/shard_map/ppermute | solution.py:23
  11.3 5.3 %collective-permute-start.8 = (bf16[1,5,112,128]{3,2,1,0:T(8,128)(2,1)S(1)}, bf16[1,5,112,128]{3,2,1,0:T(8,128)(2,1)S(1)}, u32[]{:S(2)}, u32[]{:S(2)}) collective-permute-start(bf16[1,5,112,128]{3,2,1,0:T(8,128)(2,1)S(1)} %bitcast.22), channel_id=1, source_target_pairs={{0,2},{2,0},{4,6},{6,4},{1,3},{3,1},{5,7},{7,5},{8,10},{10,8},{12,... | collective-permute-start | bytes 430088 | tf_op jit(solution)/shard_map/ppermute | solution.py:23
  16.8 9.6 %collective-permute-start.3 = (bf16[2,5,112,128]{3,2,1,0:T(8,128)(2,1)S(1)}, bf16[2,5,112,128]{3,2,1,0:T(8,128)(2,1)S(1)}, u32[]{:S(2)}, u32[]{:S(2)}) collective-permute-start(bf16[2,5,112,128]{3,2,1,0:T(8,128)(2,1)S(1)} %pad_maximum_fusion), channel_id=1, source_target_pairs={{0,2},{2,0},{4,6},{6,4},{1,3},{3,1},{5,7},{7,5},{8,10},{10,8},{12,... | collective-permute-start | bytes 860168 | tf_op jit(solution)/shard_map/ppermute | solution.py:23
  19.0 6.7 %collective-permute-start.9 = (bf16[5,112,128]{2,1,0:T(8,128)(2,1)S(1)}, bf16[5,112,128]{2,1,0:T(8,128)(2,1)S(1)}, u32[]{:S(2)}, u32[]{:S(2)}) collective-permute-start(bf16[5,112,128]{2,1,0:T(8,128)(2,1)S(1)} %get-tuple-element.40), channel_id=1, source_target_pairs={{0,4},{2,6},{4,0},{6,2},{1,5},{3,7},{5,1},{7,3},{8,12},{10,14},{12... | collective-permute-start | bytes 430088 | tf_op jit(solution)/shard_map/ppermute | solution.py:23
  26.5 10.0 %collective-permute-start.4 = (bf16[5,112,128]{2,1,0:T(8,128)(2,1)S(1)}, bf16[5,112,128]{2,1,0:T(8,128)(2,1)S(1)}, u32[]{:S(2)}, u32[]{:S(2)}) collective-permute-start(bf16[5,112,128]{2,1,0:T(8,128)(2,1)S(1)} %get-tuple-element.38), channel_id=1, source_target_pairs={{0,4},{2,6},{4,0},{6,2},{1,5},{3,7},{5,1},{7,3},{8,12},{10,14},{12... | collective-permute-start | bytes 430088 | tf_op jit(solution)/shard_map/ppermute | solution.py:23
  29.3 8.1 %collective-permute-start.2 = (bf16[5,112,128]{2,1,0:T(8,128)(2,1)S(1)}, bf16[5,112,128]{2,1,0:T(8,128)(2,1)S(1)}, u32[]{:S(2)}, u32[]{:S(2)}) collective-permute-start(bf16[5,112,128]{2,1,0:T(8,128)(2,1)S(1)} %get-tuple-element.39), channel_id=1, source_target_pairs={{0,2},{2,0},{4,6},{6,4},{1,3},{3,1},{5,7},{7,5},{8,10},{10,8},{12,... | collective-permute-start | bytes 430088 | tf_op jit(solution)/shard_map/ppermute | solution.py:23
  30.7 13.5 %collective-permute-start.12 = (bf16[5,112,128]{2,1,0:T(8,128)(2,1)S(1)}, bf16[5,112,128]{2,1,0:T(8,128)(2,1)S(1)}, u32[]{:S(2)}, u32[]{:S(2)}) collective-permute-start(bf16[5,112,128]{2,1,0:T(8,128)(2,1)S(1)} %get-tuple-element.37), channel_id=1, source_target_pairs={{0,20},{2,22},{4,16},{6,18},{8,28},{10,30},{12,24},{14,26},{16,4},... | collective-permute-start | bytes 430088 | tf_op jit(solution)/shard_map/ppermute | solution.py:544
  33.2 11.8 %collective-permute-start.11 = (bf16[5,112,128]{2,1,0:T(8,128)(2,1)S(1)}, bf16[5,112,128]{2,1,0:T(8,128)(2,1)S(1)}, u32[]{:S(2)}, u32[]{:S(2)}) collective-permute-start(bf16[5,112,128]{2,1,0:T(8,128)(2,1)S(1)} %get-tuple-element.37), channel_id=1, source_target_pairs={{0,18},{2,16},{4,22},{6,20},{8,26},{10,24},{12,30},{14,28},{16,2},... | collective-permute-start | bytes 430088 | tf_op jit(solution)/shard_map/ppermute | solution.py:544
  37.5 8.4 %collective-permute-start.6 = (bf16[5,112,128]{2,1,0:T(8,128)(2,1)S(1)}, bf16[5,112,128]{2,1,0:T(8,128)(2,1)S(1)}, u32[]{:S(2)}, u32[]{:S(2)}) collective-permute-start(bf16[5,112,128]{2,1,0:T(8,128)(2,1)S(1)} %fusion.14), channel_id=1, source_target_pairs={{0,20},{2,22},{4,16},{6,18},{8,28},{10,30},{12,24},{14,26},{16,4},... | collective-permute-start | bytes 430088 | tf_op jit(solution)/shard_map/ppermute | solution.py:544
  41.1 9.4 %collective-permute-start.10 = (bf16[5,112,128]{2,1,0:T(8,128)(2,1)S(1)}, bf16[5,112,128]{2,1,0:T(8,128)(2,1)S(1)}, u32[]{:S(2)}, u32[]{:S(2)}) collective-permute-start(bf16[5,112,128]{2,1,0:T(8,128)(2,1)S(1)} %get-tuple-element.37), channel_id=1, source_target_pairs={{0,16},{2,18},{4,20},{6,22},{8,24},{10,26},{12,28},{14,30},{16,0},... | collective-permute-start | bytes 430088 | tf_op jit(solution)/shard_map/ppermute | solution.py:544
  41.6 10.2 %collective-permute-start.14 = (bf16[5,112,128]{2,1,0:T(8,128)(2,1)S(1)}, bf16[5,112,128]{2,1,0:T(8,128)(2,1)S(1)}, u32[]{:S(2)}, u32[]{:S(2)}) collective-permute-start(bf16[5,112,128]{2,1,0:T(8,128)(2,1)S(1)} %fusion.14), channel_id=1, source_target_pairs={{0,16},{2,18},{4,20},{6,22},{8,24},{10,26},{12,28},{14,30},{16,0},... | collective-permute-start | bytes 430088 | tf_op jit(solution)/shard_map/ppermute | solution.py:544
  44.2 7.5 %collective-permute-start.13 = (bf16[5,112,128]{2,1,0:T(8,128)(2,1)S(1)}, bf16[5,112,128]{2,1,0:T(8,128)(2,1)S(1)}, u32[]{:S(2)}, u32[]{:S(2)}) collective-permute-start(bf16[5,112,128]{2,1,0:T(8,128)(2,1)S(1)} %collective-permute-done.12.rest_2_), channel_id=1, source_target_pairs={{0,2},{2,0},{4,6},{6,4},{1,3},{3,1},{5,7},{7,5},{8,10},{10,8},{12,... | collective-permute-start | bytes 430088 | tf_op jit(solution)/shard_map/ppermute | solution.py:23
  45.0 10.2 %collective-permute-start.5 = (bf16[5,112,128]{2,1,0:T(8,128)(2,1)S(1)}, bf16[5,112,128]{2,1,0:T(8,128)(2,1)S(1)}, u32[]{:S(2)}, u32[]{:S(2)}) collective-permute-start(bf16[5,112,128]{2,1,0:T(8,128)(2,1)S(1)} %fusion.14), channel_id=1, source_target_pairs={{0,18},{2,16},{4,22},{6,20},{8,26},{10,24},{12,30},{14,28},{16,2},... | collective-permute-start | bytes 430088 | tf_op jit(solution)/shard_map/ppermute | solution.py:544
  46.0 9.2 %collective-permute-start.7 = (bf16[5,112,128]{2,1,0:T(8,128)(2,1)S(1)}, bf16[5,112,128]{2,1,0:T(8,128)(2,1)S(1)}, u32[]{:S(2)}, u32[]{:S(2)}) collective-permute-start(bf16[5,112,128]{2,1,0:T(8,128)(2,1)S(1)} %collective-permute-done.6.rest_5_), channel_id=1, source_target_pairs={{0,2},{2,0},{4,6},{6,4},{1,3},{3,1},{5,7},{7,5},{8,10},{10,8},{12,... | collective-permute-start | bytes 430088 | tf_op jit(solution)/shard_map/ppermute | solution.py:23

commit v4 on v3

--- a/solution.py
+++ b/solution.py
@@ -11,9 +11,9 @@
 BAND = 192
 JITTER = 6
 LANES = 128
-ORDER = {}
-JOIN = True
-DIRECT = True
+ORDER = {('halo', 1): (('halo', 0),)}
+JOIN = 0
+DIRECT = (0, 1)
 GROUPS = (((0, 0), (0, 1), (0, 2), (0, 3), (1, 0), (1, 2)), ((1, 1), (1, 3)))
 VMEM_BYTES = 32 * 1024 * 1024
 
@@ -515,7 +515,9 @@
 
     def pair_sent(part):
         sent = [get("meet", part)[1]]
-        if part > 0 and JOIN:
+        if JOIN == 2:
+            sent.append(with_halo(part, 1))
+        elif part > 0 and JOIN:
             sent.append(with_halo(part - 1, 1))
         return exchange(ready("pair", part, jnp.stack(sent)), "pitch", 1)
 
@@ -523,6 +525,8 @@
         return get("pair_sent", part)[0]
 
     def beside(part):
+        if JOIN == 2:
+            return get("pair_sent", part)[1]
         if part + 1 < instances and JOIN:
             return get("pair_sent", part + 1)[1]
         return exchange(ready("beside", part, with_halo(part, 1)), "pitch", 1)
@@ -550,7 +554,7 @@
         return spread(ready("swap_across", part, get("total", part)), 2)
 
     def swap_beside(part):
-        if DIRECT:
+        if part in DIRECT:
             return spread(ready("swap_beside", part, get("total", part)), 1)
         return exchange(ready("swap_beside", part, get("swap", part)), "pitch", 1)
 

time: 57.2 us -> 56.6 us (0.990)
  waiting for transfers between devices: 13 us -> 9.85 us
  starting transfers between devices: 28.2 us -> 30.5 us
    ppermute x9 -> x10, waiting for transfers between devices: 10.3 us -> 8.02 us  [exchange(): return lax.ppermute(value, axis, [(i, i ^ distance) for i in range(count)])]
    ppermute x9 -> x10, starting transfers between devices: 19.5 us -> 21.5 us  [exchange(): return lax.ppermute(value, axis, [(i, i ^ distance) for i in range(count)])]
    ppermute x6, waiting for transfers between devices: 2.75 us -> 1.83 us  [spread(): return lax.ppermute(value, ('row', 'pitch'), pairs)]
  transfers between devices with their start and end apart: 15 -> 16, of which waited for: 9 -> 7; matrix products, arithmetic and copies ran while one was open for 0% -> 1% of each run, Pallas kernels for 17% -> 17%
where the time goes in v4:
time: 56.6 us; the launch traced here: 56.1 us
  starting transfers between devices  30.5 us (54%)
  Pallas kernels  15.2 us (27%)
  waiting for transfers between devices  9.85 us (17%)
    ppermute x10, starting transfers between devices, exchange(): return lax.ppermute(value, axis, [(i, i ^ distance) for i in range(count)])  21.5 us
    ppermute x6, starting transfers between devices, spread(): return lax.ppermute(value, ('row', 'pitch'), pairs)  8.94 us
    ppermute x10, waiting for transfers between devices, exchange(): return lax.ppermute(value, axis, [(i, i ^ distance) for i in range(count)])  8.02 us
    pallas_call x2, Pallas kernels, synthesise_call(): pl.pallas_call(functools.partial(synthesise_kernel, fields, ranks, shards...  5.24 us
    pallas_call x1, Pallas kernels, edge_call(): pl.pallas_call(functools.partial(edge_kernel, sizes), out_shape=[jax.Shap...  3.68 us
    pallas_call x1, Pallas kernels, first_call(): pl.pallas_call(functools.partial(first_kernel, sizes, shards), out_shape=...  3.5 us
    pallas_call x1, Pallas kernels, later_call(): pl.pallas_call(functools.partial(later_kernel, sizes, shards, part), out_...  2.8 us
    ppermute x6, waiting for transfers between devices, spread(): return lax.ppermute(value, ('row', 'pitch'), pairs)  1.83 us
  transfers between devices with their start and end apart: 16, of which 7 were waited for; matrix products, arithmetic and copies ran while one was open for 1% of the time, Pallas kernels for 17%

profile of v4, /device:TPU:0, one launch (start us, length us, event | category | flops | bytes accessed | tf_op | source)
XLA Modules:
  0.0 56.1 jit_solution(14499023974136312635)
XLA Ops:
  0.0 3.7 %edge.1 = (bf16[5,112,128]{2,1,0:T(8,128)(2,1)S(1)}, bf16[5,112,128]{2,1,0:T(8,128)(2,1)S(1)}, bf16[2,1024,128]{2,1,0:T(8,128)(2,1)S(1)}, bf16[5,512,1024]{2,1,0:T(8,128)(2,1)S(1)}) custom-call(s32[2]{0:T(128)} %counts_hbm.2, s32[2,64]{1,0:T(2,128)} %bitcast.19, s32[7,128]{1,0:T(8,128)} %bitcast.17, bf16[512,896]{1,0:T(8,128)(2,1)} %weight_hbm.3, ...), custom_call_target="tpu_custom_call" | custom-call | flops 372244480 | bytes 2621440 | tf_op jit(solution)/shard_map/edge/pallas_call | solution.py:213
  3.7 3.0 %collective-permute-start = (bf16[5,112,128]{2,1,0:T(8,128)(2,1)S(1)}, bf16[5,112,128]{2,1,0:T(8,128)(2,1)S(1)}, u32[]{:S(2)}, u32[]{:S(2)}) collective-permute-start(bf16[5,112,128]{2,1,0:T(8,128)(2,1)S(1)} %get-tuple-element.27), channel_id=1, source_target_pairs={{0,1},{1,0},{2,3},{3,2},{4,5},{5,4},{6,7},{7,6},{8,9},{9,8},{10,11... | collective-permute-start | bytes 430088 | tf_op jit(solution)/shard_map/ppermute | solution.py:23
  6.7 3.5 %first_part.1 = (f32[5,112,128]{2,1,0:T(8,128)S(1)}, bf16[5,112,128]{2,1,0:T(8,128)(2,1)S(1)}, f32[5,112,128]{2,1,0:T(8,128)S(1)}, bf16[5,112,128]{2,1,0:T(8,128...) custom-call(s32[7,128]{1,0:T(8,128)} %bitcast.18, bf16[512,896]{1,0:T(8,128)(2,1)} %weight_hbm.3, ...), custom_call_target="tpu_custom_call" | custom-call | flops 964689920 | bytes 5242880 | tf_op jit(solution)/shard_map/first_part/pallas_call | solution.py:311
  10.2 0.3 collective-permute-done
  10.5 1.7 %collective-permute-start.1 = (bf16[5,112,128]{2,1,0:T(8,128)(2,1)S(1)}, bf16[5,112,128]{2,1,0:T(8,128)(2,1)S(1)}, u32[]{:S(2)}, u32[]{:S(2)}) collective-permute-start(bf16[5,112,128]{2,1,0:T(8,128)(2,1)S(1)} %get-tuple-element.31), channel_id=1, source_target_pairs={{0,1},{1,0},{2,3},{3,2},{4,5},{5,4},{6,7},{7,6},{8,9},{9,8},{10,11... | collective-permute-start | bytes 430088 | tf_op jit(solution)/shard_map/ppermute | solution.py:23
  12.2 0.1 fusion.1.after_ref
  12.3 1.6 %collective-permute-start.9 = (bf16[1,5,112,128]{3,2,1,0:T(8,128)(2,1)S(1)}, bf16[1,5,112,128]{3,2,1,0:T(8,128)(2,1)S(1)}, u32[]{:S(2)}, u32[]{:S(2)}) collective-permute-start(bf16[1,5,112,128]{3,2,1,0:T(8,128)(2,1)S(1)} %bitcast.13), channel_id=1, source_target_pairs={{0,2},{2,0},{4,6},{6,4},{1,3},{3,1},{5,7},{7,5},{8,10},{10,8},{12,... | collective-permute-start | bytes 430088 | tf_op jit(solution)/shard_map/ppermute | solution.py:23
  13.9 2.8 %later_part.1 = (f32[5,112,128]{2,1,0:T(8,128)S(1)}, bf16[5,112,128]{2,1,0:T(8,128)(2,1)S(1)}, f32[5,112,128]{2,1,0:T(8,128)S(1)}, bf16[5,112,128]{2,1,0:T(8,128)(2,1)S(1)}, bf16[1024,128]{1,0:T(8,128)(2,1)S(1)}) custom-call(s32[2]{0:T(128)} %counts_hbm.2, s32[2,64]{1,0:T(2,128)} %bitcast.20, bf16[10,512,1024]{2,1,0:T(8,128)(2,1)} %bitcast.16, ...), custom_call_target="tpu_custom_call" | custom-call | flops 964689920 | bytes 5242880 | tf_op jit(solution)/shard_map/later_part/pallas_call | solution.py:364
  16.7 0.0 collective-permute-done.1
  16.7 0.1 fusion.22
  16.8 0.7 %collective-permute-start.3 = (bf16[1,5,112,128]{3,2,1,0:T(8,128)(2,1)S(1)}, bf16[1,5,112,128]{3,2,1,0:T(8,128)(2,1)S(1)}, u32[]{:S(2)}, u32[]{:S(2)}) collective-permute-start(bf16[1,5,112,128]{3,2,1,0:T(8,128)(2,1)S(1)} %fusion.22), channel_id=1, source_target_pairs={{0,2},{2,0},{4,6},{6,4},{1,3},{3,1},{5,7},{7,5},{8,10},{10,8},{12,... | collective-permute-start | bytes 430088 | tf_op jit(solution)/shard_map/ppermute | solution.py:23
  17.5 0.0 collective-permute-done.9
  17.5 0.1 fusion.7
  17.6 2.3 %collective-permute-start.8 = (bf16[5,112,128]{2,1,0:T(8,128)(2,1)S(1)}, bf16[5,112,128]{2,1,0:T(8,128)(2,1)S(1)}, u32[]{:S(2)}, u32[]{:S(2)}) collective-permute-start(bf16[5,112,128]{2,1,0:T(8,128)(2,1)S(1)} %get-tuple-element.39), channel_id=1, source_target_pairs={{0,2},{2,0},{4,6},{6,4},{1,3},{3,1},{5,7},{7,5},{8,10},{10,8},{12,... | collective-permute-start | bytes 430088 | tf_op jit(solution)/shard_map/ppermute | solution.py:23
  19.9 2.6 %collective-permute-start.10 = (bf16[5,112,128]{2,1,0:T(8,128)(2,1)S(1)}, bf16[5,112,128]{2,1,0:T(8,128)(2,1)S(1)}, u32[]{:S(2)}, u32[]{:S(2)}) collective-permute-start(bf16[5,112,128]{2,1,0:T(8,128)(2,1)S(1)} %get-tuple-element.40), channel_id=1, source_target_pairs={{0,4},{2,6},{4,0},{6,2},{1,5},{3,7},{5,1},{7,3},{8,12},{10,14},{12... | collective-permute-start | bytes 430088 | tf_op jit(solution)/shard_map/ppermute | solution.py:23
  22.5 3.9 %collective-permute-done.3 = bf16[1,5,112,128]{3,2,1,0:T(8,128)(2,1)S(1)} collective-permute-done((bf16[1,5,112,128]{3,2,1,0:T(8,128)(2,1)S(1)}, bf16[1,5,112,128]{3,2,1,0:T(8,128)(2,1)S(1)}, u32[]{:S(2)}, u32[]{:S(2)}) %collective-permute-start.3) | collective-permute-done | bytes 143392 | tf_op jit(solution)/shard_map/ppermute | solution.py:23
  26.4 0.1 fusion.16
  26.5 0.1 collective-permute-start.2
  26.6 4.1 %collective-permute-start.4 = (bf16[5,112,128]{2,1,0:T(8,128)(2,1)S(1)}, bf16[5,112,128]{2,1,0:T(8,128)(2,1)S(1)}, u32[]{:S(2)}, u32[]{:S(2)}) collective-permute-start(bf16[5,112,128]{2,1,0:T(8,128)(2,1)S(1)} %get-tuple-element.42), channel_id=1, source_target_pairs={{0,4},{2,6},{4,0},{6,2},{1,5},{3,7},{5,1},{7,3},{8,12},{10,14},{12... | collective-permute-start | bytes 430088 | tf_op jit(solution)/shard_map/ppermute | solution.py:23
  30.6 1.1 %collective-permute-done.8 = bf16[5,112,128]{2,1,0:T(8,128)(2,1)S(1)} collective-permute-done((bf16[5,112,128]{2,1,0:T(8,128)(2,1)S(1)}, bf16[5,112,128]{2,1,0:T(8,128)(2,1)S(1)}, u32[]{:S(2)}, u32[]{:S(2)}) %collective-permute-start.8) | collective-permute-done | bytes 143392 | tf_op jit(solution)/shard_map/ppermute | solution.py:23
  31.7 0.0 collective-permute-done.10
  31.7 0.1 fusion.5
  31.8 1.8 %collective-permute-start.13 = (bf16[5,112,128]{2,1,0:T(8,128)(2,1)S(1)}, bf16[5,112,128]{2,1,0:T(8,128)(2,1)S(1)}, u32[]{:S(2)}, u32[]{:S(2)}) collective-permute-start(bf16[5,112,128]{2,1,0:T(8,128)(2,1)S(1)} %fusion.5), channel_id=1, source_target_pairs={{0,20},{2,22},{4,16},{6,18},{8,28},{10,30},{12,24},{14,26},{16,4},... | collective-permute-start | bytes 430088 | tf_op jit(solution)/shard_map/ppermute | solution.py:548
  33.6 2.9 %collective-permute-start.12 = (bf16[5,112,128]{2,1,0:T(8,128)(2,1)S(1)}, bf16[5,112,128]{2,1,0:T(8,128)(2,1)S(1)}, u32[]{:S(2)}, u32[]{:S(2)}) collective-permute-start(bf16[5,112,128]{2,1,0:T(8,128)(2,1)S(1)} %fusion.5), channel_id=1, source_target_pairs={{0,18},{2,16},{4,22},{6,20},{8,26},{10,24},{12,30},{14,28},{16,2},... | collective-permute-start | bytes 430088 | tf_op jit(solution)/shard_map/ppermute | solution.py:548
  36.5 0.0 collective-permute-done.2
  36.5 2.1 %collective-permute-done.4 = bf16[5,112,128]{2,1,0:T(8,128)(2,1)S(1)} collective-permute-done((bf16[5,112,128]{2,1,0:T(8,128)(2,1)S(1)}, bf16[5,112,128]{2,1,0:T(8,128)(2,1)S(1)}, u32[]{:S(2)}, u32[]{:S(2)}) %collective-permute-start.4) | collective-permute-done | bytes 143392 | tf_op jit(solution)/shard_map/ppermute | solution.py:23
  38.6 0.1 fusion.14
  38.7 0.7 %collective-permute-start.6 = (bf16[5,112,128]{2,1,0:T(8,128)(2,1)S(1)}, bf16[5,112,128]{2,1,0:T(8,128)(2,1)S(1)}, u32[]{:S(2)}, u32[]{:S(2)}) collective-permute-start(bf16[5,112,128]{2,1,0:T(8,128)(2,1)S(1)} %fusion.14), channel_id=1, source_target_pairs={{0,20},{2,22},{4,16},{6,18},{8,28},{10,30},{12,24},{14,26},{16,4},... | collective-permute-start | bytes 430088 | tf_op jit(solution)/shard_map/ppermute | solution.py:548
  39.3 3.5 %collective-permute-start.11 = (bf16[5,112,128]{2,1,0:T(8,128)(2,1)S(1)}, bf16[5,112,128]{2,1,0:T(8,128)(2,1)S(1)}, u32[]{:S(2)}, u32[]{:S(2)}) collective-permute-start(bf16[5,112,128]{2,1,0:T(8,128)(2,1)S(1)} %fusion.5), channel_id=1, source_target_pairs={{0,16},{2,18},{4,20},{6,22},{8,24},{10,26},{12,28},{14,30},{16,0},... | collective-permute-start | bytes 430088 | tf_op jit(solution)/shard_map/ppermute | solution.py:548
  42.9 0.1 collective-permute-start.15
  42.9 1.7 %collective-permute-done.13.rest_2_ = bf16[5,112,128]{2,1,0:T(8,128)(2,1)S(1)} collective-permute-done((bf16[5,112,128]{2,1,0:T(8,128)(2,1)S(1)}, bf16[5,112,128]{2,1,0:T(8,128)(2,1)S(1)}, u32[]{:S(2)}, u32[]{:S(2)}) %collective-permute-start.13) | collective-permute-done | bytes 143392 | tf_op jit(solution)/shard_map/ppermute | solution.py:548
  44.7 2.8 %collective-permute-start.14 = (bf16[5,112,128]{2,1,0:T(8,128)(2,1)S(1)}, bf16[5,112,128]{2,1,0:T(8,128)(2,1)S(1)}, u32[]{:S(2)}, u32[]{:S(2)}) collective-permute-start(bf16[5,112,128]{2,1,0:T(8,128)(2,1)S(1)} %collective-permute-done.13.rest_2_), channel_id=1, source_target_pairs={{0,2},{2,0},{4,6},{6,4},{1,3},{3,1},{5,7},{7,5},{8,10},{10,8},{12,... | collective-permute-start | bytes 430088 | tf_op jit(solution)/shard_map/ppermute | solution.py:23
  47.4 0.0 collective-permute-done.12.rest_1_
  47.4 0.0 collective-permute-start.5
  47.4 0.0 collective-permute-done.6.rest_5_
  47.4 2.6 %collective-permute-start.7 = (bf16[5,112,128]{2,1,0:T(8,128)(2,1)S(1)}, bf16[5,112,128]{2,1,0:T(8,128)(2,1)S(1)}, u32[]{:S(2)}, u32[]{:S(2)}) collective-permute-start(bf16[5,112,128]{2,1,0:T(8,128)(2,1)S(1)} %collective-permute-done.6.rest_5_), channel_id=1, source_target_pairs={{0,2},{2,0},{4,6},{6,4},{1,3},{3,1},{5,7},{7,5},{8,10},{10,8},{12,... | collective-permute-start | bytes 430088 | tf_op jit(solution)/shard_map/ppermute | solution.py:23
  50.1 0.0 collective-permute-done.11.rest_0_
  50.1 0.1 collective-permute-done.15.rest_4_
  50.2 0.7 %collective-permute-done.14.rest_3_ = bf16[5,112,128]{2,1,0:T(8,128)(2,1)S(1)} collective-permute-done((bf16[5,112,128]{2,1,0:T(8,128)(2,1)S(1)}, bf16[5,112,128]{2,1,0:T(8,128)(2,1)S(1)}, u32[]{:S(2)}, u32[]{:S(2)}) %collective-permute-start.14) | collective-permute-done | bytes 143392 | tf_op jit(solution)/shard_map/ppermute | solution.py:23
  50.9 3.4 %synthesise.2.rest_2_ = bf16[10,448,1024]{2,1,0:T(8,128)(2,1)} custom-call(bf16[1024,128]{1,0:T(8,128)(2,1)S(1)} %get-tuple-element.29.table_ref, bf16[5,112,128]{2,1,0:T(8,128)(2,1)S(1)} %collective-permute-done.11.rest_0_, bf16[5,112,128]{2,1,0:T(8,128)(2,1)S(1)} %collective-permute-done.12.rest_1_, ...), custom_call_target="tpu_custom_call" | custom-call | flops 880803840 | bytes 6881280 | tf_op jit(solution)/shard_map/synthesise/pallas_call | solution.py:428
  54.2 0.0 collective-permute-done.5.rest_0_
  54.3 0.0 collective-permute-done.7.rest_1_
  54.3 1.9 %synthesise.3 = bf16[10,448,1024]{2,1,0:T(8,128)(2,1)} custom-call(bf16[1024,128]{1,0:T(8,128)(2,1)S(1)} %get-tuple-element.29.table_ref, bf16[5,112,128]{2,1,0:T(8,128)(2,1)S(1)} %collective-permute-done.5.rest_0_, bf16[5,112,128]{2,1,0:T(8,128)(2,1)S(1)} %collective-permute-done.7.rest_1_, ...), custom_call_target="tpu_custom_call", output_to_operand_aliasing={{}: (3, {})} | custom-call | flops 293601280 | bytes 2293760 | tf_op jit(solution)/shard_map/synthesise/pallas_call | solution.py:428
Async XLA Ops:
  3.7 6.8 %collective-permute-start = (bf16[5,112,128]{2,1,0:T(8,128)(2,1)S(1)}, bf16[5,112,128]{2,1,0:T(8,128)(2,1)S(1)}, u32[]{:S(2)}, u32[]{:S(2)}) collective-permute-start(bf16[5,112,128]{2,1,0:T(8,128)(2,1)S(1)} %get-tuple-element.27), channel_id=1, source_target_pairs={{0,1},{1,0},{2,3},{3,2},{4,5},{5,4},{6,7},{7,6},{8,9},{9,8},{10,11... | collective-permute-start | bytes 430088 | tf_op jit(solution)/shard_map/ppermute | solution.py:23
  10.5 6.2 %collective-permute-start.1 = (bf16[5,112,128]{2,1,0:T(8,128)(2,1)S(1)}, bf16[5,112,128]{2,1,0:T(8,128)(2,1)S(1)}, u32[]{:S(2)}, u32[]{:S(2)}) collective-permute-start(bf16[5,112,128]{2,1,0:T(8,128)(2,1)S(1)} %get-tuple-element.31), channel_id=1, source_target_pairs={{0,1},{1,0},{2,3},{3,2},{4,5},{5,4},{6,7},{7,6},{8,9},{9,8},{10,11... | collective-permute-start | bytes 430088 | tf_op jit(solution)/shard_map/ppermute | solution.py:23
  12.3 5.2 %collective-permute-start.9 = (bf16[1,5,112,128]{3,2,1,0:T(8,128)(2,1)S(1)}, bf16[1,5,112,128]{3,2,1,0:T(8,128)(2,1)S(1)}, u32[]{:S(2)}, u32[]{:S(2)}) collective-permute-start(bf16[1,5,112,128]{3,2,1,0:T(8,128)(2,1)S(1)} %bitcast.13), channel_id=1, source_target_pairs={{0,2},{2,0},{4,6},{6,4},{1,3},{3,1},{5,7},{7,5},{8,10},{10,8},{12,... | collective-permute-start | bytes 430088 | tf_op jit(solution)/shard_map/ppermute | solution.py:23
  16.8 9.6 %collective-permute-start.3 = (bf16[1,5,112,128]{3,2,1,0:T(8,128)(2,1)S(1)}, bf16[1,5,112,128]{3,2,1,0:T(8,128)(2,1)S(1)}, u32[]{:S(2)}, u32[]{:S(2)}) collective-permute-start(bf16[1,5,112,128]{3,2,1,0:T(8,128)(2,1)S(1)} %fusion.22), channel_id=1, source_target_pairs={{0,2},{2,0},{4,6},{6,4},{1,3},{3,1},{5,7},{7,5},{8,10},{10,8},{12,... | collective-permute-start | bytes 430088 | tf_op jit(solution)/shard_map/ppermute | solution.py:23
  17.6 14.1 %collective-permute-start.8 = (bf16[5,112,128]{2,1,0:T(8,128)(2,1)S(1)}, bf16[5,112,128]{2,1,0:T(8,128)(2,1)S(1)}, u32[]{:S(2)}, u32[]{:S(2)}) collective-permute-start(bf16[5,112,128]{2,1,0:T(8,128)(2,1)S(1)} %get-tuple-element.39), channel_id=1, source_target_pairs={{0,2},{2,0},{4,6},{6,4},{1,3},{3,1},{5,7},{7,5},{8,10},{10,8},{12,... | collective-permute-start | bytes 430088 | tf_op jit(solution)/shard_map/ppermute | solution.py:23
  19.9 11.8 %collective-permute-start.10 = (bf16[5,112,128]{2,1,0:T(8,128)(2,1)S(1)}, bf16[5,112,128]{2,1,0:T(8,128)(2,1)S(1)}, u32[]{:S(2)}, u32[]{:S(2)}) collective-permute-start(bf16[5,112,128]{2,1,0:T(8,128)(2,1)S(1)} %get-tuple-element.40), channel_id=1, source_target_pairs={{0,4},{2,6},{4,0},{6,2},{1,5},{3,7},{5,1},{7,3},{8,12},{10,14},{12... | collective-permute-start | bytes 430088 | tf_op jit(solution)/shard_map/ppermute | solution.py:23
  26.5 10.0 %collective-permute-start.2 = (bf16[5,112,128]{2,1,0:T(8,128)(2,1)S(1)}, bf16[5,112,128]{2,1,0:T(8,128)(2,1)S(1)}, u32[]{:S(2)}, u32[]{:S(2)}) collective-permute-start(bf16[5,112,128]{2,1,0:T(8,128)(2,1)S(1)} %get-tuple-element.41), channel_id=1, source_target_pairs={{0,2},{2,0},{4,6},{6,4},{1,3},{3,1},{5,7},{7,5},{8,10},{10,8},{12,... | collective-permute-start | bytes 430088 | tf_op jit(solution)/shard_map/ppermute | solution.py:23
  26.6 12.0 %collective-permute-start.4 = (bf16[5,112,128]{2,1,0:T(8,128)(2,1)S(1)}, bf16[5,112,128]{2,1,0:T(8,128)(2,1)S(1)}, u32[]{:S(2)}, u32[]{:S(2)}) collective-permute-start(bf16[5,112,128]{2,1,0:T(8,128)(2,1)S(1)} %get-tuple-element.42), channel_id=1, source_target_pairs={{0,4},{2,6},{4,0},{6,2},{1,5},{3,7},{5,1},{7,3},{8,12},{10,14},{12... | collective-permute-start | bytes 430088 | tf_op jit(solution)/shard_map/ppermute | solution.py:23
  31.8 12.8 %collective-permute-start.13 = (bf16[5,112,128]{2,1,0:T(8,128)(2,1)S(1)}, bf16[5,112,128]{2,1,0:T(8,128)(2,1)S(1)}, u32[]{:S(2)}, u32[]{:S(2)}) collective-permute-start(bf16[5,112,128]{2,1,0:T(8,128)(2,1)S(1)} %fusion.5), channel_id=1, source_target_pairs={{0,20},{2,22},{4,16},{6,18},{8,28},{10,30},{12,24},{14,26},{16,4},... | collective-permute-start | bytes 430088 | tf_op jit(solution)/shard_map/ppermute | solution.py:548
  33.6 13.8 %collective-permute-start.12 = (bf16[5,112,128]{2,1,0:T(8,128)(2,1)S(1)}, bf16[5,112,128]{2,1,0:T(8,128)(2,1)S(1)}, u32[]{:S(2)}, u32[]{:S(2)}) collective-permute-start(bf16[5,112,128]{2,1,0:T(8,128)(2,1)S(1)} %fusion.5), channel_id=1, source_target_pairs={{0,18},{2,16},{4,22},{6,20},{8,26},{10,24},{12,30},{14,28},{16,2},... | collective-permute-start | bytes 430088 | tf_op jit(solution)/shard_map/ppermute | solution.py:548
  38.7 8.8 %collective-permute-start.6 = (bf16[5,112,128]{2,1,0:T(8,128)(2,1)S(1)}, bf16[5,112,128]{2,1,0:T(8,128)(2,1)S(1)}, u32[]{:S(2)}, u32[]{:S(2)}) collective-permute-start(bf16[5,112,128]{2,1,0:T(8,128)(2,1)S(1)} %fusion.14), channel_id=1, source_target_pairs={{0,20},{2,22},{4,16},{6,18},{8,28},{10,30},{12,24},{14,26},{16,4},... | collective-permute-start | bytes 430088 | tf_op jit(solution)/shard_map/ppermute | solution.py:548
  39.3 10.7 %collective-permute-start.11 = (bf16[5,112,128]{2,1,0:T(8,128)(2,1)S(1)}, bf16[5,112,128]{2,1,0:T(8,128)(2,1)S(1)}, u32[]{:S(2)}, u32[]{:S(2)}) collective-permute-start(bf16[5,112,128]{2,1,0:T(8,128)(2,1)S(1)} %fusion.5), channel_id=1, source_target_pairs={{0,16},{2,18},{4,20},{6,22},{8,24},{10,26},{12,28},{14,30},{16,0},... | collective-permute-start | bytes 430088 | tf_op jit(solution)/shard_map/ppermute | solution.py:548
  42.9 7.3 %collective-permute-start.15 = (bf16[5,112,128]{2,1,0:T(8,128)(2,1)S(1)}, bf16[5,112,128]{2,1,0:T(8,128)(2,1)S(1)}, u32[]{:S(2)}, u32[]{:S(2)}) collective-permute-start(bf16[5,112,128]{2,1,0:T(8,128)(2,1)S(1)} %fusion.14), channel_id=1, source_target_pairs={{0,16},{2,18},{4,20},{6,22},{8,24},{10,26},{12,28},{14,30},{16,0},... | collective-permute-start | bytes 430088 | tf_op jit(solution)/shard_map/ppermute | solution.py:548
  44.7 6.2 %collective-permute-start.14 = (bf16[5,112,128]{2,1,0:T(8,128)(2,1)S(1)}, bf16[5,112,128]{2,1,0:T(8,128)(2,1)S(1)}, u32[]{:S(2)}, u32[]{:S(2)}) collective-permute-start(bf16[5,112,128]{2,1,0:T(8,128)(2,1)S(1)} %collective-permute-done.13.rest_2_), channel_id=1, source_target_pairs={{0,2},{2,0},{4,6},{6,4},{1,3},{3,1},{5,7},{7,5},{8,10},{10,8},{12,... | collective-permute-start | bytes 430088 | tf_op jit(solution)/shard_map/ppermute | solution.py:23
  47.4 6.8 %collective-permute-start.5 = (bf16[5,112,128]{2,1,0:T(8,128)(2,1)S(1)}, bf16[5,112,128]{2,1,0:T(8,128)(2,1)S(1)}, u32[]{:S(2)}, u32[]{:S(2)}) collective-permute-start(bf16[5,112,128]{2,1,0:T(8,128)(2,1)S(1)} %fusion.14), channel_id=1, source_target_pairs={{0,18},{2,16},{4,22},{6,20},{8,26},{10,24},{12,30},{14,28},{16,2},... | collective-permute-start | bytes 430088 | tf_op jit(solution)/shard_map/ppermute | solution.py:548
  47.4 6.8 %collective-permute-start.7 = (bf16[5,112,128]{2,1,0:T(8,128)(2,1)S(1)}, bf16[5,112,128]{2,1,0:T(8,128)(2,1)S(1)}, u32[]{:S(2)}, u32[]{:S(2)}) collective-permute-start(bf16[5,112,128]{2,1,0:T(8,128)(2,1)S(1)} %collective-permute-done.6.rest_5_), channel_id=1, source_target_pairs={{0,2},{2,0},{4,6},{6,4},{1,3},{3,1},{5,7},{7,5},{8,10},{10,8},{12,... | collective-permute-start | bytes 430088 | tf_op jit(solution)/shard_map/ppermute | solution.py:23

commit v5 on v4

--- a/solution.py
+++ b/solution.py
@@ -11,10 +11,10 @@
 BAND = 192
 JITTER = 6
 LANES = 128
-ORDER = {('halo', 1): (('halo', 0),)}
+ORDER = {}
 JOIN = 0
-DIRECT = (0, 1)
-GROUPS = (((0, 0), (0, 1), (0, 2), (0, 3), (1, 0), (1, 2)), ((1, 1), (1, 3)))
+DIRECT = (1,)
+GROUPS = (((0, 0), (0, 3)), ((1, 0), (1, 3), (0, 1), (0, 2)), ((1, 1), (1, 2)))
 VMEM_BYTES = 32 * 1024 * 1024
 
 
@@ -296,7 +296,7 @@
 
 
 def own_shapes(shards, fields, per, columns):
-    kinds = [jnp.bfloat16 if k % 2 else jnp.float32 for k in range(shards)]
+    kinds = [jnp.bfloat16 if k in (1, 2) else jnp.float32 for k in range(shards)]
     return [jax.ShapeDtypeStruct((fields, per, columns), kind) for kind in kinds]
 
 
@@ -511,7 +511,7 @@
         return total.astype(jnp.bfloat16)
 
     def meet(part):
-        return None, with_halo(part, 3)
+        return None, with_halo(part, 2)
 
     def pair_sent(part):
         sent = [get("meet", part)[1]]
@@ -533,7 +533,7 @@
 
     def across(part):
         return exchange(
-            ready("across", part, with_halo(part, 2, get("pair", part))), "pitch", 2
+            ready("across", part, with_halo(part, 3, get("pair", part))), "pitch", 3
         )
 
     def total(part):
@@ -551,7 +551,7 @@
         return spread(ready("swap", part, get("total", part)), 0)
 
     def swap_across(part):
-        return spread(ready("swap_across", part, get("total", part)), 2)
+        return spread(ready("swap_across", part, get("total", part)), 3)
 
     def swap_beside(part):
         if part in DIRECT:
@@ -571,7 +571,7 @@
         later=later, halo=halo, meet=meet, pair_sent=pair_sent, pair=pair, beside=beside, across=across, total=total,
         swap=swap, swap_across=swap_across, swap_beside=swap_beside, across_on=across_on,
     )
-    names = ("swap", "swap_beside", "swap_across", "across_on")
+    names = ("swap", "swap_beside", "across_on", "swap_across")
 
     def whole_sum(part):
         get("later", part)

time: 56.6 us -> 55.5 us (0.981)
  starting transfers between devices: 30.5 us -> 27.6 us
  Pallas kernels: 15.2 us -> 16.3 us
  waiting for transfers between devices: 9.85 us -> 10.8 us
    ppermute x10 -> x11, starting transfers between devices: 21.5 us -> 19.7 us  [exchange(): return lax.ppermute(value, axis, [(i, i ^ distance) for i in range(count)])]
    ppermute x10 -> x11, waiting for transfers between devices: 8.02 us -> 9.63 us  [exchange(): return lax.ppermute(value, axis, [(i, i ^ distance) for i in range(count)])]
    pallas_call x2 -> x3, Pallas kernels: 5.24 us -> 6.35 us  [synthesise_call(): pl.pallas_call(functools.partial(synthesise_kernel, fields, ranks, shards...]
    ppermute x6 -> x5, starting transfers between devices: 8.94 us -> 7.91 us  [spread(): return lax.ppermute(value, ('row', 'pitch'), pairs)]
    ppermute x6 -> x5, waiting for transfers between devices: 1.83 us -> 1.17 us  [spread(): return lax.ppermute(value, ('row', 'pitch'), pairs)]
  transfers between devices with their start and end apart: 16 -> 16, of which waited for: 7 -> 9; matrix products, arithmetic and copies ran while one was open for 1% -> 1% of each run, Pallas kernels for 17% -> 20%
where the time goes in v5:
time: 55.5 us; the launch traced here: 55.3 us
  starting transfers between devices  27.6 us (50%)
  Pallas kernels  16.3 us (29%)
  waiting for transfers between devices  10.8 us (19%)
    ppermute x11, starting transfers between devices, exchange(): return lax.ppermute(value, axis, [(i, i ^ distance) for i in range(count)])  19.7 us
    ppermute x11, waiting for transfers between devices, exchange(): return lax.ppermute(value, axis, [(i, i ^ distance) for i in range(count)])  9.63 us
    ppermute x5, starting transfers between devices, spread(): return lax.ppermute(value, ('row', 'pitch'), pairs)  7.91 us
    pallas_call x3, Pallas kernels, synthesise_call(): pl.pallas_call(functools.partial(synthesise_kernel, fields, ranks, shards...  6.35 us
    pallas_call x1, Pallas kernels, edge_call(): pl.pallas_call(functools.partial(edge_kernel, sizes), out_shape=[jax.Shap...  3.68 us
    pallas_call x1, Pallas kernels, first_call(): pl.pallas_call(functools.partial(first_kernel, sizes, shards), out_shape=...  3.5 us
    pallas_call x1, Pallas kernels, later_call(): pl.pallas_call(functools.partial(later_kernel, sizes, shards, part), out_...  2.8 us
    ppermute x5, waiting for transfers between devices, spread(): return lax.ppermute(value, ('row', 'pitch'), pairs)  1.17 us
  transfers between devices with their start and end apart: 16, of which 9 were waited for; matrix products, arithmetic and copies ran while one was open for 1% of the time, Pallas kernels for 20%

profile of v5, /device:TPU:0, one launch (start us, length us, event | category | flops | bytes accessed | tf_op | source)
XLA Modules:
  0.0 55.3 jit_solution(7714242340110800721)
XLA Ops:
  0.0 3.7 %edge.1 = (bf16[5,112,128]{2,1,0:T(8,128)(2,1)S(1)}, bf16[5,112,128]{2,1,0:T(8,128)(2,1)S(1)}, bf16[2,1024,128]{2,1,0:T(8,128)(2,1)S(1)}, bf16[5,512,1024]{2,1,0:T(8,128)(2,1)S(1)}) custom-call(s32[2]{0:T(128)} %counts_hbm.2, s32[2,64]{1,0:T(2,128)} %bitcast.19, s32[7,128]{1,0:T(8,128)} %bitcast.17, bf16[512,896]{1,0:T(8,128)(2,1)} %weight_hbm.3, ...), custom_call_target="tpu_custom_call" | custom-call | flops 372244480 | bytes 2621440 | tf_op jit(solution)/shard_map/edge/pallas_call | solution.py:213
  3.7 3.0 %collective-permute-start = (bf16[5,112,128]{2,1,0:T(8,128)(2,1)S(1)}, bf16[5,112,128]{2,1,0:T(8,128)(2,1)S(1)}, u32[]{:S(2)}, u32[]{:S(2)}) collective-permute-start(bf16[5,112,128]{2,1,0:T(8,128)(2,1)S(1)} %get-tuple-element.26), channel_id=1, source_target_pairs={{0,1},{1,0},{2,3},{3,2},{4,5},{5,4},{6,7},{7,6},{8,9},{9,8},{10,11... | collective-permute-start | bytes 430088 | tf_op jit(solution)/shard_map/ppermute | solution.py:23
  6.7 0.1 collective-permute-start.1
  6.8 3.5 %first_part.1 = (f32[5,112,128]{2,1,0:T(8,128)S(1)}, bf16[5,112,128]{2,1,0:T(8,128)(2,1)S(1)}, bf16[5,112,128]{2,1,0:T(8,128)(2,1)S(1)}, f32[5,112,128]{2,1,0:T(...) custom-call(s32[7,128]{1,0:T(8,128)} %bitcast.18, bf16[512,896]{1,0:T(8,128)(2,1)} %weight_hbm.3, ...), custom_call_target="tpu_custom_call" | custom-call | flops 964689920 | bytes 5242880 | tf_op jit(solution)/shard_map/first_part/pallas_call | solution.py:311
  10.3 1.0 %collective-permute-done = bf16[5,112,128]{2,1,0:T(8,128)(2,1)S(1)} collective-permute-done((bf16[5,112,128]{2,1,0:T(8,128)(2,1)S(1)}, bf16[5,112,128]{2,1,0:T(8,128)(2,1)S(1)}, u32[]{:S(2)}, u32[]{:S(2)}) %collective-permute-start) | collective-permute-done | bytes 143392 | tf_op jit(solution)/shard_map/ppermute | solution.py:23
  11.3 0.1 fusion.1.after_ref
  11.3 2.2 %collective-permute-start.10 = (bf16[1,5,112,128]{3,2,1,0:T(8,128)(2,1)S(1)}, bf16[1,5,112,128]{3,2,1,0:T(8,128)(2,1)S(1)}, u32[]{:S(2)}, u32[]{:S(2)}) collective-permute-start(bf16[1,5,112,128]{3,2,1,0:T(8,128)(2,1)S(1)} %bitcast.13), channel_id=1, source_target_pairs={{0,2},{2,0},{4,6},{6,4},{1,3},{3,1},{5,7},{7,5},{8,10},{10,8},{12,... | collective-permute-start | bytes 430088 | tf_op jit(solution)/shard_map/ppermute | solution.py:23
  13.5 2.8 %later_part.1 = (f32[5,112,128]{2,1,0:T(8,128)S(1)}, bf16[5,112,128]{2,1,0:T(8,128)(2,1)S(1)}, bf16[5,112,128]{2,1,0:T(8,128)(2,1)S(1)}, f32[5,112,128]{2,1,0:T(8,128)S(1)}, bf16[1024,128]{1,0:T(8,128)(2,1)S(1)}) custom-call(s32[2]{0:T(128)} %counts_hbm.2, s32[2,64]{1,0:T(2,128)} %bitcast.20, bf16[10,512,1024]{2,1,0:T(8,128)(2,1)} %bitcast.16, ...), custom_call_target="tpu_custom_call" | custom-call | flops 964689920 | bytes 5242880 | tf_op jit(solution)/shard_map/later_part/pallas_call | solution.py:364
  16.4 0.0 collective-permute-done.1
  16.4 0.1 fusion.22
  16.4 0.1 collective-permute-start.3
  16.5 1.0 %collective-permute-done.10 = bf16[1,5,112,128]{3,2,1,0:T(8,128)(2,1)S(1)} collective-permute-done((bf16[1,5,112,128]{3,2,1,0:T(8,128)(2,1)S(1)}, bf16[1,5,112,128]{3,2,1,0:T(8,128)(2,1)S(1)}, u32[]{:S(2)}, u32[]{:S(2)}) %collective-permute-start.10) | collective-permute-done | bytes 143392 | tf_op jit(solution)/shard_map/ppermute | solution.py:23
  17.5 0.1 fusion.7
  17.6 4.4 %collective-permute-start.11 = (bf16[5,112,128]{2,1,0:T(8,128)(2,1)S(1)}, bf16[5,112,128]{2,1,0:T(8,128)(2,1)S(1)}, u32[]{:S(2)}, u32[]{:S(2)}) collective-permute-start(bf16[5,112,128]{2,1,0:T(8,128)(2,1)S(1)} %get-tuple-element.38), channel_id=1, source_target_pairs={{0,6},{2,4},{4,2},{6,0},{1,7},{3,5},{5,3},{7,1},{8,14},{10,12},{12... | collective-permute-start | bytes 430088 | tf_op jit(solution)/shard_map/ppermute | solution.py:23
  22.1 0.0 collective-permute-start.9
  22.1 2.1 %collective-permute-done.3 = bf16[1,5,112,128]{3,2,1,0:T(8,128)(2,1)S(1)} collective-permute-done((bf16[1,5,112,128]{3,2,1,0:T(8,128)(2,1)S(1)}, bf16[1,5,112,128]{3,2,1,0:T(8,128)(2,1)S(1)}, u32[]{:S(2)}, u32[]{:S(2)}) %collective-permute-start.3) | collective-permute-done | bytes 143392 | tf_op jit(solution)/shard_map/ppermute | solution.py:23
  24.1 0.1 fusion.16
  24.2 0.1 collective-permute-start.2
  24.3 3.1 %collective-permute-start.4 = (bf16[5,112,128]{2,1,0:T(8,128)(2,1)S(1)}, bf16[5,112,128]{2,1,0:T(8,128)(2,1)S(1)}, u32[]{:S(2)}, u32[]{:S(2)}) collective-permute-start(bf16[5,112,128]{2,1,0:T(8,128)(2,1)S(1)} %get-tuple-element.40), channel_id=1, source_target_pairs={{0,6},{2,4},{4,2},{6,0},{1,7},{3,5},{5,3},{7,1},{8,14},{10,12},{12... | collective-permute-start | bytes 430088 | tf_op jit(solution)/shard_map/ppermute | solution.py:23
  27.4 0.8 %collective-permute-done.11 = bf16[5,112,128]{2,1,0:T(8,128)(2,1)S(1)} collective-permute-done((bf16[5,112,128]{2,1,0:T(8,128)(2,1)S(1)}, bf16[5,112,128]{2,1,0:T(8,128)(2,1)S(1)}, u32[]{:S(2)}, u32[]{:S(2)}) %collective-permute-start.11) | collective-permute-done | bytes 143392 | tf_op jit(solution)/shard_map/ppermute | solution.py:23
  28.3 1.9 %collective-permute-done.9 = bf16[5,112,128]{2,1,0:T(8,128)(2,1)S(1)} collective-permute-done((bf16[5,112,128]{2,1,0:T(8,128)(2,1)S(1)}, bf16[5,112,128]{2,1,0:T(8,128)(2,1)S(1)}, u32[]{:S(2)}, u32[]{:S(2)}) %collective-permute-start.9) | collective-permute-done | bytes 143392 | tf_op jit(solution)/shard_map/ppermute | solution.py:23
  30.2 0.1 fusion.5
  30.3 1.6 %collective-permute-start.12 = (bf16[5,112,128]{2,1,0:T(8,128)(2,1)S(1)}, bf16[5,112,128]{2,1,0:T(8,128)(2,1)S(1)}, u32[]{:S(2)}, u32[]{:S(2)}) collective-permute-start(bf16[5,112,128]{2,1,0:T(8,128)(2,1)S(1)} %fusion.5), channel_id=1, source_target_pairs={{0,16},{2,18},{4,20},{6,22},{8,24},{10,26},{12,28},{14,30},{16,0},... | collective-permute-start | bytes 430088 | tf_op jit(solution)/shard_map/ppermute | solution.py:548
  31.9 3.3 %collective-permute-start.14 = (bf16[5,112,128]{2,1,0:T(8,128)(2,1)S(1)}, bf16[5,112,128]{2,1,0:T(8,128)(2,1)S(1)}, u32[]{:S(2)}, u32[]{:S(2)}) collective-permute-start(bf16[5,112,128]{2,1,0:T(8,128)(2,1)S(1)} %fusion.5), channel_id=1, source_target_pairs={{0,22},{2,20},{4,18},{6,16},{8,30},{10,28},{12,26},{14,24},{16,6},... | collective-permute-start | bytes 430088 | tf_op jit(solution)/shard_map/ppermute | solution.py:548
  35.2 0.0 collective-permute-done.2
  35.2 0.9 %collective-permute-done.4 = bf16[5,112,128]{2,1,0:T(8,128)(2,1)S(1)} collective-permute-done((bf16[5,112,128]{2,1,0:T(8,128)(2,1)S(1)}, bf16[5,112,128]{2,1,0:T(8,128)(2,1)S(1)}, u32[]{:S(2)}, u32[]{:S(2)}) %collective-permute-start.4) | collective-permute-done | bytes 143392 | tf_op jit(solution)/shard_map/ppermute | solution.py:23
  36.1 0.1 fusion.14
  36.2 2.9 %collective-permute-start.6 = (bf16[5,112,128]{2,1,0:T(8,128)(2,1)S(1)}, bf16[5,112,128]{2,1,0:T(8,128)(2,1)S(1)}, u32[]{:S(2)}, u32[]{:S(2)}) collective-permute-start(bf16[5,112,128]{2,1,0:T(8,128)(2,1)S(1)} %fusion.14), channel_id=1, source_target_pairs={{0,22},{2,20},{4,18},{6,16},{8,30},{10,28},{12,26},{14,24},{16,6},... | collective-permute-start | bytes 430088 | tf_op jit(solution)/shard_map/ppermute | solution.py:548
  39.1 0.1 collective-permute-start.8
  39.2 0.0 collective-permute-done.12.rest_0_
  39.2 2.1 %collective-permute-start.13 = (bf16[5,112,128]{2,1,0:T(8,128)(2,1)S(1)}, bf16[5,112,128]{2,1,0:T(8,128)(2,1)S(1)}, u32[]{:S(2)}, u32[]{:S(2)}) collective-permute-start(bf16[5,112,128]{2,1,0:T(8,128)(2,1)S(1)} %collective-permute-done.12.rest_0_), channel_id=1, source_target_pairs={{0,2},{2,0},{4,6},{6,4},{1,3},{3,1},{5,7},{7,5},{8,10},{10,8},{12,... | collective-permute-start | bytes 430088 | tf_op jit(solution)/shard_map/ppermute | solution.py:23
  41.3 0.0 collective-permute-done.14.rest_1_
  41.3 3.2 %collective-permute-start.15 = (bf16[5,112,128]{2,1,0:T(8,128)(2,1)S(1)}, bf16[5,112,128]{2,1,0:T(8,128)(2,1)S(1)}, u32[]{:S(2)}, u32[]{:S(2)}) collective-permute-start(bf16[5,112,128]{2,1,0:T(8,128)(2,1)S(1)} %collective-permute-done.14.rest_1_), channel_id=1, source_target_pairs={{0,2},{2,0},{4,6},{6,4},{1,3},{3,1},{5,7},{7,5},{8,10},{10,8},{12,... | collective-permute-start | bytes 430088 | tf_op jit(solution)/shard_map/ppermute | solution.py:23
  44.5 0.0 collective-permute-start.5
  44.5 1.2 %collective-permute-done.6.rest_1_ = bf16[5,112,128]{2,1,0:T(8,128)(2,1)S(1)} collective-permute-done((bf16[5,112,128]{2,1,0:T(8,128)(2,1)S(1)}, bf16[5,112,128]{2,1,0:T(8,128)(2,1)S(1)}, u32[]{:S(2)}, u32[]{:S(2)}) %collective-permute-start.6) | collective-permute-done | bytes 143392 | tf_op jit(solution)/shard_map/ppermute | solution.py:548
  45.6 1.4 %collective-permute-start.7 = (bf16[5,112,128]{2,1,0:T(8,128)(2,1)S(1)}, bf16[5,112,128]{2,1,0:T(8,128)(2,1)S(1)}, u32[]{:S(2)}, u32[]{:S(2)}) collective-permute-start(bf16[5,112,128]{2,1,0:T(8,128)(2,1)S(1)} %collective-permute-done.6.rest_1_), channel_id=1, source_target_pairs={{0,2},{2,0},{4,6},{6,4},{1,3},{3,1},{5,7},{7,5},{8,10},{10,8},{12,... | collective-permute-start | bytes 430088 | tf_op jit(solution)/shard_map/ppermute | solution.py:23
  47.1 1.9 %synthesise.3.rest_4_ = bf16[10,448,1024]{2,1,0:T(8,128)(2,1)} custom-call(bf16[1024,128]{1,0:T(8,128)(2,1)S(1)} %get-tuple-element.28.table_ref, bf16[5,112,128]{2,1,0:T(8,128)(2,1)S(1)} %collective-permute-done.12.rest_0_, bf16[5,112,128]{2,1,0:T(8,128)(2,1)S(1)} %collective-permute-done.14.rest_1_), custom_call_target="tpu_custom_call" | custom-call | flops 293601280 | bytes 2293760 | tf_op jit(solution)/shard_map/synthesise/pallas_call | solution.py:428
  48.9 0.0 collective-permute-done.8.rest_0_
  48.9 0.0 collective-permute-done.13.rest_2_
  49.0 1.5 %collective-permute-done.15.rest_3_ = bf16[5,112,128]{2,1,0:T(8,128)(2,1)S(1)} collective-permute-done((bf16[5,112,128]{2,1,0:T(8,128)(2,1)S(1)}, bf16[5,112,128]{2,1,0:T(8,128)(2,1)S(1)}, u32[]{:S(2)}, u32[]{:S(2)}) %collective-permute-start.15) | collective-permute-done | bytes 143392 | tf_op jit(solution)/shard_map/ppermute | solution.py:23
  50.4 2.6 %synthesise.4.rest_2_ = bf16[10,448,1024]{2,1,0:T(8,128)(2,1)} custom-call(bf16[1024,128]{1,0:T(8,128)(2,1)S(1)} %get-tuple-element.28.table_ref, bf16[5,112,128]{2,1,0:T(8,128)(2,1)S(1)} %collective-permute-done.8.rest_0_, bf16[5,112,128]{2,1,0:T(8,128)(2,1)S(1)} %collective-permute-done.6.rest_1_, ...), custom_call_target="tpu_custom_call", output_to_operand_aliasing={{}: (5, {})} | custom-call | flops 587202560 | bytes 4587520 | tf_op jit(solution)/shard_map/synthesise/pallas_call | solution.py:428
  53.0 0.0 collective-permute-done.5.rest_0_
  53.1 0.4 collective-permute-done.7.rest_1_
  53.5 1.9 %synthesise.5 = bf16[10,448,1024]{2,1,0:T(8,128)(2,1)} custom-call(bf16[1024,128]{1,0:T(8,128)(2,1)S(1)} %get-tuple-element.28.table_ref, bf16[5,112,128]{2,1,0:T(8,128)(2,1)S(1)} %collective-permute-done.5.rest_0_, bf16[5,112,128]{2,1,0:T(8,128)(2,1)S(1)} %collective-permute-done.7.rest_1_, ...), custom_call_target="tpu_custom_call", output_to_operand_aliasing={{}: (3, {})} | custom-call | flops 293601280 | bytes 2293760 | tf_op jit(solution)/shard_map/synthesise/pallas_call | solution.py:428
Async XLA Ops:
  3.7 7.6 %collective-permute-start = (bf16[5,112,128]{2,1,0:T(8,128)(2,1)S(1)}, bf16[5,112,128]{2,1,0:T(8,128)(2,1)S(1)}, u32[]{:S(2)}, u32[]{:S(2)}) collective-permute-start(bf16[5,112,128]{2,1,0:T(8,128)(2,1)S(1)} %get-tuple-element.26), channel_id=1, source_target_pairs={{0,1},{1,0},{2,3},{3,2},{4,5},{5,4},{6,7},{7,6},{8,9},{9,8},{10,11... | collective-permute-start | bytes 430088 | tf_op jit(solution)/shard_map/ppermute | solution.py:23
  6.7 9.7 %collective-permute-start.1 = (bf16[5,112,128]{2,1,0:T(8,128)(2,1)S(1)}, bf16[5,112,128]{2,1,0:T(8,128)(2,1)S(1)}, u32[]{:S(2)}, u32[]{:S(2)}) collective-permute-start(bf16[5,112,128]{2,1,0:T(8,128)(2,1)S(1)} %get-tuple-element.29), channel_id=1, source_target_pairs={{0,1},{1,0},{2,3},{3,2},{4,5},{5,4},{6,7},{7,6},{8,9},{9,8},{10,11... | collective-permute-start | bytes 430088 | tf_op jit(solution)/shard_map/ppermute | solution.py:23
  11.3 6.2 %collective-permute-start.10 = (bf16[1,5,112,128]{3,2,1,0:T(8,128)(2,1)S(1)}, bf16[1,5,112,128]{3,2,1,0:T(8,128)(2,1)S(1)}, u32[]{:S(2)}, u32[]{:S(2)}) collective-permute-start(bf16[1,5,112,128]{3,2,1,0:T(8,128)(2,1)S(1)} %bitcast.13), channel_id=1, source_target_pairs={{0,2},{2,0},{4,6},{6,4},{1,3},{3,1},{5,7},{7,5},{8,10},{10,8},{12,... | collective-permute-start | bytes 430088 | tf_op jit(solution)/shard_map/ppermute | solution.py:23
  16.4 7.7 %collective-permute-start.3 = (bf16[1,5,112,128]{3,2,1,0:T(8,128)(2,1)S(1)}, bf16[1,5,112,128]{3,2,1,0:T(8,128)(2,1)S(1)}, u32[]{:S(2)}, u32[]{:S(2)}) collective-permute-start(bf16[1,5,112,128]{3,2,1,0:T(8,128)(2,1)S(1)} %fusion.22), channel_id=1, source_target_pairs={{0,2},{2,0},{4,6},{6,4},{1,3},{3,1},{5,7},{7,5},{8,10},{10,8},{12,... | collective-permute-start | bytes 430088 | tf_op jit(solution)/shard_map/ppermute | solution.py:23
  17.6 10.6 %collective-permute-start.11 = (bf16[5,112,128]{2,1,0:T(8,128)(2,1)S(1)}, bf16[5,112,128]{2,1,0:T(8,128)(2,1)S(1)}, u32[]{:S(2)}, u32[]{:S(2)}) collective-permute-start(bf16[5,112,128]{2,1,0:T(8,128)(2,1)S(1)} %get-tuple-element.38), channel_id=1, source_target_pairs={{0,6},{2,4},{4,2},{6,0},{1,7},{3,5},{5,3},{7,1},{8,14},{10,12},{12... | collective-permute-start | bytes 430088 | tf_op jit(solution)/shard_map/ppermute | solution.py:23
  22.1 8.1 %collective-permute-start.9 = (bf16[5,112,128]{2,1,0:T(8,128)(2,1)S(1)}, bf16[5,112,128]{2,1,0:T(8,128)(2,1)S(1)}, u32[]{:S(2)}, u32[]{:S(2)}) collective-permute-start(bf16[5,112,128]{2,1,0:T(8,128)(2,1)S(1)} %get-tuple-element.37), channel_id=1, source_target_pairs={{0,2},{2,0},{4,6},{6,4},{1,3},{3,1},{5,7},{7,5},{8,10},{10,8},{12,... | collective-permute-start | bytes 430088 | tf_op jit(solution)/shard_map/ppermute | solution.py:23
  24.2 11.0 %collective-permute-start.2 = (bf16[5,112,128]{2,1,0:T(8,128)(2,1)S(1)}, bf16[5,112,128]{2,1,0:T(8,128)(2,1)S(1)}, u32[]{:S(2)}, u32[]{:S(2)}) collective-permute-start(bf16[5,112,128]{2,1,0:T(8,128)(2,1)S(1)} %get-tuple-element.39), channel_id=1, source_target_pairs={{0,2},{2,0},{4,6},{6,4},{1,3},{3,1},{5,7},{7,5},{8,10},{10,8},{12,... | collective-permute-start | bytes 430088 | tf_op jit(solution)/shard_map/ppermute | solution.py:23
  24.3 11.8 %collective-permute-start.4 = (bf16[5,112,128]{2,1,0:T(8,128)(2,1)S(1)}, bf16[5,112,128]{2,1,0:T(8,128)(2,1)S(1)}, u32[]{:S(2)}, u32[]{:S(2)}) collective-permute-start(bf16[5,112,128]{2,1,0:T(8,128)(2,1)S(1)} %get-tuple-element.40), channel_id=1, source_target_pairs={{0,6},{2,4},{4,2},{6,0},{1,7},{3,5},{5,3},{7,1},{8,14},{10,12},{12... | collective-permute-start | bytes 430088 | tf_op jit(solution)/shard_map/ppermute | solution.py:23
  30.3 8.9 %collective-permute-start.12 = (bf16[5,112,128]{2,1,0:T(8,128)(2,1)S(1)}, bf16[5,112,128]{2,1,0:T(8,128)(2,1)S(1)}, u32[]{:S(2)}, u32[]{:S(2)}) collective-permute-start(bf16[5,112,128]{2,1,0:T(8,128)(2,1)S(1)} %fusion.5), channel_id=1, source_target_pairs={{0,16},{2,18},{4,20},{6,22},{8,24},{10,26},{12,28},{14,30},{16,0},... | collective-permute-start | bytes 430088 | tf_op jit(solution)/shard_map/ppermute | solution.py:548
  31.9 9.4 %collective-permute-start.14 = (bf16[5,112,128]{2,1,0:T(8,128)(2,1)S(1)}, bf16[5,112,128]{2,1,0:T(8,128)(2,1)S(1)}, u32[]{:S(2)}, u32[]{:S(2)}) collective-permute-start(bf16[5,112,128]{2,1,0:T(8,128)(2,1)S(1)} %fusion.5), channel_id=1, source_target_pairs={{0,22},{2,20},{4,18},{6,16},{8,30},{10,28},{12,26},{14,24},{16,6},... | collective-permute-start | bytes 430088 | tf_op jit(solution)/shard_map/ppermute | solution.py:548
  36.2 9.5 %collective-permute-start.6 = (bf16[5,112,128]{2,1,0:T(8,128)(2,1)S(1)}, bf16[5,112,128]{2,1,0:T(8,128)(2,1)S(1)}, u32[]{:S(2)}, u32[]{:S(2)}) collective-permute-start(bf16[5,112,128]{2,1,0:T(8,128)(2,1)S(1)} %fusion.14), channel_id=1, source_target_pairs={{0,22},{2,20},{4,18},{6,16},{8,30},{10,28},{12,26},{14,24},{16,6},... | collective-permute-start | bytes 430088 | tf_op jit(solution)/shard_map/ppermute | solution.py:548
  39.1 9.9 %collective-permute-start.8 = (bf16[5,112,128]{2,1,0:T(8,128)(2,1)S(1)}, bf16[5,112,128]{2,1,0:T(8,128)(2,1)S(1)}, u32[]{:S(2)}, u32[]{:S(2)}) collective-permute-start(bf16[5,112,128]{2,1,0:T(8,128)(2,1)S(1)} %fusion.14), channel_id=1, source_target_pairs={{0,16},{2,18},{4,20},{6,22},{8,24},{10,26},{12,28},{14,30},{16,0},... | collective-permute-start | bytes 430088 | tf_op jit(solution)/shard_map/ppermute | solution.py:548
  39.2 9.7 %collective-permute-start.13 = (bf16[5,112,128]{2,1,0:T(8,128)(2,1)S(1)}, bf16[5,112,128]{2,1,0:T(8,128)(2,1)S(1)}, u32[]{:S(2)}, u32[]{:S(2)}) collective-permute-start(bf16[5,112,128]{2,1,0:T(8,128)(2,1)S(1)} %collective-permute-done.12.rest_0_), channel_id=1, source_target_pairs={{0,2},{2,0},{4,6},{6,4},{1,3},{3,1},{5,7},{7,5},{8,10},{10,8},{12,... | collective-permute-start | bytes 430088 | tf_op jit(solution)/shard_map/ppermute | solution.py:23
  41.3 9.1 %collective-permute-start.15 = (bf16[5,112,128]{2,1,0:T(8,128)(2,1)S(1)}, bf16[5,112,128]{2,1,0:T(8,128)(2,1)S(1)}, u32[]{:S(2)}, u32[]{:S(2)}) collective-permute-start(bf16[5,112,128]{2,1,0:T(8,128)(2,1)S(1)} %collective-permute-done.14.rest_1_), channel_id=1, source_target_pairs={{0,2},{2,0},{4,6},{6,4},{1,3},{3,1},{5,7},{7,5},{8,10},{10,8},{12,... | collective-permute-start | bytes 430088 | tf_op jit(solution)/shard_map/ppermute | solution.py:23
  44.5 8.6 %collective-permute-start.5 = (bf16[5,112,128]{2,1,0:T(8,128)(2,1)S(1)}, bf16[5,112,128]{2,1,0:T(8,128)(2,1)S(1)}, u32[]{:S(2)}, u32[]{:S(2)}) collective-permute-start(bf16[5,112,128]{2,1,0:T(8,128)(2,1)S(1)} %fusion.14), channel_id=1, source_target_pairs={{0,18},{2,16},{4,22},{6,20},{8,26},{10,24},{12,30},{14,28},{16,2},... | collective-permute-start | bytes 430088 | tf_op jit(solution)/shard_map/ppermute | solution.py:548
  45.6 7.8 %collective-permute-start.7 = (bf16[5,112,128]{2,1,0:T(8,128)(2,1)S(1)}, bf16[5,112,128]{2,1,0:T(8,128)(2,1)S(1)}, u32[]{:S(2)}, u32[]{:S(2)}) collective-permute-start(bf16[5,112,128]{2,1,0:T(8,128)(2,1)S(1)} %collective-permute-done.6.rest_1_), channel_id=1, source_target_pairs={{0,2},{2,0},{4,6},{6,4},{1,3},{3,1},{5,7},{7,5},{8,10},{10,8},{12,... | collective-permute-start | bytes 430088 | tf_op jit(solution)/shard_map/ppermute | solution.py:23

commit v6 on v5

--- a/solution.py
+++ b/solution.py
@@ -390,24 +390,25 @@
     pitch_at = lax.axis_index("pitch")
     copies = []
     for i, (part, k) in enumerate(ranks):
-        piece = piece_refs[i][...]
-        value = lax.dot_general(
-            piece.reshape(fields * per, piece.shape[2]),
-            table_ref[...],
-            (((1,), (1,)), ((), ())),
-            preferred_element_type=jnp.float32,
-        )
-        rows_ref[i] = value.astype(rows_ref.dtype).reshape(fields, per, value.shape[1])
         at = jnp.bitwise_xor(pitch_at, k) if shards > 1 else 0
-        copies += started(
-            pltpu.make_async_copy(
-                rows_ref.at[i],
-                out_hbm.at[
-                    pl.ds(part * fields, fields), pl.ds(pl.multiple_of(at * per, 16), per), :
-                ],
-                sems.at[i],
+        place = pl.ds(pl.multiple_of(at * per, 16), per)
+        cuts = [0, (fields + 1) // 2, fields]
+        for half, (low, high) in enumerate(zip(cuts, cuts[1:])):
+            piece = piece_refs[i][low:high]
+            value = lax.dot_general(
+                piece.reshape((high - low) * per, piece.shape[2]),
+                table_ref[...],
+                (((1,), (1,)), ((), ())),
+                preferred_element_type=jnp.float32,
             )
-        )
+            rows_ref[i, low:high] = value.astype(rows_ref.dtype).reshape(high - low, per, -1)
+            copies += started(
+                pltpu.make_async_copy(
+                    rows_ref.at[i, pl.ds(low, high - low)],
+                    out_hbm.at[pl.ds(part * fields + low, high - low), place, :],
+                    sems.at[i, half],
+                )
+            )
     for copy in copies:
         copy.wait()
 
@@ -432,7 +433,7 @@
         out_specs=hbm,
         scratch_shapes=[
             pltpu.VMEM((len(ranks), fields, per, pitch), jnp.bfloat16),
-            pltpu.SemaphoreType.DMA((len(ranks),)),
+            pltpu.SemaphoreType.DMA((len(ranks), 2)),
         ],
         input_output_aliases=aliases,
         compiler_params=pltpu.CompilerParams(vmem_limit_bytes=VMEM_BYTES),

time: 55.5 us -> 55.4 us (level)
  transfers between devices with their start and end apart: 16 -> 16, of which waited for: 9 -> 9; matrix products, arithmetic and copies ran while one was open for 1% -> 1% of each run, Pallas kernels for 20% -> 19%
where the time goes in v6:
time: 55.4 us; the launch traced here: 55.2 us
  starting transfers between devices  27.6 us (50%)
  Pallas kernels  16 us (29%)
  waiting for transfers between devices  11 us (20%)
    ppermute x11, starting transfers between devices, exchange(): return lax.ppermute(value, axis, [(i, i ^ distance) for i in range(count)])  19.7 us
    ppermute x11, waiting for transfers between devices, exchange(): return lax.ppermute(value, axis, [(i, i ^ distance) for i in range(count)])  9.84 us
    ppermute x5, starting transfers between devices, spread(): return lax.ppermute(value, ('row', 'pitch'), pairs)  7.91 us
    pallas_call x3, Pallas kernels, synthesise_call(): pl.pallas_call(functools.partial(synthesise_kernel, fields, ranks, shards...  6.03 us
    pallas_call x1, Pallas kernels, edge_call(): pl.pallas_call(functools.partial(edge_kernel, sizes), out_shape=[jax.Shap...  3.68 us
    pallas_call x1, Pallas kernels, first_call(): pl.pallas_call(functools.partial(first_kernel, sizes, shards), out_shape=...  3.5 us
    pallas_call x1, Pallas kernels, later_call(): pl.pallas_call(functools.partial(later_kernel, sizes, shards, part), out_...  2.8 us
    ppermute x5, waiting for transfers between devices, spread(): return lax.ppermute(value, ('row', 'pitch'), pairs)  1.17 us
  transfers between devices with their start and end apart: 16, of which 9 were waited for; matrix products, arithmetic and copies ran while one was open for 1% of the time, Pallas kernels for 19%

profile of v6, /device:TPU:0, one launch (start us, length us, event | category | flops | bytes accessed | tf_op | source)
XLA Modules:
  0.0 55.2 jit_solution(7349280316328481258)
XLA Ops:
  0.0 3.7 %edge.1 = (bf16[5,112,128]{2,1,0:T(8,128)(2,1)S(1)}, bf16[5,112,128]{2,1,0:T(8,128)(2,1)S(1)}, bf16[2,1024,128]{2,1,0:T(8,128)(2,1)S(1)}, bf16[5,512,1024]{2,1,0:T(8,128)(2,1)S(1)}) custom-call(s32[2]{0:T(128)} %counts_hbm.2, s32[2,64]{1,0:T(2,128)} %bitcast.19, s32[7,128]{1,0:T(8,128)} %bitcast.17, bf16[512,896]{1,0:T(8,128)(2,1)} %weight_hbm.3, ...), custom_call_target="tpu_custom_call" | custom-call | flops 372244480 | bytes 2621440 | tf_op jit(solution)/shard_map/edge/pallas_call | solution.py:213
  3.7 3.0 %collective-permute-start = (bf16[5,112,128]{2,1,0:T(8,128)(2,1)S(1)}, bf16[5,112,128]{2,1,0:T(8,128)(2,1)S(1)}, u32[]{:S(2)}, u32[]{:S(2)}) collective-permute-start(bf16[5,112,128]{2,1,0:T(8,128)(2,1)S(1)} %get-tuple-element.26), channel_id=1, source_target_pairs={{0,1},{1,0},{2,3},{3,2},{4,5},{5,4},{6,7},{7,6},{8,9},{9,8},{10,11... | collective-permute-start | bytes 430088 | tf_op jit(solution)/shard_map/ppermute | solution.py:23
  6.7 0.1 collective-permute-start.1
  6.8 3.5 %first_part.1 = (f32[5,112,128]{2,1,0:T(8,128)S(1)}, bf16[5,112,128]{2,1,0:T(8,128)(2,1)S(1)}, bf16[5,112,128]{2,1,0:T(8,128)(2,1)S(1)}, f32[5,112,128]{2,1,0:T(...) custom-call(s32[7,128]{1,0:T(8,128)} %bitcast.18, bf16[512,896]{1,0:T(8,128)(2,1)} %weight_hbm.3, ...), custom_call_target="tpu_custom_call" | custom-call | flops 964689920 | bytes 5242880 | tf_op jit(solution)/shard_map/first_part/pallas_call | solution.py:311
  10.3 1.0 %collective-permute-done = bf16[5,112,128]{2,1,0:T(8,128)(2,1)S(1)} collective-permute-done((bf16[5,112,128]{2,1,0:T(8,128)(2,1)S(1)}, bf16[5,112,128]{2,1,0:T(8,128)(2,1)S(1)}, u32[]{:S(2)}, u32[]{:S(2)}) %collective-permute-start) | collective-permute-done | bytes 143392 | tf_op jit(solution)/shard_map/ppermute | solution.py:23
  11.3 0.1 fusion.1.after_ref
  11.3 2.2 %collective-permute-start.10 = (bf16[1,5,112,128]{3,2,1,0:T(8,128)(2,1)S(1)}, bf16[1,5,112,128]{3,2,1,0:T(8,128)(2,1)S(1)}, u32[]{:S(2)}, u32[]{:S(2)}) collective-permute-start(bf16[1,5,112,128]{3,2,1,0:T(8,128)(2,1)S(1)} %bitcast.13), channel_id=1, source_target_pairs={{0,2},{2,0},{4,6},{6,4},{1,3},{3,1},{5,7},{7,5},{8,10},{10,8},{12,... | collective-permute-start | bytes 430088 | tf_op jit(solution)/shard_map/ppermute | solution.py:23
  13.5 2.8 %later_part.1 = (f32[5,112,128]{2,1,0:T(8,128)S(1)}, bf16[5,112,128]{2,1,0:T(8,128)(2,1)S(1)}, bf16[5,112,128]{2,1,0:T(8,128)(2,1)S(1)}, f32[5,112,128]{2,1,0:T(8,128)S(1)}, bf16[1024,128]{1,0:T(8,128)(2,1)S(1)}) custom-call(s32[2]{0:T(128)} %counts_hbm.2, s32[2,64]{1,0:T(2,128)} %bitcast.20, bf16[10,512,1024]{2,1,0:T(8,128)(2,1)} %bitcast.16, ...), custom_call_target="tpu_custom_call" | custom-call | flops 964689920 | bytes 5242880 | tf_op jit(solution)/shard_map/later_part/pallas_call | solution.py:364
  16.4 0.0 collective-permute-done.1
  16.4 0.1 fusion.22
  16.4 0.1 collective-permute-start.3
  16.5 1.0 %collective-permute-done.10 = bf16[1,5,112,128]{3,2,1,0:T(8,128)(2,1)S(1)} collective-permute-done((bf16[1,5,112,128]{3,2,1,0:T(8,128)(2,1)S(1)}, bf16[1,5,112,128]{3,2,1,0:T(8,128)(2,1)S(1)}, u32[]{:S(2)}, u32[]{:S(2)}) %collective-permute-start.10) | collective-permute-done | bytes 143392 | tf_op jit(solution)/shard_map/ppermute | solution.py:23
  17.5 0.1 fusion.7
  17.6 4.4 %collective-permute-start.11 = (bf16[5,112,128]{2,1,0:T(8,128)(2,1)S(1)}, bf16[5,112,128]{2,1,0:T(8,128)(2,1)S(1)}, u32[]{:S(2)}, u32[]{:S(2)}) collective-permute-start(bf16[5,112,128]{2,1,0:T(8,128)(2,1)S(1)} %get-tuple-element.38), channel_id=1, source_target_pairs={{0,6},{2,4},{4,2},{6,0},{1,7},{3,5},{5,3},{7,1},{8,14},{10,12},{12... | collective-permute-start | bytes 430088 | tf_op jit(solution)/shard_map/ppermute | solution.py:23
  22.1 0.0 collective-permute-start.9
  22.1 2.1 %collective-permute-done.3 = bf16[1,5,112,128]{3,2,1,0:T(8,128)(2,1)S(1)} collective-permute-done((bf16[1,5,112,128]{3,2,1,0:T(8,128)(2,1)S(1)}, bf16[1,5,112,128]{3,2,1,0:T(8,128)(2,1)S(1)}, u32[]{:S(2)}, u32[]{:S(2)}) %collective-permute-start.3) | collective-permute-done | bytes 143392 | tf_op jit(solution)/shard_map/ppermute | solution.py:23
  24.1 0.1 fusion.16
  24.2 0.1 collective-permute-start.2
  24.3 3.1 %collective-permute-start.4 = (bf16[5,112,128]{2,1,0:T(8,128)(2,1)S(1)}, bf16[5,112,128]{2,1,0:T(8,128)(2,1)S(1)}, u32[]{:S(2)}, u32[]{:S(2)}) collective-permute-start(bf16[5,112,128]{2,1,0:T(8,128)(2,1)S(1)} %get-tuple-element.40), channel_id=1, source_target_pairs={{0,6},{2,4},{4,2},{6,0},{1,7},{3,5},{5,3},{7,1},{8,14},{10,12},{12... | collective-permute-start | bytes 430088 | tf_op jit(solution)/shard_map/ppermute | solution.py:23
  27.4 0.8 %collective-permute-done.11 = bf16[5,112,128]{2,1,0:T(8,128)(2,1)S(1)} collective-permute-done((bf16[5,112,128]{2,1,0:T(8,128)(2,1)S(1)}, bf16[5,112,128]{2,1,0:T(8,128)(2,1)S(1)}, u32[]{:S(2)}, u32[]{:S(2)}) %collective-permute-start.11) | collective-permute-done | bytes 143392 | tf_op jit(solution)/shard_map/ppermute | solution.py:23
  28.3 1.9 %collective-permute-done.9 = bf16[5,112,128]{2,1,0:T(8,128)(2,1)S(1)} collective-permute-done((bf16[5,112,128]{2,1,0:T(8,128)(2,1)S(1)}, bf16[5,112,128]{2,1,0:T(8,128)(2,1)S(1)}, u32[]{:S(2)}, u32[]{:S(2)}) %collective-permute-start.9) | collective-permute-done | bytes 143392 | tf_op jit(solution)/shard_map/ppermute | solution.py:23
  30.2 0.1 fusion.5
  30.3 1.6 %collective-permute-start.12 = (bf16[5,112,128]{2,1,0:T(8,128)(2,1)S(1)}, bf16[5,112,128]{2,1,0:T(8,128)(2,1)S(1)}, u32[]{:S(2)}, u32[]{:S(2)}) collective-permute-start(bf16[5,112,128]{2,1,0:T(8,128)(2,1)S(1)} %fusion.5), channel_id=1, source_target_pairs={{0,16},{2,18},{4,20},{6,22},{8,24},{10,26},{12,28},{14,30},{16,0},... | collective-permute-start | bytes 430088 | tf_op jit(solution)/shard_map/ppermute | solution.py:549
  31.9 3.3 %collective-permute-start.14 = (bf16[5,112,128]{2,1,0:T(8,128)(2,1)S(1)}, bf16[5,112,128]{2,1,0:T(8,128)(2,1)S(1)}, u32[]{:S(2)}, u32[]{:S(2)}) collective-permute-start(bf16[5,112,128]{2,1,0:T(8,128)(2,1)S(1)} %fusion.5), channel_id=1, source_target_pairs={{0,22},{2,20},{4,18},{6,16},{8,30},{10,28},{12,26},{14,24},{16,6},... | collective-permute-start | bytes 430088 | tf_op jit(solution)/shard_map/ppermute | solution.py:549
  35.2 0.0 collective-permute-done.2
  35.2 0.9 %collective-permute-done.4 = bf16[5,112,128]{2,1,0:T(8,128)(2,1)S(1)} collective-permute-done((bf16[5,112,128]{2,1,0:T(8,128)(2,1)S(1)}, bf16[5,112,128]{2,1,0:T(8,128)(2,1)S(1)}, u32[]{:S(2)}, u32[]{:S(2)}) %collective-permute-start.4) | collective-permute-done | bytes 143392 | tf_op jit(solution)/shard_map/ppermute | solution.py:23
  36.1 0.1 fusion.14
  36.2 2.9 %collective-permute-start.6 = (bf16[5,112,128]{2,1,0:T(8,128)(2,1)S(1)}, bf16[5,112,128]{2,1,0:T(8,128)(2,1)S(1)}, u32[]{:S(2)}, u32[]{:S(2)}) collective-permute-start(bf16[5,112,128]{2,1,0:T(8,128)(2,1)S(1)} %fusion.14), channel_id=1, source_target_pairs={{0,22},{2,20},{4,18},{6,16},{8,30},{10,28},{12,26},{14,24},{16,6},... | collective-permute-start | bytes 430088 | tf_op jit(solution)/shard_map/ppermute | solution.py:549
  39.1 0.1 collective-permute-start.8
  39.2 0.0 collective-permute-done.12.rest_0_
  39.2 2.1 %collective-permute-start.13 = (bf16[5,112,128]{2,1,0:T(8,128)(2,1)S(1)}, bf16[5,112,128]{2,1,0:T(8,128)(2,1)S(1)}, u32[]{:S(2)}, u32[]{:S(2)}) collective-permute-start(bf16[5,112,128]{2,1,0:T(8,128)(2,1)S(1)} %collective-permute-done.12.rest_0_), channel_id=1, source_target_pairs={{0,2},{2,0},{4,6},{6,4},{1,3},{3,1},{5,7},{7,5},{8,10},{10,8},{12,... | collective-permute-start | bytes 430088 | tf_op jit(solution)/shard_map/ppermute | solution.py:23
  41.3 0.0 collective-permute-done.14.rest_1_
  41.3 3.2 %collective-permute-start.15 = (bf16[5,112,128]{2,1,0:T(8,128)(2,1)S(1)}, bf16[5,112,128]{2,1,0:T(8,128)(2,1)S(1)}, u32[]{:S(2)}, u32[]{:S(2)}) collective-permute-start(bf16[5,112,128]{2,1,0:T(8,128)(2,1)S(1)} %collective-permute-done.14.rest_1_), channel_id=1, source_target_pairs={{0,2},{2,0},{4,6},{6,4},{1,3},{3,1},{5,7},{7,5},{8,10},{10,8},{12,... | collective-permute-start | bytes 430088 | tf_op jit(solution)/shard_map/ppermute | solution.py:23
  44.5 0.0 collective-permute-start.5
  44.5 1.2 %collective-permute-done.6.rest_1_ = bf16[5,112,128]{2,1,0:T(8,128)(2,1)S(1)} collective-permute-done((bf16[5,112,128]{2,1,0:T(8,128)(2,1)S(1)}, bf16[5,112,128]{2,1,0:T(8,128)(2,1)S(1)}, u32[]{:S(2)}, u32[]{:S(2)}) %collective-permute-start.6) | collective-permute-done | bytes 143392 | tf_op jit(solution)/shard_map/ppermute | solution.py:549
  45.6 1.4 %collective-permute-start.7 = (bf16[5,112,128]{2,1,0:T(8,128)(2,1)S(1)}, bf16[5,112,128]{2,1,0:T(8,128)(2,1)S(1)}, u32[]{:S(2)}, u32[]{:S(2)}) collective-permute-start(bf16[5,112,128]{2,1,0:T(8,128)(2,1)S(1)} %collective-permute-done.6.rest_1_), channel_id=1, source_target_pairs={{0,2},{2,0},{4,6},{6,4},{1,3},{3,1},{5,7},{7,5},{8,10},{10,8},{12,... | collective-permute-start | bytes 430088 | tf_op jit(solution)/shard_map/ppermute | solution.py:23
  47.1 1.7 %synthesise.3.rest_4_ = bf16[10,448,1024]{2,1,0:T(8,128)(2,1)} custom-call(bf16[1024,128]{1,0:T(8,128)(2,1)S(1)} %get-tuple-element.28.table_ref, bf16[5,112,128]{2,1,0:T(8,128)(2,1)S(1)} %collective-permute-done.12.rest_0_, bf16[5,112,128]{2,1,0:T(8,128)(2,1)S(1)} %collective-permute-done.14.rest_1_), custom_call_target="tpu_custom_call" | custom-call | flops 293601280 | bytes 2293760 | tf_op jit(solution)/shard_map/synthesise/pallas_call | solution.py:429
  48.8 0.0 collective-permute-done.8.rest_0_
  48.8 0.0 collective-permute-done.13.rest_2_
  48.8 1.6 %collective-permute-done.15.rest_3_ = bf16[5,112,128]{2,1,0:T(8,128)(2,1)S(1)} collective-permute-done((bf16[5,112,128]{2,1,0:T(8,128)(2,1)S(1)}, bf16[5,112,128]{2,1,0:T(8,128)(2,1)S(1)}, u32[]{:S(2)}, u32[]{:S(2)}) %collective-permute-start.15) | collective-permute-done | bytes 143392 | tf_op jit(solution)/shard_map/ppermute | solution.py:23
  50.4 2.5 %synthesise.4.rest_2_ = bf16[10,448,1024]{2,1,0:T(8,128)(2,1)} custom-call(bf16[1024,128]{1,0:T(8,128)(2,1)S(1)} %get-tuple-element.28.table_ref, bf16[5,112,128]{2,1,0:T(8,128)(2,1)S(1)} %collective-permute-done.8.rest_0_, bf16[5,112,128]{2,1,0:T(8,128)(2,1)S(1)} %collective-permute-done.6.rest_1_, ...), custom_call_target="tpu_custom_call", output_to_operand_aliasing={{}: (5, {})} | custom-call | flops 587202560 | bytes 4587520 | tf_op jit(solution)/shard_map/synthesise/pallas_call | solution.py:429
  53.0 0.0 collective-permute-done.5.rest_0_
  53.0 0.5 collective-permute-done.7.rest_1_
  53.5 1.7 %synthesise.5 = bf16[10,448,1024]{2,1,0:T(8,128)(2,1)} custom-call(bf16[1024,128]{1,0:T(8,128)(2,1)S(1)} %get-tuple-element.28.table_ref, bf16[5,112,128]{2,1,0:T(8,128)(2,1)S(1)} %collective-permute-done.5.rest_0_, bf16[5,112,128]{2,1,0:T(8,128)(2,1)S(1)} %collective-permute-done.7.rest_1_, ...), custom_call_target="tpu_custom_call", output_to_operand_aliasing={{}: (3, {})} | custom-call | flops 293601280 | bytes 2293760 | tf_op jit(solution)/shard_map/synthesise/pallas_call | solution.py:429
Async XLA Ops:
  3.7 7.6 %collective-permute-start = (bf16[5,112,128]{2,1,0:T(8,128)(2,1)S(1)}, bf16[5,112,128]{2,1,0:T(8,128)(2,1)S(1)}, u32[]{:S(2)}, u32[]{:S(2)}) collective-permute-start(bf16[5,112,128]{2,1,0:T(8,128)(2,1)S(1)} %get-tuple-element.26), channel_id=1, source_target_pairs={{0,1},{1,0},{2,3},{3,2},{4,5},{5,4},{6,7},{7,6},{8,9},{9,8},{10,11... | collective-permute-start | bytes 430088 | tf_op jit(solution)/shard_map/ppermute | solution.py:23
  6.7 9.7 %collective-permute-start.1 = (bf16[5,112,128]{2,1,0:T(8,128)(2,1)S(1)}, bf16[5,112,128]{2,1,0:T(8,128)(2,1)S(1)}, u32[]{:S(2)}, u32[]{:S(2)}) collective-permute-start(bf16[5,112,128]{2,1,0:T(8,128)(2,1)S(1)} %get-tuple-element.29), channel_id=1, source_target_pairs={{0,1},{1,0},{2,3},{3,2},{4,5},{5,4},{6,7},{7,6},{8,9},{9,8},{10,11... | collective-permute-start | bytes 430088 | tf_op jit(solution)/shard_map/ppermute | solution.py:23
  11.3 6.2 %collective-permute-start.10 = (bf16[1,5,112,128]{3,2,1,0:T(8,128)(2,1)S(1)}, bf16[1,5,112,128]{3,2,1,0:T(8,128)(2,1)S(1)}, u32[]{:S(2)}, u32[]{:S(2)}) collective-permute-start(bf16[1,5,112,128]{3,2,1,0:T(8,128)(2,1)S(1)} %bitcast.13), channel_id=1, source_target_pairs={{0,2},{2,0},{4,6},{6,4},{1,3},{3,1},{5,7},{7,5},{8,10},{10,8},{12,... | collective-permute-start | bytes 430088 | tf_op jit(solution)/shard_map/ppermute | solution.py:23
  16.4 7.7 %collective-permute-start.3 = (bf16[1,5,112,128]{3,2,1,0:T(8,128)(2,1)S(1)}, bf16[1,5,112,128]{3,2,1,0:T(8,128)(2,1)S(1)}, u32[]{:S(2)}, u32[]{:S(2)}) collective-permute-start(bf16[1,5,112,128]{3,2,1,0:T(8,128)(2,1)S(1)} %fusion.22), channel_id=1, source_target_pairs={{0,2},{2,0},{4,6},{6,4},{1,3},{3,1},{5,7},{7,5},{8,10},{10,8},{12,... | collective-permute-start | bytes 430088 | tf_op jit(solution)/shard_map/ppermute | solution.py:23
  17.6 10.6 %collective-permute-start.11 = (bf16[5,112,128]{2,1,0:T(8,128)(2,1)S(1)}, bf16[5,112,128]{2,1,0:T(8,128)(2,1)S(1)}, u32[]{:S(2)}, u32[]{:S(2)}) collective-permute-start(bf16[5,112,128]{2,1,0:T(8,128)(2,1)S(1)} %get-tuple-element.38), channel_id=1, source_target_pairs={{0,6},{2,4},{4,2},{6,0},{1,7},{3,5},{5,3},{7,1},{8,14},{10,12},{12... | collective-permute-start | bytes 430088 | tf_op jit(solution)/shard_map/ppermute | solution.py:23
  22.1 8.1 %collective-permute-start.9 = (bf16[5,112,128]{2,1,0:T(8,128)(2,1)S(1)}, bf16[5,112,128]{2,1,0:T(8,128)(2,1)S(1)}, u32[]{:S(2)}, u32[]{:S(2)}) collective-permute-start(bf16[5,112,128]{2,1,0:T(8,128)(2,1)S(1)} %get-tuple-element.37), channel_id=1, source_target_pairs={{0,2},{2,0},{4,6},{6,4},{1,3},{3,1},{5,7},{7,5},{8,10},{10,8},{12,... | collective-permute-start | bytes 430088 | tf_op jit(solution)/shard_map/ppermute | solution.py:23
  24.2 11.0 %collective-permute-start.2 = (bf16[5,112,128]{2,1,0:T(8,128)(2,1)S(1)}, bf16[5,112,128]{2,1,0:T(8,128)(2,1)S(1)}, u32[]{:S(2)}, u32[]{:S(2)}) collective-permute-start(bf16[5,112,128]{2,1,0:T(8,128)(2,1)S(1)} %get-tuple-element.39), channel_id=1, source_target_pairs={{0,2},{2,0},{4,6},{6,4},{1,3},{3,1},{5,7},{7,5},{8,10},{10,8},{12,... | collective-permute-start | bytes 430088 | tf_op jit(solution)/shard_map/ppermute | solution.py:23
  24.3 11.8 %collective-permute-start.4 = (bf16[5,112,128]{2,1,0:T(8,128)(2,1)S(1)}, bf16[5,112,128]{2,1,0:T(8,128)(2,1)S(1)}, u32[]{:S(2)}, u32[]{:S(2)}) collective-permute-start(bf16[5,112,128]{2,1,0:T(8,128)(2,1)S(1)} %get-tuple-element.40), channel_id=1, source_target_pairs={{0,6},{2,4},{4,2},{6,0},{1,7},{3,5},{5,3},{7,1},{8,14},{10,12},{12... | collective-permute-start | bytes 430088 | tf_op jit(solution)/shard_map/ppermute | solution.py:23
  30.3 8.9 %collective-permute-start.12 = (bf16[5,112,128]{2,1,0:T(8,128)(2,1)S(1)}, bf16[5,112,128]{2,1,0:T(8,128)(2,1)S(1)}, u32[]{:S(2)}, u32[]{:S(2)}) collective-permute-start(bf16[5,112,128]{2,1,0:T(8,128)(2,1)S(1)} %fusion.5), channel_id=1, source_target_pairs={{0,16},{2,18},{4,20},{6,22},{8,24},{10,26},{12,28},{14,30},{16,0},... | collective-permute-start | bytes 430088 | tf_op jit(solution)/shard_map/ppermute | solution.py:549
  31.9 9.4 %collective-permute-start.14 = (bf16[5,112,128]{2,1,0:T(8,128)(2,1)S(1)}, bf16[5,112,128]{2,1,0:T(8,128)(2,1)S(1)}, u32[]{:S(2)}, u32[]{:S(2)}) collective-permute-start(bf16[5,112,128]{2,1,0:T(8,128)(2,1)S(1)} %fusion.5), channel_id=1, source_target_pairs={{0,22},{2,20},{4,18},{6,16},{8,30},{10,28},{12,26},{14,24},{16,6},... | collective-permute-start | bytes 430088 | tf_op jit(solution)/shard_map/ppermute | solution.py:549
  36.2 9.5 %collective-permute-start.6 = (bf16[5,112,128]{2,1,0:T(8,128)(2,1)S(1)}, bf16[5,112,128]{2,1,0:T(8,128)(2,1)S(1)}, u32[]{:S(2)}, u32[]{:S(2)}) collective-permute-start(bf16[5,112,128]{2,1,0:T(8,128)(2,1)S(1)} %fusion.14), channel_id=1, source_target_pairs={{0,22},{2,20},{4,18},{6,16},{8,30},{10,28},{12,26},{14,24},{16,6},... | collective-permute-start | bytes 430088 | tf_op jit(solution)/shard_map/ppermute | solution.py:549
  39.1 9.7 %collective-permute-start.8 = (bf16[5,112,128]{2,1,0:T(8,128)(2,1)S(1)}, bf16[5,112,128]{2,1,0:T(8,128)(2,1)S(1)}, u32[]{:S(2)}, u32[]{:S(2)}) collective-permute-start(bf16[5,112,128]{2,1,0:T(8,128)(2,1)S(1)} %fusion.14), channel_id=1, source_target_pairs={{0,16},{2,18},{4,20},{6,22},{8,24},{10,26},{12,28},{14,30},{16,0},... | collective-permute-start | bytes 430088 | tf_op jit(solution)/shard_map/ppermute | solution.py:549
  39.2 9.6 %collective-permute-start.13 = (bf16[5,112,128]{2,1,0:T(8,128)(2,1)S(1)}, bf16[5,112,128]{2,1,0:T(8,128)(2,1)S(1)}, u32[]{:S(2)}, u32[]{:S(2)}) collective-permute-start(bf16[5,112,128]{2,1,0:T(8,128)(2,1)S(1)} %collective-permute-done.12.rest_0_), channel_id=1, source_target_pairs={{0,2},{2,0},{4,6},{6,4},{1,3},{3,1},{5,7},{7,5},{8,10},{10,8},{12,... | collective-permute-start | bytes 430088 | tf_op jit(solution)/shard_map/ppermute | solution.py:23
  41.3 9.1 %collective-permute-start.15 = (bf16[5,112,128]{2,1,0:T(8,128)(2,1)S(1)}, bf16[5,112,128]{2,1,0:T(8,128)(2,1)S(1)}, u32[]{:S(2)}, u32[]{:S(2)}) collective-permute-start(bf16[5,112,128]{2,1,0:T(8,128)(2,1)S(1)} %collective-permute-done.14.rest_1_), channel_id=1, source_target_pairs={{0,2},{2,0},{4,6},{6,4},{1,3},{3,1},{5,7},{7,5},{8,10},{10,8},{12,... | collective-permute-start | bytes 430088 | tf_op jit(solution)/shard_map/ppermute | solution.py:23
  44.5 8.5 %collective-permute-start.5 = (bf16[5,112,128]{2,1,0:T(8,128)(2,1)S(1)}, bf16[5,112,128]{2,1,0:T(8,128)(2,1)S(1)}, u32[]{:S(2)}, u32[]{:S(2)}) collective-permute-start(bf16[5,112,128]{2,1,0:T(8,128)(2,1)S(1)} %fusion.14), channel_id=1, source_target_pairs={{0,18},{2,16},{4,22},{6,20},{8,26},{10,24},{12,30},{14,28},{16,2},... | collective-permute-start | bytes 430088 | tf_op jit(solution)/shard_map/ppermute | solution.py:549
  45.6 7.8 %collective-permute-start.7 = (bf16[5,112,128]{2,1,0:T(8,128)(2,1)S(1)}, bf16[5,112,128]{2,1,0:T(8,128)(2,1)S(1)}, u32[]{:S(2)}, u32[]{:S(2)}) collective-permute-start(bf16[5,112,128]{2,1,0:T(8,128)(2,1)S(1)} %collective-permute-done.6.rest_1_), channel_id=1, source_target_pairs={{0,2},{2,0},{4,6},{6,4},{1,3},{3,1},{5,7},{7,5},{8,10},{10,8},{12,... | collective-permute-start | bytes 430088 | tf_op jit(solution)/shard_map/ppermute | solution.py:23
